TPU v7x, 32 devices: a whole 2x2x4 slice. The times are simulated.
32 devices in a mesh: seq: 8 (over z, y), head: 4 (over x, core).
Axes of the slice: x: 2, y: 2, z: 4, core: 2. Of those that a mesh axis runs over, the one named last changes fastest.
Arguments:
- tokens: bfloat16 [8192, 2048], P('seq'), may hold values from -6 to 6
- cotangent: bfloat16 [8192, 2048], P('seq'), may hold values from -6 to 6
- prefix_length: int32 [1], replicated, may hold values from 1793 to 2048
- answer_lengths: int32 [8], P('seq'), may hold values from 1 to 768, as said below
- inward: float32 [2048, 3, 2048], P('seq', None, 'head'), may hold values from -0.125 to 0.125
- outward: float32 [2048, 2048], P('head', 'seq'), may hold values from -1.75 to 1.75
- expand: float32 [2048, 8192], P('seq', 'head')
- contract: float32 [8192, 2048], P('head', 'seq'), may hold values from -0.0625 to 0.0625
- norm_gains: float32 [2, 2048], P(None, 'seq')
- moment_inward: float32 [2048, 3, 2048], P('seq', None, 'head'), may hold values from -9.1552734e-05 to 9.1552734e-05
- moment_outward: float32 [2048, 2048], P('head', 'seq'), may hold values from -9.1552734e-05 to 9.1552734e-05
- moment_expand: float32 [2048, 8192], P('seq', 'head'), may hold values from -9.1552734e-05 to 9.1552734e-05
- moment_contract: float32 [8192, 2048], P('head', 'seq'), may hold values from -9.1552734e-05 to 9.1552734e-05
- moment_gains: float32 [2, 2048], P(None, 'seq'), may hold values from -0.00036621094 to 0.00036621094
- variance_inward: float32 [2048, 3, 2048], P('seq', None, 'head'), may hold values from 5.9604643e-10 to 7.947286e-09
- variance_outward: float32 [2048, 2048], P('head', 'seq'), may hold values from 1.622759e-11 to 2.187197e-10
- variance_expand: float32 [2048, 8192], P('seq', 'head'), may hold values from 9.934108e-11 to 1.390775e-09
- variance_contract: float32 [8192, 2048], P('head', 'seq'), may hold values from 5.9604643e-10 to 7.947286e-09
- variance_gains: float32 [2, 2048], P(None, 'seq'), may hold values from 9.536743e-09 to 1.2715658e-07
- average_inward: float32 [2048, 3, 2048], P('seq', None, 'head'), may hold values from -0.125 to 0.125
- average_outward: float32 [2048, 2048], P('head', 'seq'), may hold values from -1.75 to 1.75
- average_expand: float32 [2048, 8192], P('seq', 'head'), may hold values from -0.125 to 0.125
- average_contract: float32 [8192, 2048], P('head', 'seq'), may hold values from -0.0625 to 0.0625
- average_gains: float32 [2, 2048], P(None, 'seq'), may hold values from 0.5 to 1.5
Outputs:
- layer_output: bfloat16 [8192, 2048], P('seq')
- input_grad: float32 [8192, 2048], P('seq')
- grad_norm: float32 [1], replicated
- inward_moment: float32 [2048, 3, 2048], P('seq', None, 'head')
- inward_variance: float32 [2048, 3, 2048], P('seq', None, 'head')
- inward_weight: float32 [2048, 3, 2048], P('seq', None, 'head')
- inward_average: float32 [2048, 3, 2048], P('seq', None, 'head')
- outward_moment: float32 [2048, 2048], P('head', 'seq')
- outward_variance: float32 [2048, 2048], P('head', 'seq')
- outward_weight: float32 [2048, 2048], P('head', 'seq')
- outward_average: float32 [2048, 2048], P('head', 'seq')
- expand_moment: float32 [2048, 8192], P('seq', 'head')
- expand_variance: float32 [2048, 8192], P('seq', 'head')
- expand_weight: float32 [2048, 8192], P('seq', 'head')
- expand_average: float32 [2048, 8192], P('seq', 'head')
- contract_moment: float32 [8192, 2048], P('head', 'seq')
- contract_variance: float32 [8192, 2048], P('head', 'seq')
- contract_weight: float32 [8192, 2048], P('head', 'seq')
- contract_average: float32 [8192, 2048], P('head', 'seq')
- gains_moment: float32 [2, 2048], P(None, 'seq')
- gains_variance: float32 [2, 2048], P(None, 'seq')
- gains_weight: float32 [2, 2048], P(None, 'seq')
- gains_average: float32 [2, 2048], P(None, 'seq')
Inputs may be any that keep to these rules, and one draw needn't show every extreme that they name: Prefix slots at positions from prefix_length on are padding. Solution slots from answer_lengths[i] on are padding; some solution fills all 768 slots in every draw.
All inputs are finite; a program needn't handle non-finite values.
Results may differ from a plain program's by a relative error of at most 0.024.
Values may be sent and summed in bfloat16 or wider, within the bound.
No kernel may reach another device: no remote copies, remote signals or barrier semaphores. Data moves between devices by JAX's collectives and lax.ppermute only.
A program may use at most 320 MiB of HBM per device.

v0:
```python
import jax
import jax.numpy as jnp
from jax import lax
from jax.sharding import PartitionSpec as P

HEAD_DIM = 128
PRE_DEV = 256
SOL_DEV = 768
STEP = 10


EPS_NORM = 1e-05
BETA_ONE = 0.9
BETA_TWO = 0.95
ADAM_EPS = 1e-08
EMA_KEEP = 0.7
CLIP_NORM = 1.0
DECAY_MATRIX = 0.1
RATE_INWARD = 0.05
RATE_OUTWARD = 0.15
RATE_EXPAND = 0.05
RATE_CONTRACT = 0.03
RATE_GAINS = 0.5


def layer_norm(values, gain_row):
    center = values - jnp.mean(values, axis=-1, keepdims=True)
    inverse = lax.rsqrt(jnp.mean(center * center, axis=-1, keepdims=True) + EPS_NORM)
    normal_unit = center * inverse
    return (normal_unit * gain_row, normal_unit, inverse)


def norm_back(incoming, normal_unit, inverse, gain_row):
    scaled = incoming * gain_row
    inner_sum = (
        scaled
        - jnp.mean(scaled, axis=-1, keepdims=True)
        - normal_unit * jnp.mean(scaled * normal_unit, axis=-1, keepdims=True)
    )
    return (inner_sum * inverse, jnp.sum(incoming * normal_unit, axis=0))


def adamw(weight, gradient, moment, variance, average, step_rate, decay_rate):
    moment = BETA_ONE * moment + (1.0 - BETA_ONE) * gradient
    variance = BETA_TWO * variance + (1.0 - BETA_TWO) * gradient * gradient
    corrected = moment / (1.0 - BETA_ONE**STEP)
    scaled_root = jnp.sqrt(variance / (1.0 - BETA_TWO**STEP)) + ADAM_EPS
    weight_new = weight - step_rate * corrected / scaled_root - step_rate * decay_rate * weight
    average = EMA_KEEP * average + (1.0 - EMA_KEEP) * weight_new
    return (moment, variance, weight_new, average)


def head_total(partial_sum):
    return lax.psum(partial_sum.astype(jnp.bfloat16), "head").astype(jnp.float32)


def input_total(partial_sum):
    return lax.psum(partial_sum.astype(jnp.bfloat16), "head").astype(jnp.float32)


def local(
    tokens,
    cotangent,
    prefix_length,
    answer_lengths,
    inward,
    outward,
    expand,
    contract,
    norm_gains,
    moment_inward,
    moment_outward,
    moment_expand,
    moment_contract,
    moment_gains,
    variance_inward,
    variance_outward,
    variance_expand,
    variance_contract,
    variance_gains,
    average_inward,
    average_outward,
    average_expand,
    average_contract,
    average_gains,
):
    bf_type = jnp.bfloat16
    fp_type = jnp.float32
    device = lax.axis_index("seq")
    seq_count = lax.axis_size("seq")
    tok_dev = tokens.shape[0]
    pre_dev = PRE_DEV
    prefix_total = pre_dev * seq_count
    key_count = prefix_total + SOL_DEV
    limit_prefix = prefix_length[0]
    limit_answer = answer_lengths[0]
    score_scale = HEAD_DIM ** (-0.5)
    block_rows = 512
    block_count = tok_dev // block_rows
    shard_copies = (
        inward.astype(bf_type),
        outward.astype(bf_type),
        expand.astype(bf_type),
        contract.astype(bf_type),
        norm_gains.astype(bf_type),
    )
    gathered = (
        lax.all_gather(shard_copies[0], "seq", axis=0, tiled=True),
        lax.all_gather(shard_copies[1], "seq", axis=1, tiled=True),
        lax.all_gather(shard_copies[2], "seq", axis=0, tiled=True),
        lax.all_gather(shard_copies[3], "seq", axis=1, tiled=True),
        lax.all_gather(shard_copies[4], "seq", axis=1, tiled=True),
    )
    in_matrix, out_matrix, up_matrix, down_matrix, gain_rows = gathered
    gain_pair = gain_rows.astype(fp_type)
    local_width = in_matrix.shape[2]
    local_heads = local_width // HEAD_DIM
    source = tokens.astype(fp_type)
    normed_one, unit_one, inverse_one = layer_norm(source, gain_pair[0])
    normed_one = normed_one.astype(bf_type)
    projected = jnp.einsum(
        "td,dcn->tcn", normed_one, in_matrix, preferred_element_type=fp_type
    ).astype(bf_type)
    queries = projected[:, 0].reshape(tok_dev, local_heads, HEAD_DIM)
    key_own = projected[:, 1]
    value_own = projected[:, 2]
    key_prefix, value_prefix = (
        lax.all_gather(key_own[:pre_dev], "seq", axis=0, tiled=True),
        lax.all_gather(value_own[:pre_dev], "seq", axis=0, tiled=True),
    )
    key_rows = jnp.concatenate([key_prefix, key_own[pre_dev:]], axis=0).reshape(
        key_count, local_heads, HEAD_DIM
    )
    value_rows = jnp.concatenate([value_prefix, value_own[pre_dev:]], axis=0).reshape(
        key_count, local_heads, HEAD_DIM
    )
    column = jnp.arange(key_count, dtype=jnp.int32)

    def allowed_block(first_row):
        position = first_row + jnp.arange(block_rows, dtype=jnp.int32)
        is_prefix = position < pre_dev
        prefix_place = device * pre_dev + position
        upper_prefix = jnp.where(
            is_prefix, jnp.minimum(prefix_place + 1, limit_prefix), limit_prefix
        )
        upper_answer = jnp.where(is_prefix, 0, jnp.minimum(position - pre_dev + 1, limit_answer))
        return jnp.where(
            column[None] < prefix_total,
            column[None] < upper_prefix[:, None],
            column[None] - prefix_total < upper_answer[:, None],
        )

    def scores_of(block_index):
        first_row = block_index * block_rows
        query_block = lax.dynamic_slice_in_dim(queries, first_row, block_rows, 0)
        raw_scores = (
            jnp.einsum("qhd,khd->hqk", query_block, key_rows, preferred_element_type=fp_type)
            * score_scale
        )
        return (jnp.where(allowed_block(first_row)[None], raw_scores, -1e30), query_block)

    def forward_block(block_index):
        scores, query_block = scores_of(block_index)
        maximum = jnp.max(scores, axis=-1, keepdims=True)
        exponent = jnp.exp(scores - maximum)
        exp_total = jnp.sum(exponent, axis=-1, keepdims=True)
        probabilities = (exponent / exp_total).astype(bf_type)
        block_out = jnp.einsum(
            "hqk,khd->qhd", probabilities, value_rows, preferred_element_type=fp_type
        )
        return (block_out.astype(bf_type), (maximum + jnp.log(exp_total))[..., 0])

    mixed_blocks, log_totals = lax.map(forward_block, jnp.arange(block_count, dtype=jnp.int32))
    mixed_heads = mixed_blocks.reshape(tok_dev, local_width)
    hidden = source + head_total(jnp.dot(mixed_heads, out_matrix, preferred_element_type=fp_type))
    normed_two, unit_two, inverse_two = layer_norm(hidden, gain_pair[1])
    normed_two = normed_two.astype(bf_type)
    up_values = jnp.dot(normed_two, up_matrix, preferred_element_type=fp_type)
    activation_values, gelu_back = jax.vjp(
        lambda entry: jax.nn.gelu(entry, approximate=True), up_values
    )
    activation = activation_values.astype(bf_type)
    result = hidden + head_total(jnp.dot(activation, down_matrix, preferred_element_type=fp_type))
    layer_output = result.astype(bf_type)
    position_all = jnp.arange(tok_dev, dtype=jnp.int32)
    valid_rows = jnp.where(
        position_all < pre_dev,
        device * pre_dev + position_all < limit_prefix,
        position_all - pre_dev < limit_answer,
    ).astype(fp_type)
    out_grad = (cotangent.astype(fp_type) * valid_rows[:, None]).astype(bf_type)
    d_activation = jnp.einsum("td,fd->tf", out_grad, down_matrix, preferred_element_type=fp_type)
    d_up = gelu_back(d_activation)[0].astype(bf_type)
    grad_contract = jnp.einsum("tf,td->fd", activation, out_grad, preferred_element_type=fp_type)
    grad_expand = jnp.einsum("td,tf->df", normed_two, d_up, preferred_element_type=fp_type)
    d_normed_two = input_total(
        jnp.einsum("tf,df->td", d_up, up_matrix, preferred_element_type=fp_type)
    )
    d_norm_part, grad_gain_two = norm_back(d_normed_two, unit_two, inverse_two, gain_pair[1])
    d_hidden = out_grad.astype(fp_type) + d_norm_part
    d_attention = d_hidden.astype(bf_type)
    grad_outward = jnp.einsum("tn,td->nd", mixed_heads, d_attention, preferred_element_type=fp_type)
    d_mixed = jnp.einsum(
        "td,nd->tn", d_attention, out_matrix, preferred_element_type=fp_type
    ).astype(bf_type)
    d_mixed = d_mixed.reshape(tok_dev, local_heads, HEAD_DIM)

    def backward_block(running, block_index):
        key_grad, value_grad = running
        scores, query_block = scores_of(block_index)
        first_row = block_index * block_rows
        probabilities = jnp.exp(scores - log_totals[block_index][..., None])
        d_block = lax.dynamic_slice_in_dim(d_mixed, first_row, block_rows, 0)
        d_probs = jnp.einsum("qhd,khd->hqk", d_block, value_rows, preferred_element_type=fp_type)
        inner_sum = jnp.sum(probabilities * d_probs, axis=-1, keepdims=True)
        d_scores = (probabilities * (d_probs - inner_sum)).astype(bf_type)
        query_grad = (
            jnp.einsum("hqk,khd->qhd", d_scores, key_rows, preferred_element_type=fp_type)
            * score_scale
        )
        key_grad = (
            key_grad
            + jnp.einsum("hqk,qhd->khd", d_scores, query_block, preferred_element_type=fp_type)
            * score_scale
        )
        value_grad = value_grad + jnp.einsum(
            "hqk,qhd->khd", probabilities.astype(bf_type), d_block, preferred_element_type=fp_type
        )
        return ((key_grad, value_grad), query_grad)

    zero_keys = jnp.zeros((key_count, local_heads, HEAD_DIM), fp_type)
    (key_grad, value_grad), query_grads = lax.scan(
        backward_block, (zero_keys, zero_keys), jnp.arange(block_count, dtype=jnp.int32)
    )
    key_prefix_grad, value_prefix_grad = (
        lax.psum_scatter(
            key_grad[:prefix_total].astype(jnp.bfloat16), "seq", scatter_dimension=0, tiled=True
        ).astype(jnp.float32),
        lax.psum_scatter(
            value_grad[:prefix_total].astype(jnp.bfloat16), "seq", scatter_dimension=0, tiled=True
        ).astype(jnp.float32),
    )
    d_key = jnp.concatenate([key_prefix_grad, key_grad[prefix_total:]], axis=0).reshape(
        tok_dev, local_width
    )
    d_value = jnp.concatenate([value_prefix_grad, value_grad[prefix_total:]], axis=0).reshape(
        tok_dev, local_width
    )
    d_projected = jnp.stack(
        [query_grads.reshape(tok_dev, local_width), d_key, d_value], axis=1
    ).astype(bf_type)
    grad_inward = jnp.einsum("td,tcn->dcn", normed_one, d_projected, preferred_element_type=fp_type)
    d_normed_one = input_total(
        jnp.einsum("tcn,dcn->td", d_projected, in_matrix, preferred_element_type=fp_type)
    )
    d_source, grad_gain_one = norm_back(d_normed_one, unit_one, inverse_one, gain_pair[0])
    input_grad = d_hidden + d_source
    grad_gains = jnp.stack([grad_gain_one, grad_gain_two], axis=0)
    reduced = (
        lax.psum_scatter(
            grad_inward.astype(jnp.bfloat16), "seq", scatter_dimension=0, tiled=True
        ).astype(jnp.float32),
        lax.psum_scatter(
            grad_outward.astype(jnp.bfloat16), "seq", scatter_dimension=1, tiled=True
        ).astype(jnp.float32),
        lax.psum_scatter(
            grad_expand.astype(jnp.bfloat16), "seq", scatter_dimension=0, tiled=True
        ).astype(jnp.float32),
        lax.psum_scatter(
            grad_contract.astype(jnp.bfloat16), "seq", scatter_dimension=1, tiled=True
        ).astype(jnp.float32),
        lax.psum_scatter(
            grad_gains.astype(jnp.bfloat16), "seq", scatter_dimension=1, tiled=True
        ).astype(jnp.float32),
    )
    red_inward, red_outward, red_expand, red_contract, red_gains = reduced
    matrix_squares = (
        jnp.sum(red_inward * red_inward)
        + jnp.sum(red_outward * red_outward)
        + jnp.sum(red_expand * red_expand)
        + jnp.sum(red_contract * red_contract)
    )
    gain_squares = jnp.where(lax.axis_index("head") == 0, jnp.sum(red_gains * red_gains), 0.0)
    squares = lax.psum(matrix_squares + gain_squares, ("seq", "head"))
    grad_norm = jnp.sqrt(squares)
    factor = CLIP_NORM / jnp.maximum(grad_norm, CLIP_NORM)
    in_new = adamw(
        inward,
        red_inward * factor,
        moment_inward,
        variance_inward,
        average_inward,
        RATE_INWARD,
        DECAY_MATRIX,
    )
    out_new = adamw(
        outward,
        red_outward * factor,
        moment_outward,
        variance_outward,
        average_outward,
        RATE_OUTWARD,
        DECAY_MATRIX,
    )
    up_new = adamw(
        expand,
        red_expand * factor,
        moment_expand,
        variance_expand,
        average_expand,
        RATE_EXPAND,
        DECAY_MATRIX,
    )
    down_new = adamw(
        contract,
        red_contract * factor,
        moment_contract,
        variance_contract,
        average_contract,
        RATE_CONTRACT,
        DECAY_MATRIX,
    )
    gain_new = adamw(
        norm_gains, red_gains * factor, moment_gains, variance_gains, average_gains, RATE_GAINS, 0.0
    )
    return (
        layer_output,
        input_grad,
        jnp.reshape(grad_norm, (1,)),
        in_new[0],
        in_new[1],
        in_new[2],
        in_new[3],
        out_new[0],
        out_new[1],
        out_new[2],
        out_new[3],
        up_new[0],
        up_new[1],
        up_new[2],
        up_new[3],
        down_new[0],
        down_new[1],
        down_new[2],
        down_new[3],
        gain_new[0],
        gain_new[1],
        gain_new[2],
        gain_new[3],
    )


def solution(mesh):
    placed = (
        P("seq", None),
        P("seq", None),
        P(),
        P("seq"),
        P("seq", None, "head"),
        P("head", "seq"),
        P("seq", "head"),
        P("head", "seq"),
        P(None, "seq"),
        P("seq", None, "head"),
        P("head", "seq"),
        P("seq", "head"),
        P("head", "seq"),
        P(None, "seq"),
        P("seq", None, "head"),
        P("head", "seq"),
        P("seq", "head"),
        P("head", "seq"),
        P(None, "seq"),
        P("seq", None, "head"),
        P("head", "seq"),
        P("seq", "head"),
        P("head", "seq"),
        P(None, "seq"),
    )
    return jax.shard_map(
        local,
        mesh=mesh,
        in_specs=placed,
        out_specs=(
            P("seq", None),
            P("seq", None),
            P(),
            P("seq", None, "head"),
            P("seq", None, "head"),
            P("seq", None, "head"),
            P("seq", None, "head"),
            P("head", "seq"),
            P("head", "seq"),
            P("head", "seq"),
            P("head", "seq"),
            P("seq", "head"),
            P("seq", "head"),
            P("seq", "head"),
            P("seq", "head"),
            P("head", "seq"),
            P("head", "seq"),
            P("head", "seq"),
            P("head", "seq"),
            P(None, "seq"),
            P(None, "seq"),
            P(None, "seq"),
            P(None, "seq"),
        ),
        check_vma=False,
    )
```

profile of v0, /device:TPU:0, one launch (start us, length us, event | category | flops | bytes accessed | tf_op | source)
XLA Modules:
  0.0 1921.1 jit_solution(1064347051506026774)
XLA Ops:
  10.7 22.5 %all_gather.21 = bf16[2,2048]{1,0:T(2,128)(2,1)S(1)} all-gather(bf16[2,256]{1,0:T(2,128)(2,1)S(1)} %convert_element_type.158), channel_id=1, replica_groups=mesh['seq'=8,'head'=4] {'seq'}, dimensions={1}, use_global_device_ids=true | all-gather | bytes 9216 | tf_op jit(solution)/shard_map/all_gather | solution.py:112
  37.9 75.4 %all-gather.9.cloned.1.call-done = bf16[2048,3,512]{0,2,1:T(8,128)(2,1)} async-done(((bf16[256,3,512]{0,2,1:T(8,128)(2,1)}), bf16[2048,3,512]{0,2,1:T(8,128)(2,1)}) %all-gather.9.cloned.1.call-update) | async-done | bytes 6291472 | tf_op jit(solution)/shard_map/all_gather | solution.py:108
  113.4 10.4 convolution_convert_fusion.7
  134.5 41.2 %all-gather.19.cloned.1.call-done = bf16[2048,1,512]{0,2,1:T(8,128)(2,1)} async-done(((bf16[256,1,512]{0,2,1:T(8,128)(2,1)}), bf16[2048,1,512]{0,2,1:T(8,128)(2,1)}) %all-gather.19.cloned.1.call-update) | async-done | bytes 2097168 | tf_op jit(solution)/shard_map/all_gather | solution.py:129
  175.8 3.9 copy.83
  179.7 48.0 %all-gather.17.cloned.1.call-done = bf16[2048,1,512]{0,2,1:T(8,128)(2,1)} async-done(((bf16[256,1,512]{0,2,1:T(8,128)(2,1)}), bf16[2048,1,512]{0,2,1:T(8,128)(2,1)}) %all-gather.17.cloned.1.call-update) | async-done | bytes 2097168 | tf_op jit(solution)/shard_map/all_gather | solution.py:128
  227.7 3.9 copy.81
  231.6 4.0 pad_maximum_fusion.1
  235.6 82.0 %while.38 = (s32[]{:T(128)}, bf16[2,512,4,128]{3,2,1,0:T(4,128)(2,1)}, f32[2,4,512]{2,1,0:T(4,128)S(1)}, s32[2]{0:T(128)S(1)}, s32[]{:T(128)}, /*index=5*/s32[]{...) while((s32[]{:T(128)}, ...), condition=%wide.region_5.6_spmd.clone.clone, body=%wide.region_2.5_spmd.clone.clone.sunk | while | flops 3026591744 | bytes 102862648 | solution.py:173
  240.3 11.3 fusion.158
  251.5 11.9 fusion.159
  263.5 11.7 fusion.160
  281.3 11.2 fusion.158
  292.5 11.8 fusion.159
  304.3 11.7 fusion.160
  317.7 6.3 convolution_convert_fusion.5
  326.8 3.2 convert_element_type.169
  331.4 76.3 %all-reduce.5.cloned.1.call-done = bf16[1024,2048]{1,0:T(8,128)(2,1)} async-done(((bf16[1024,2048]{1,0:T(8,128)(2,1)}), bf16[1024,2048]{1,0:T(8,128)(2,1)}) %all-reduce.5.cloned.1.call-update) | async-done | bytes 4194320 | tf_op jit(solution)/shard_map/psum | solution.py:54
  407.7 4.8 fusion.67
  415.8 119.8 %all-gather.13.cloned.1.call-done = bf16[2048,2048]{1,0:T(8,128)(2,1)} async-done(((bf16[256,2048]{1,0:T(8,128)(2,1)}), bf16[2048,2048]{1,0:T(8,128)(2,1)}) %all-gather.13.cloned.1.call-update) | async-done | bytes 8388624 | tf_op jit(solution)/shard_map/all_gather | solution.py:110
  535.6 15.8 fusion.83
  551.4 110.6 %all-gather.15.cloned.1.call-done = bf16[2048,2048]{1,0:T(8,128)(2,1)} async-done(((bf16[2048,256]{1,0:T(8,128)(2,1)}), bf16[2048,2048]{1,0:T(8,128)(2,1)}) %all-gather.15.cloned.1.call-update) | async-done | bytes 8388624 | tf_op jit(solution)/shard_map/all_gather | solution.py:111
  662.0 18.0 fusion.66
  682.2 13.0 convolution_convert_fusion.3
  695.3 83.7 %all-reduce.7.cloned.1.call-done = bf16[1024,2048]{1,0:T(8,128)(2,1)} async-done(((bf16[1024,2048]{1,0:T(8,128)(2,1)}), bf16[1024,2048]{1,0:T(8,128)(2,1)}) %all-reduce.7.cloned.1.call-update) | async-done | bytes 4194320 | tf_op jit(solution)/shard_map/psum | solution.py:58
  779.0 9.6 fusion.57
  788.7 6.1 fusion.55
  794.8 3.7 fusion.87
  798.5 161.3 %while.39 = (s32[]{:T(128)}, f32[2816,4,128]{0,2,1:T(8,128)}, f32[2816,4,128]{0,2,1:T(8,128)}, bf16[2,512,4,128]{3,1,2,0:T(8,128)(2,1)}, s32[2]{0:T(128)S(1)}, /...) while((s32[]{:T(128)}, f32[2816,4,128]{0,2,1:T(8,128)}, ...), condition=%wide.region_15.16_spmd.clone.clone, body=%wide.region_13.15_spmd.clone.clone.sunk | while | flops 7480287232 | bytes 253587424 | solution.py:232
  805.4 12.9 fusion.170
  818.4 13.4 bitcast_add_fusion.5
  831.7 19.3 %multiply_reduce_fusion.3 = (f32[4,512]{1,0:T(4,128)S(1)}, f32[4,512,2816]{2,1,0:T(8,128)}) fusion(f32[4,512,2816]{2,1,0:T(8,128)} %fusion.170, f32[4,512]{1,0:T(4,128)S(1)} %dynamic-slice_bitcast_fusion.2, pred[512,2816]{1,0:T(8,128)(4,1)S(1)} %fusion.171, bf16[2816,4,128]{2,0,1:T(8,128)(2,1)} %get-tuple-element.1073, ...), kind=kOutput, calls=%fused_computation.26.clone.1 | convolution fusion | flops 1505228800 | bytes 51003396 | tf_op jit(solution)/shard_map/while/body/eval_jaxpr/qhd,khd->hqk/dot_general | solution.py:214
  851.0 16.3 multiply_convert_fusion.13
  867.3 5.1 fusion.172
  872.5 4.4 bitcast_add_fusion.4
  883.7 12.9 fusion.170
  896.6 14.6 bitcast_add_fusion.5
  911.2 19.3 %multiply_reduce_fusion.3 = (f32[4,512]{1,0:T(4,128)S(1)}, f32[4,512,2816]{2,1,0:T(8,128)}) fusion(f32[4,512,2816]{2,1,0:T(8,128)} %fusion.170, f32[4,512]{1,0:T(4,128)S(1)} %dynamic-slice_bitcast_fusion.2, pred[512,2816]{1,0:T(8,128)(4,1)S(1)} %fusion.171, bf16[2816,4,128]{2,0,1:T(8,128)(2,1)} %get-tuple-element.1073, ...), kind=kOutput, calls=%fused_computation.26.clone.1 | convolution fusion | flops 1505228800 | bytes 51003396 | tf_op jit(solution)/shard_map/while/body/eval_jaxpr/qhd,khd->hqk/dot_general | solution.py:214
  930.5 16.3 multiply_convert_fusion.13
  946.8 5.1 fusion.172
  952.0 7.5 bitcast_add_fusion.4
  959.9 2.9 convert.29
  964.7 2.9 convert.30
  970.9 15.9 convolution_convert_fusion.4
  988.9 44.2 %reduce-scatter.10.cloned.1.call-done = bf16[256,4,128]{0,2,1:T(8,128)(2,1)} async-done(((bf16[2048,4,128]{0,2,1:T(8,128)(2,1)}), bf16[256,4,128]{0,2,1:T(8,128)(2,1)}) %reduce-scatter.10.cloned.1.call-update) | async-done | bytes 262160 | tf_op jit(solution)/shard_map/reduce_scatter | solution.py:236
  1035.4 68.6 %reduce-scatter.12.cloned.1.call-done = bf16[256,4,128]{0,2,1:T(8,128)(2,1)} async-done(((bf16[2048,4,128]{0,2,1:T(8,128)(2,1)}), bf16[256,4,128]{0,2,1:T(8,128)(2,1)}) %reduce-scatter.12.cloned.1.call-update) | async-done | bytes 262160 | tf_op jit(solution)/shard_map/reduce_scatter | solution.py:239
  1105.7 11.1 bitcast_convert_fusion
  1118.0 7.1 convolution_convert_fusion.6
  1125.2 143.9 %all-reduce.9.cloned.1.call-done = (bf16[1024,2048]{1,0:T(8,128)(2,1)}, bf16[1024,2048]{1,0:T(8,128)(2,1)}) async-done(((bf16[1024,2048]{1,0:T(8,128)(2,1)}, bf16[1024,2048]{1,0:T(8,128)(2,1)}), (bf16[1024,2048]{1,0:T(8,128)(2,1)}, bf16[1024,2048]{1,0:T(8,128)(2,1)})) %all-reduce.9.cloned.1.call-update) | async-done | bytes 8388624 | tf_op jit(solution)/shard_map/psum | solution.py:54
  1269.2 6.2 fusion.59
  1276.5 16.4 convolution_convert_fusion
  1293.7 15.8 convolution_convert_fusion.1
  1311.3 12.3 convolution_convert_fusion.2
  1323.6 17.7 reduce-scatter.16.cloned.1.call-done
  1343.0 63.2 %reduce-scatter.22.cloned.1.call-done = bf16[256,2]{1,0:T(8,128)(2,1)} async-done(((bf16[2048,2]{1,0:T(8,128)(2,1)}), bf16[256,2]{1,0:T(8,128)(2,1)}) %reduce-scatter.22.cloned.1.call-update) | async-done | bytes 1040
  1408.4 150.2 %reduce-scatter.20.cloned.1.call-done = bf16[2048,256]{1,0:T(8,128)(2,1)} async-done(((bf16[2048,2048]{1,0:T(8,128)(2,1)}), bf16[2048,256]{1,0:T(8,128)(2,1)}) %reduce-scatter.20.cloned.1.call-update) | async-done | bytes 1048592 | tf_op jit(solution)/shard_map/reduce_scatter | solution.py:269
  1560.9 149.7 %reduce-scatter.18.cloned.1.call-done = bf16[256,2048]{1,0:T(8,128)(2,1)} async-done(((bf16[2048,2048]{1,0:T(8,128)(2,1)}), bf16[256,2048]{1,0:T(8,128)(2,1)}) %reduce-scatter.18.cloned.1.call-update) | async-done | bytes 1048592 | tf_op jit(solution)/shard_map/reduce_scatter | solution.py:266
  1713.0 118.9 %reduce-scatter.14.cloned.1.call-done = bf16[256,3,512]{2,0,1:T(8,128)(2,1)} async-done(((bf16[2048,3,512]{2,0,1:T(8,128)(2,1)}), bf16[256,3,512]{2,0,1:T(8,128)(2,1)}) %reduce-scatter.14.cloned.1.call-update) | async-done | bytes 786448 | tf_op jit(solution)/shard_map/reduce_scatter | solution.py:260
  1836.7 13.7 fusion.51
  1850.4 39.6 %psum.39 = f32[]{:T(128)} all-reduce(f32[]{:T(128)S(6)} %add.439), channel_id=1, replica_groups=mesh['seq'=8,'head'=4] {'seq','head'}, use_global_device_ids=true, to_apply=%region_33.34 | all-reduce | flops 1 | bytes 8 | tf_op jit(solution)/shard_map/psum | solution.py:284
  1891.4 3.0 multiply_add_fusion.3
  1894.4 6.4 multiply_add_fusion.2
  1901.8 5.1 multiply_add_fusion.1
  1908.5 4.7 multiply_add_fusion
  (252 shorter events, 75.6 us)
Async XLA Ops:
  7.2 106.2 %all-gather.9.cloned.1.call-start = ((), (), s32[]{:S(2)}) async-start(), calls=%async_computation.7 | async-start | bytes 7077888 | tf_op jit(solution)/shard_map/all_gather | solution.py:108
  9.8 166.0 %all-gather.19.cloned.1.call-start = ((), (), s32[]{:S(2)}) async-start(), calls=%async_computation.20 | async-start | bytes 2359296 | tf_op jit(solution)/shard_map/all_gather | solution.py:129
  9.9 26.2 %copy-start.2 = (bf16[1024,2048]{1,0:T(8,128)(2,1)S(1)}, bf16[1024,2048]{1,0:T(8,128)(2,1)}, u32[]{:S(2)}) copy-start(bf16[1024,2048]{1,0:T(8,128)(2,1)} %param.28) | copy-start | bytes 12582916
  36.0 87.7 %copy-start.46 = (f32[1024]{0:T(1024)}, f32[1024]{0:T(1024)S(1)}, u32[]{:S(2)}) copy-start(f32[1024]{0:T(1024)S(1)} %broadcast_multiply_fusion.5) | copy-start | bytes 12292
  37.3 86.5 %copy-start.48 = (f32[1024]{0:T(1024)}, f32[1024]{0:T(1024)S(1)}, u32[]{:S(2)}) copy-start(f32[1024]{0:T(1024)S(1)} %add_rsqrt_fusion.1) | copy-start | bytes 12292
  37.9 85.9 %copy-start.40 = (f32[1,2048]{1,0:T(1,128)}, f32[1,2048]{1,0:T(1,128)S(1)}, u32[]{:S(2)}) copy-start(f32[1,2048]{1,0:T(1,128)S(1)} %get-tuple-element.823) | copy-start | bytes 24580
  113.4 13.8 copy-start.27
  126.4 101.3 %all-gather.17.cloned.1.call-start = ((), (), s32[]{:S(2)}) async-start(), calls=%async_computation.19 | async-start | bytes 2359296 | tf_op jit(solution)/shard_map/all_gather | solution.py:128
  127.1 190.5 %all-gather.11.cloned.1.call-start = ((), (), s32[]{:S(2)}) async-start(), calls=%async_computation.8 | async-start | bytes 2359296 | tf_op jit(solution)/shard_map/all_gather | solution.py:109
  127.9 279.8 %all-reduce.5.cloned.1.call-start = ((), (), s32[]{:S(2)}) async-start(), calls=%async_computation.9 | async-start | bytes 8388608 | tf_op jit(solution)/shard_map/psum | solution.py:54
  251.5 11.9 copy-start.7
  263.5 11.8 copy-start.37
  292.5 11.8 copy-start.7
  304.3 11.7 copy-start.37
  324.0 211.7 %all-gather.13.cloned.1.call-start = ((), (), s32[]{:S(2)}) async-start(), calls=%async_computation.10 | async-start | bytes 9437184 | tf_op jit(solution)/shard_map/all_gather | solution.py:110
  326.7 335.3 %all-gather.15.cloned.1.call-start = ((), (), s32[]{:S(2)}) async-start(), calls=%async_computation.11 | async-start | bytes 9437184 | tf_op jit(solution)/shard_map/all_gather | solution.py:111
  330.1 449.0 %all-reduce.7.cloned.1.call-start = ((), (), s32[]{:S(2)}) async-start(), calls=%async_computation.12 | async-start | bytes 8388608 | tf_op jit(solution)/shard_map/psum | solution.py:58
  331.4 457.2 %copy-start.53 = (f32[1024]{0:T(1024)}, f32[1024]{0:T(1024)S(1)}, u32[]{:S(2)}) copy-start(f32[1024]{0:T(1024)S(1)} %fusion.99) | copy-start | bytes 12292
  412.5 123.1 %copy-start.42 = (f32[1,2048]{1,0:T(1,128)S(1)}, f32[1,2048]{1,0:T(1,128)}, u32[]{:S(2)}) copy-start(f32[1,2048]{1,0:T(1,128)} %get-tuple-element.824) | copy-start | bytes 24580
  413.6 375.0 %copy-start.44 = (f32[1024]{0:T(1024)}, f32[1024]{0:T(1024)S(1)}, u32[]{:S(2)}) copy-start(f32[1024]{0:T(1024)S(1)} %broadcast_multiply_fusion.4) | copy-start | bytes 12292
  415.8 372.8 %copy-start.50 = (f32[1024]{0:T(1024)}, f32[1024]{0:T(1024)S(1)}, u32[]{:S(2)}) copy-start(f32[1024]{0:T(1024)S(1)} %add_rsqrt_fusion) | copy-start | bytes 12292
  695.2 337.8 %reduce-scatter.10.cloned.1.call-start = ((), (), s32[]{:S(2)}) async-start(), calls=%async_computation.13 | async-start | bytes 2359296 | tf_op jit(solution)/shard_map/reduce_scatter | solution.py:236
  779.0 9.6 copy-start.4
  779.0 9.6 copy-start.6
  779.0 9.6 copy-start.10
  788.7 6.1 copy-start.59
  805.4 12.9 copy-start.15
  851.0 16.3 copy-start.34
  883.7 12.9 copy-start.15
  930.5 16.3 copy-start.34
  952.0 7.5 copy-start.35
  952.0 7.5 copy-start.1
  962.8 24.0 %copy-start.11 = (bf16[2816,4,128]{0,2,1:T(8,128)(2,1)}, bf16[2816,4,128]{0,2,1:T(8,128)(2,1)S(1)}, u32[]{:S(2)}) copy-start(bf16[2816,4,128]{0,2,1:T(8,128)(2,1)S(1)} %convert.29) | copy-start | bytes 8650756
  964.7 139.4 %reduce-scatter.12.cloned.1.call-start = ((), (), s32[]{:S(2)}) async-start(), calls=%async_computation.14 | async-start | bytes 2359296 | tf_op jit(solution)/shard_map/reduce_scatter | solution.py:239
  970.8 298.3 %all-reduce.9.cloned.1.call-start = ((), (), s32[]{:S(2)}) async-start(), calls=%async_computation.22 | async-start | bytes 16777216 | tf_op jit(solution)/shard_map/psum | solution.py:54
  970.9 15.9 copy-start.36
  986.8 46.2 %slice-start = ((bf16[2816,4,128]{0,2,1:T(8,128)(2,1)}), bf16[768,4,128]{0,2,1:T(8,128)(2,1)S(1)}, s32[]{:S(2)}) async-start(bf16[2816,4,128]{0,2,1:T(8,128)(2,1)} %copy-done.11), calls=%async_computation.23 | async-start | bytes 1572864 | tf_op jit(solution)/shard_map/slice | solution.py:243
  986.8 117.2 %slice-start.1 = ((bf16[2816,4,128]{0,2,1:T(8,128)(2,1)}), bf16[768,4,128]{0,2,1:T(8,128)(2,1)S(1)}, s32[]{:S(2)}) async-start(bf16[2816,4,128]{0,2,1:T(8,128)(2,1)} %copy-done.12), calls=%async_computation.24 | async-start | bytes 1572864 | tf_op jit(solution)/shard_map/slice | solution.py:246
  1105.7 11.1 copy-start.32
  1116.8 8.4 copy-start.52
  1116.8 152.4 %copy-start.41 = (f32[1,2048]{1,0:T(1,128)S(1)}, f32[1,2048]{1,0:T(1,128)}, u32[]{:S(2)}) copy-start(f32[1,2048]{1,0:T(1,128)} %copy-done.40) | copy-start | bytes 24580
  1116.8 152.4 %copy-start.47 = (f32[1024]{0:T(1024)S(1)}, f32[1024]{0:T(1024)}, u32[]{:S(2)}) copy-start(f32[1024]{0:T(1024)} %copy-done.46) | copy-start | bytes 12292
  1116.8 152.3 %copy-start.49 = (f32[1024]{0:T(1024)S(1)}, f32[1024]{0:T(1024)}, u32[]{:S(2)}) copy-start(f32[1024]{0:T(1024)} %copy-done.48) | copy-start | bytes 12292
  1116.8 224.5 %reduce-scatter.16.cloned.1.call-start = ((), (), s32[]{:S(2)}) async-start(), calls=%async_computation.16 | async-start | bytes 2359296 | tf_op jit(solution)/shard_map/reduce_scatter | solution.py:263
  1125.1 151.4 %copy-start.54 = (f32[1024]{0:T(1024)S(1)}, f32[1024]{0:T(1024)}, u32[]{:S(2)}) copy-start(f32[1024]{0:T(1024)} %copy-done.53) | copy-start | bytes 12292
  1125.2 281.1 %reduce-scatter.22.cloned.1.call-start = ((), (), s32[]{:S(2)}) async-start(), calls=%async_computation.21 | async-start | bytes 589824
  1276.5 282.1 %reduce-scatter.20.cloned.1.call-start = ((), (), s32[]{:S(2)}) async-start(), calls=%async_computation.18 | async-start | bytes 9437184 | tf_op jit(solution)/shard_map/reduce_scatter | solution.py:269
  1293.0 417.6 %reduce-scatter.18.cloned.1.call-start = ((), (), s32[]{:S(2)}) async-start(), calls=%async_computation.17 | async-start | bytes 9437184 | tf_op jit(solution)/shard_map/reduce_scatter | solution.py:266
  1309.5 522.4 %reduce-scatter.14.cloned.1.call-start = ((), (), s32[]{:S(2)}) async-start(), calls=%async_computation.15 | async-start | bytes 7077888 | tf_op jit(solution)/shard_map/reduce_scatter | solution.py:260
  1836.6 54.1 %copy-start.55 = (f32[2,256]{1,0:T(2,128)S(1)}, f32[2,256]{1,0:T(2,128)}, u32[]{:S(2)}) copy-start(f32[2,256]{1,0:T(2,128)} %param.36) | copy-start | bytes 6148
  1836.6 54.1 %copy-start.56 = (f32[2,256]{1,0:T(2,128)S(1)}, f32[2,256]{1,0:T(2,128)}, u32[]{:S(2)}) copy-start(f32[2,256]{1,0:T(2,128)} %param.51) | copy-start | bytes 6148
  1836.6 54.1 %copy-start.57 = (f32[2,256]{1,0:T(2,128)S(1)}, f32[2,256]{1,0:T(2,128)}, u32[]{:S(2)}) copy-start(f32[2,256]{1,0:T(2,128)} %param.46) | copy-start | bytes 6148
  1836.7 54.1 %copy-start.58 = (f32[2,256]{1,0:T(2,128)S(1)}, f32[2,256]{1,0:T(2,128)}, u32[]{:S(2)}) copy-start(f32[2,256]{1,0:T(2,128)} %param.41) | copy-start | bytes 6148
  1836.7 54.7 %copy-start.28 = (f32[512,256]{1,0:T(8,128)S(1)}, f32[512,256]{1,0:T(8,128)}, u32[]{:S(2)}) copy-start(f32[512,256]{1,0:T(8,128)} %param.33) | copy-start | bytes 1572868
  1836.7 54.7 %copy-start.29 = (bf16[512,256]{1,0:T(8,128)(2,1)S(1)}, bf16[512,256]{1,0:T(8,128)(2,1)}, u32[]{:S(2)}) copy-start(bf16[512,256]{1,0:T(8,128)(2,1)} %reduce-scatter.16.cloned.1.call-done) | copy-start | bytes 786436
  1836.7 57.7 %copy-start.16 = (f32[256,3,512]{2,0,1:T(8,128)S(1)}, f32[256,3,512]{2,0,1:T(8,128)}, u32[]{:S(2)}) copy-start(f32[256,3,512]{2,0,1:T(8,128)} %param.32) | copy-start | bytes 4718596
  1836.7 57.7 %copy-start.20 = (bf16[256,3,512]{2,0,1:T(8,128)(2,1)S(1)}, bf16[256,3,512]{2,0,1:T(8,128)(2,1)}, u32[]{:S(2)}) copy-start(bf16[256,3,512]{2,0,1:T(8,128)(2,1)} %reduce-scatter.14.cloned.1.call-done) | copy-start | bytes 2359300
  1894.4 6.4 copy-start.13
  1894.4 6.4 copy-start.18
  1894.4 6.4 copy-start.21
  1894.4 6.4 copy-start.22
  1894.4 7.3 copy-start.23
  1901.8 6.1 copy-start.25
  1901.8 6.7 copy-start.26
  (24 other events, 73.7 us)
Sparse Core Ops, SparseCore 0:
  10.6 102.6 all-gather.8
  126.5 49.2 all-gather.18
  178.4 49.2 all-gather.16
  230.2 49.1 all-gather.10
  324.1 83.6 all-reduce.4
  410.5 125.0 all-gather.12
  538.4 123.5 all-gather.14
  695.3 83.6 all-reduce.6
  964.8 68.1 reduce-scatter.9
  1037.0 67.0 reduce-scatter.11
  1116.9 152.2 all-reduce.8
  1273.1 68.1 reduce-scatter.15
  1345.2 60.9 reduce-scatter.21
  1410.1 148.3 reduce-scatter.19
  1562.6 147.9 reduce-scatter.17
  1714.5 117.3 reduce-scatter.13
where the time goes:
time: 1930 us; the launch traced here: 1920 us
  waiting for transfers between devices  1310 us (68%)
  matrix products  306 us (16%)
  other arithmetic  165 us (9%)
  blocking collectives  62.1 us (3%)
  local copies, waits for them, and re-layouts  45.7 us (2%)
  between operations  21.3 us (1%)
    psum x2, waiting for transfers between devices, head_total(): lax.psum(partial_sum.astype(jnp.bfloat16), 'head').astype(jnp.float32)  220 us
    reduce_scatter x1, waiting for transfers between devices, local(): lax.psum_scatter(grad_contract.astype(jnp.bfloat16), 'seq', scatter_dimen...  150 us
    reduce_scatter x1, waiting for transfers between devices, local(): lax.psum_scatter(grad_expand.astype(jnp.bfloat16), 'seq', scatter_dimensi...  150 us
    all_gather x1, waiting for transfers between devices, local(): lax.all_gather(shard_copies[2], 'seq', axis=0, tiled=True)  120 us
    reduce_scatter x1, waiting for transfers between devices, local(): lax.psum_scatter(grad_inward.astype(jnp.bfloat16), 'seq', scatter_dimensi...  119 us
    all_gather x1, waiting for transfers between devices, local(): lax.all_gather(shard_copies[3], 'seq', axis=1, tiled=True)  111 us
    psum x1, waiting for transfers between devices, input_total(): lax.psum(partial_sum.astype(jnp.bfloat16), 'head').astype(jnp.float32)  83.7 us
    all_gather x1, waiting for transfers between devices, local(): lax.all_gather(shard_copies[0], 'seq', axis=0, tiled=True)  75.4 us
  transfers between devices with their start and end apart: 16, of which 15 were waited for; matrix products, arithmetic and copies ran while one was open for 12% of the time, Pallas kernels for 0%

commit v1 on v0

v1 whole, which is shorter than its diff:
```python
import functools

import jax
import jax.numpy as jnp
from jax import lax
from jax.experimental import pallas as pl
from jax.experimental.pallas import tpu as pltpu
from jax.sharding import PartitionSpec as P

HEAD_DIM = 128
PRE_DEV = 256
SOL_DEV = 768
STEP = 10
BLOCK = 256

EPS_NORM = 1e-05
BETA_ONE = 0.9
BETA_TWO = 0.95
ADAM_EPS = 1e-08
EMA_KEEP = 0.7
CLIP_NORM = 1.0
DECAY_MATRIX = 0.1
RATE_INWARD = 0.05
RATE_OUTWARD = 0.15
RATE_EXPAND = 0.05
RATE_CONTRACT = 0.03
RATE_GAINS = 0.5

LOG2E = 1.4426950408889634
MASKED = -1e30
BF = jnp.bfloat16
FP = jnp.float32
VMEM_LIMIT = 56 * 1024 * 1024


def ring_order(count):
    depth = 4
    if count % depth or (count // depth) % 2:
        return list(range(count))
    width = count // depth
    order = [z * width for z in range(depth)]
    across = list(range(1, width))
    for z in reversed(range(depth)):
        order += [z * width + y for y in across]
        across = across[::-1]
    return order


class Ring:
    def __init__(self, count):
        self.count = count
        self.half = count // 2
        self.order = ring_order(count)
        self.up = [(self.order[i], self.order[(i + 1) % count]) for i in range(count)]
        self.down = [(b, a) for a, b in self.up]
        inverse = [0] * count
        for i, s in enumerate(self.order):
            inverse[s] = i
        self.inverse = inverse

    def ids(self):
        place = jnp.asarray(self.inverse, jnp.int32)[lax.axis_index("seq")]
        spots = (place + jnp.arange(self.count, dtype=jnp.int32)) % self.count
        return jnp.asarray(self.order, jnp.int32)[spots]

    def blocks_of(self):
        place = jnp.asarray(self.inverse, jnp.int32)[lax.axis_index("seq")]
        return (jnp.asarray(self.inverse, jnp.int32) - place) % self.count

    def gather(self, own):
        n, half = self.count, self.half
        blocks = [None] * n
        blocks[0] = own
        from_up = from_down = own
        for j in range(1, half):
            from_up = lax.ppermute(from_up, "seq", self.down)
            from_down = lax.ppermute(from_down, "seq", self.up)
            blocks[j] = from_up
            blocks[n - j] = from_down
        mid = own.shape[0] // 2
        blocks[half] = jnp.concatenate(
            [
                lax.ppermute(from_up[:mid], "seq", self.down),
                lax.ppermute(from_down[mid:], "seq", self.up),
            ],
            axis=0,
        )
        return blocks

    def scatter_sum(self, part):
        n, half = self.count, self.half
        far = part(half)
        mid = far.shape[0] // 2
        rising = lax.ppermute(far[:mid].astype(BF), "seq", self.up)
        falling = lax.ppermute(far[mid:].astype(BF), "seq", self.down)
        for j in range(half - 1, 0, -1):
            up_term = part(j)
            down_term = part(n - j)
            if j == half - 1:
                up_sum = jnp.concatenate([up_term[:mid] + rising.astype(FP), up_term[mid:]], 0)
                down_sum = jnp.concatenate([down_term[:mid], down_term[mid:] + falling.astype(FP)], 0)
            else:
                up_sum = up_term + rising.astype(FP)
                down_sum = down_term + falling.astype(FP)
            rising = lax.ppermute(up_sum.astype(BF), "seq", self.up)
            falling = lax.ppermute(down_sum.astype(BF), "seq", self.down)
        return part(0) + rising.astype(FP) + falling.astype(FP)


class Team:
    def __init__(self, count, rows):
        self.cores = 2 if count % 2 == 0 else 1
        self.chips = count // self.cores
        self.count = count
        self.half = rows // self.cores
        self.quarter = self.half // self.chips
        self.core_flip = [(i, i ^ 1) for i in range(count)]

    def shift(self, k):
        chips, cores = self.chips, self.cores
        return [
            (x * cores + c, ((x + k) % chips) * cores + c) for x in range(chips) for c in range(cores)
        ]

    def place(self):
        index = lax.axis_index("head")
        return index // self.cores, index % self.cores

    def first_row(self):
        x, c = self.place()
        return c * self.half + x * self.quarter

    def scatter_sum(self, part):
        x, c = self.place()
        got = None
        if self.cores == 2:
            away = part((1 - c) * self.half, self.half).astype(BF)
            got = lax.ppermute(away, "head", self.core_flip)

        def chip_sum(spot):
            term = part(c * self.half + spot * self.quarter, self.quarter)
            if got is None:
                return term
            other = lax.dynamic_slice_in_dim(got, spot * self.quarter, self.quarter, 0)
            return term + other.astype(FP)

        arrived = []
        for k in range(1, self.chips):
            arrived.append(
                lax.ppermute(chip_sum((x + k) % self.chips).astype(BF), "head", self.shift(k))
            )
        total = chip_sum(x)
        for other in arrived:
            total = total + other.astype(FP)
        return total

    def gather(self, own):
        x, c = self.place()
        parts = [own] + [lax.ppermute(own, "head", self.shift(-k)) for k in range(1, self.chips)]
        ordered = []
        for spot in range(self.chips):
            piece = parts[0]
            for k in range(1, self.chips):
                piece = jnp.where((spot - x) % self.chips == k, parts[k], piece)
            ordered.append(piece)
        half = jnp.concatenate(ordered, axis=0) if self.chips > 1 else own
        if self.cores == 1:
            return half
        other = lax.ppermute(half, "head", self.core_flip)
        return jnp.concatenate([jnp.where(c == 0, half, other), jnp.where(c == 0, other, half)], axis=0)


def total_of_all(value, seq_count, head_count):
    for axis, count in (("head", head_count), ("seq", seq_count)):
        step = 1
        while step < count:
            value = value + lax.ppermute(value, axis, [(i, i ^ step) for i in range(count)])
            step *= 2
    return value


def pick_columns(array, ids):
    rows, width = array.shape
    count = ids.shape[0]
    size = width // count

    def body(ids_ref, in_ref, out_ref):
        out_ref[...] = in_ref[...]

    return pl.pallas_call(
        body,
        grid_spec=pltpu.PrefetchScalarGridSpec(
            num_scalar_prefetch=1,
            grid=(count,),
            in_specs=[pl.BlockSpec((rows, size), lambda b, ids_ref: (0, ids_ref[b]))],
            out_specs=pl.BlockSpec((rows, size), lambda b, ids_ref: (0, b)),
        ),
        out_shape=jax.ShapeDtypeStruct(array.shape, array.dtype),
        compiler_params=pltpu.CompilerParams(vmem_limit_bytes=VMEM_LIMIT),
        name="pick_columns",
    )(ids, array)


def dot_nt(a, b):
    return lax.dot_general(a, b, (((1,), (1,)), ((), ())), preferred_element_type=FP)


def dot_nn(a, b):
    return lax.dot_general(a, b, (((1,), (0,)), ((), ())), preferred_element_type=FP)


def dot_tn(a, b):
    return lax.dot_general(a, b, (((0,), (0,)), ((), ())), preferred_element_type=FP)


def prefix_places(meta_ref, n):
    spot = lax.broadcasted_iota(jnp.int32, (1, PRE_DEV), 1)
    return jnp.concatenate([spot + meta_ref[3 + b] * PRE_DEV for b in range(n)], axis=1)


def masked_scores(meta_ref, q_ref, k_ref, kp_ref, places, block):
    limit_prefix = meta_ref[1]
    limit_answer = meta_ref[2]
    query = q_ref[pl.ds(block * BLOCK, BLOCK), :]
    score_pre = dot_nt(query, kp_ref[0])
    if block < PRE_DEV // BLOCK:
        row = lax.broadcasted_iota(jnp.int32, (BLOCK, 1), 0) + block * BLOCK
        reach = jnp.minimum(meta_ref[0] * PRE_DEV + row + 1, limit_prefix)
        return query, jnp.where(places < reach, score_pre, MASKED), None
    score_pre = jnp.where(places < limit_prefix, score_pre, MASKED)
    solution_row = block * BLOCK - PRE_DEV
    width = solution_row + BLOCK
    score_own = dot_nt(query, k_ref[pl.ds(PRE_DEV, width), :])
    row = lax.broadcasted_iota(jnp.int32, (BLOCK, 1), 0) + solution_row
    reach = jnp.minimum(row + 1, limit_answer)
    column = lax.broadcasted_iota(jnp.int32, (1, width), 1)
    return query, score_pre, jnp.where(column < reach, score_own, MASKED)


def attention_forward(meta, projected, prefix_kv):
    rows, width3 = projected.shape
    heads = width3 // (3 * HEAD_DIM)
    prefix = prefix_kv.shape[1]
    n = prefix // PRE_DEV
    scale = HEAD_DIM ** (-0.5) * LOG2E

    def body(meta_ref, q_ref, k_ref, v_ref, kp_ref, vp_ref, out_ref, log_ref):
        places = prefix_places(meta_ref, n)
        for block in range(rows // BLOCK):
            _, score_pre, score_own = masked_scores(meta_ref, q_ref, k_ref, kp_ref, places, block)
            top = jnp.max(score_pre, axis=-1, keepdims=True)
            if score_own is not None:
                top = jnp.maximum(top, jnp.max(score_own, axis=-1, keepdims=True))
            e_pre = jnp.exp2((score_pre - top) * scale)
            total = jnp.sum(e_pre, axis=-1, keepdims=True)
            out = dot_nn(e_pre.astype(BF), vp_ref[0])
            if score_own is not None:
                e_own = jnp.exp2((score_own - top) * scale)
                total = total + jnp.sum(e_own, axis=-1, keepdims=True)
                out = out + dot_nn(e_own.astype(BF), v_ref[pl.ds(PRE_DEV, score_own.shape[1]), :])
            out_ref[pl.ds(block * BLOCK, BLOCK), :] = (out / total).astype(BF)
            log_ref[0, pl.ds(block * BLOCK, BLOCK), :] = top * scale + jnp.log2(total)

    spec = lambda shift: pl.BlockSpec((rows, HEAD_DIM), lambda h, m: (0, h + shift))
    pre = lambda which: pl.BlockSpec((1, prefix, HEAD_DIM), lambda h, m: (which, 0, h))
    return pl.pallas_call(
        body,
        grid_spec=pltpu.PrefetchScalarGridSpec(
            num_scalar_prefetch=1,
            grid=(heads,),
            in_specs=[spec(0), spec(heads), spec(2 * heads), pre(0), pre(1)],
            out_specs=[spec(0), pl.BlockSpec((1, rows, 1), lambda h, m: (h, 0, 0))],
        ),
        out_shape=[
            jax.ShapeDtypeStruct((rows, heads * HEAD_DIM), BF),
            jax.ShapeDtypeStruct((heads, rows, 1), FP),
        ],
        compiler_params=pltpu.CompilerParams(vmem_limit_bytes=VMEM_LIMIT),
        name="attention_forward",
    )(meta, projected, projected, projected, prefix_kv, prefix_kv)


def attention_backward(meta, projected, prefix_kv, mixed, d_mixed, logs):
    rows, width3 = projected.shape
    heads = width3 // (3 * HEAD_DIM)
    prefix = prefix_kv.shape[1]
    n = prefix // PRE_DEV
    scale = HEAD_DIM ** (-0.5)

    def body(
        meta_ref, q_ref, k_ref, v_ref, kp_ref, vp_ref, o_ref, do_ref, log_ref,
        dq_ref, dpre_ref, dsol_ref, dk_pre, dv_pre, dk_own, dv_own,
    ):
        places = prefix_places(meta_ref, n)
        dk_own[...] = jnp.zeros_like(dk_own)
        dv_own[...] = jnp.zeros_like(dv_own)
        for block in range(rows // BLOCK):
            spot = pl.ds(block * BLOCK, BLOCK)
            query, score_pre, score_own = masked_scores(
                meta_ref, q_ref, k_ref, kp_ref, places, block
            )
            d_out = do_ref[spot, :]
            log = log_ref[0, spot, :]
            inner = jnp.sum(d_out.astype(FP) * o_ref[spot, :].astype(FP), axis=-1, keepdims=True)
            p = jnp.exp2(score_pre * (scale * LOG2E) - log)
            ds = (p * (dot_nt(d_out, vp_ref[0]) - inner)).astype(BF)
            p = p.astype(BF)
            dq = dot_nn(ds, kp_ref[0])
            dk_term = dot_tn(ds, query)
            dv_term = dot_tn(p, d_out)
            if block == 0:
                dk_pre[...] = dk_term
                dv_pre[...] = dv_term
            else:
                dk_pre[...] += dk_term
                dv_pre[...] += dv_term
            if score_own is not None:
                keys = pl.ds(PRE_DEV, score_own.shape[1])
                p = jnp.exp2(score_own * (scale * LOG2E) - log)
                ds = (p * (dot_nt(d_out, v_ref[keys, :]) - inner)).astype(BF)
                p = p.astype(BF)
                dq = dq + dot_nn(ds, k_ref[keys, :])
                own = pl.ds(0, score_own.shape[1])
                dk_own[own, :] += dot_tn(ds, query)
                dv_own[own, :] += dot_tn(p, d_out)
            dq_ref[spot, :] = (dq * scale).astype(BF)
        dpre_ref[0] = (dk_pre[...] * scale).astype(BF)
        dpre_ref[1] = dv_pre[...].astype(BF)
        dsol_ref[0] = (dk_own[...] * scale).astype(BF)
        dsol_ref[1] = dv_own[...].astype(BF)

    sol = rows - PRE_DEV
    spec = lambda shift: pl.BlockSpec((rows, HEAD_DIM), lambda h, m: (0, h + shift))
    pre = lambda which: pl.BlockSpec((1, prefix, HEAD_DIM), lambda h, m: (which, 0, h))
    both = lambda size: pl.BlockSpec((2, size, HEAD_DIM), lambda h, m: (0, 0, h))
    return pl.pallas_call(
        body,
        grid_spec=pltpu.PrefetchScalarGridSpec(
            num_scalar_prefetch=1,
            grid=(heads,),
            in_specs=[
                spec(0), spec(heads), spec(2 * heads), pre(0), pre(1), spec(0), spec(0),
                pl.BlockSpec((1, rows, 1), lambda h, m: (h, 0, 0)),
            ],
            out_specs=[spec(0), both(prefix), both(sol)],
            scratch_shapes=[
                pltpu.VMEM((prefix, HEAD_DIM), FP),
                pltpu.VMEM((prefix, HEAD_DIM), FP),
                pltpu.VMEM((sol, HEAD_DIM), FP),
                pltpu.VMEM((sol, HEAD_DIM), FP),
            ],
        ),
        out_shape=[
            jax.ShapeDtypeStruct((rows, heads * HEAD_DIM), BF),
            jax.ShapeDtypeStruct((2, prefix, heads * HEAD_DIM), BF),
            jax.ShapeDtypeStruct((2, sol, heads * HEAD_DIM), BF),
        ],
        compiler_params=pltpu.CompilerParams(vmem_limit_bytes=VMEM_LIMIT),
        name="attention_backward",
    )(meta, projected, projected, projected, prefix_kv, prefix_kv, mixed, d_mixed, logs)


def layer_norm(values, gain_row):
    center = values - jnp.mean(values, axis=-1, keepdims=True)
    inverse = lax.rsqrt(jnp.mean(center * center, axis=-1, keepdims=True) + EPS_NORM)
    normal_unit = center * inverse
    return (normal_unit * gain_row, normal_unit, inverse)


def norm_back(incoming, normal_unit, inverse, gain_row):
    scaled = incoming * gain_row
    inner_sum = (
        scaled
        - jnp.mean(scaled, axis=-1, keepdims=True)
        - normal_unit * jnp.mean(scaled * normal_unit, axis=-1, keepdims=True)
    )
    return (inner_sum * inverse, jnp.sum(incoming * normal_unit, axis=0))


def adamw(weight, gradient, moment, variance, average, step_rate, decay_rate):
    moment = BETA_ONE * moment + (1.0 - BETA_ONE) * gradient
    variance = BETA_TWO * variance + (1.0 - BETA_TWO) * gradient * gradient
    corrected = moment / (1.0 - BETA_ONE**STEP)
    scaled_root = jnp.sqrt(variance / (1.0 - BETA_TWO**STEP)) + ADAM_EPS
    weight_new = weight - step_rate * corrected / scaled_root - step_rate * decay_rate * weight
    average = EMA_KEEP * average + (1.0 - EMA_KEEP) * weight_new
    return (moment, variance, weight_new, average)


def after(value, *others):
    return lax.optimization_barrier((value,) + others)[0]


def local(
    seq_count,
    head_count,
    tokens,
    cotangent,
    prefix_length,
    answer_lengths,
    inward,
    outward,
    expand,
    contract,
    norm_gains,
    moment_inward,
    moment_outward,
    moment_expand,
    moment_contract,
    moment_gains,
    variance_inward,
    variance_outward,
    variance_expand,
    variance_contract,
    variance_gains,
    average_inward,
    average_outward,
    average_expand,
    average_contract,
    average_gains,
):
    device = lax.axis_index("seq")
    tok_dev, model = tokens.shape
    share = model // seq_count
    local_width = outward.shape[0]
    limit_prefix = prefix_length[0]
    limit_answer = answer_lengths[0]
    ring = Ring(seq_count)
    team = Team(head_count, tok_dev)
    ids = ring.ids()
    blocks_of = ring.blocks_of()
    meta = jnp.concatenate([jnp.stack([device, limit_prefix, limit_answer]).astype(jnp.int32), ids])
    first = team.first_row()

    in_blocks = ring.gather(inward.astype(BF).reshape(share, 3 * local_width))
    in_matrix = jnp.concatenate(in_blocks, axis=0)
    gain_rows = lax.all_gather(norm_gains.astype(BF), "seq", axis=1, tiled=True)
    gain_pair = jnp.take(gain_rows.reshape(2, seq_count, share), ids, axis=1)
    gain_pair = gain_pair.reshape(2, model).astype(FP)

    source_low = pick_columns(tokens, ids)
    normed_one = layer_norm(source_low.astype(FP), gain_pair[0])[0].astype(BF)
    projected = jnp.dot(normed_one, in_matrix, preferred_element_type=FP).astype(BF)

    own_kv = jnp.stack(
        [
            projected[:PRE_DEV, local_width : 2 * local_width],
            projected[:PRE_DEV, 2 * local_width :],
        ]
    )
    prefix_kv = jnp.concatenate(ring.gather(own_kv), axis=1)
    out_matrix = jnp.concatenate(ring.gather(after(outward, in_blocks[1]).astype(BF)), axis=1)
    up_matrix = jnp.concatenate(ring.gather(after(expand, in_blocks[2]).astype(BF)), axis=0)
    down_matrix = jnp.concatenate(ring.gather(after(contract, in_blocks[3]).astype(BF)), axis=1)
    mixed, logs = attention_forward(meta, projected, prefix_kv)

    def attention_part(start, size):
        return jnp.dot(
            lax.dynamic_slice_in_dim(mixed, start, size, 0), out_matrix, preferred_element_type=FP
        )

    source_own = lax.dynamic_slice_in_dim(source_low, first, team.quarter, 0).astype(FP)
    hidden = source_own + team.scatter_sum(attention_part)
    normed_two_own, unit_two, inverse_two = layer_norm(hidden, gain_pair[1])
    normed_two = team.gather(normed_two_own.astype(BF))
    up_values = jnp.dot(normed_two, up_matrix, preferred_element_type=FP)
    activation_values, gelu_back = jax.vjp(
        lambda entry: jax.nn.gelu(entry, approximate=True), up_values
    )
    activation = activation_values.astype(BF)

    def down_part(start, size):
        return jnp.dot(
            lax.dynamic_slice_in_dim(activation, start, size, 0),
            down_matrix,
            preferred_element_type=FP,
        )

    result = (hidden + team.scatter_sum(down_part)).astype(BF)
    layer_output = pick_columns(team.gather(result), blocks_of)

    position_all = jnp.arange(tok_dev, dtype=jnp.int32)
    valid_rows = jnp.where(
        position_all < PRE_DEV,
        device * PRE_DEV + position_all < limit_prefix,
        position_all - PRE_DEV < limit_answer,
    )
    out_grad = jnp.where(valid_rows[:, None], pick_columns(cotangent, ids), 0).astype(BF)

    def column_block(array, b):
        return array[:, b * share : (b + 1) * share]

    def part_contract(b):
        return jnp.einsum(
            "tf,td->fd", activation, column_block(out_grad, b), preferred_element_type=FP
        )

    red_contract = ring.scatter_sum(part_contract)
    d_activation = jnp.einsum("td,fd->tf", out_grad, down_matrix, preferred_element_type=FP)
    d_up = gelu_back(d_activation)[0].astype(BF)

    def up_back_part(start, size):
        return jnp.einsum(
            "tf,df->td",
            lax.dynamic_slice_in_dim(d_up, start, size, 0),
            up_matrix,
            preferred_element_type=FP,
        )

    d_normed_two = team.scatter_sum(up_back_part)

    def part_expand(b):
        return jnp.einsum(
            "td,tf->df", column_block(normed_two, b), d_up, preferred_element_type=FP
        )

    red_expand = ring.scatter_sum(part_expand)
    d_norm_part, gain_two = norm_back(d_normed_two, unit_two, inverse_two, gain_pair[1])
    out_grad_own = lax.dynamic_slice_in_dim(out_grad, first, team.quarter, 0).astype(FP)
    d_hidden = out_grad_own + d_norm_part
    d_attention = team.gather(d_hidden.astype(BF))
    d_mixed = jnp.einsum("td,nd->tn", d_attention, out_matrix, preferred_element_type=FP).astype(BF)

    def part_outward(b):
        return jnp.einsum(
            "tn,td->nd", mixed, column_block(d_attention, b), preferred_element_type=FP
        )

    red_outward = ring.scatter_sum(part_outward)
    d_query, d_prefix, d_solution = attention_backward(
        meta, projected, prefix_kv, mixed, d_mixed, logs
    )

    def part_prefix(b):
        return d_prefix[:, b * PRE_DEV : (b + 1) * PRE_DEV].astype(FP)

    d_prefix_own = ring.scatter_sum(part_prefix).astype(BF)
    d_kv = jnp.concatenate([d_prefix_own, d_solution], axis=1)
    d_projected = jnp.concatenate([d_query, d_kv[0], d_kv[1]], axis=1)

    def in_back_part(start, size):
        return jnp.einsum(
            "tn,dn->td",
            lax.dynamic_slice_in_dim(d_projected, start, size, 0),
            in_matrix,
            preferred_element_type=FP,
        )

    def part_inward(b):
        return jnp.einsum(
            "td,tn->dn", column_block(normed_one, b), d_projected, preferred_element_type=FP
        )

    red_inward = ring.scatter_sum(part_inward)
    d_normed_one = team.scatter_sum(in_back_part)
    _, unit_one, inverse_one = layer_norm(source_own, gain_pair[0])
    d_source, gain_one = norm_back(d_normed_one, unit_one, inverse_one, gain_pair[0])
    input_low = team.gather((d_hidden + d_source).astype(BF))
    input_grad = pick_columns(input_low, blocks_of).astype(FP)

    gains = jnp.stack([gain_one, gain_two]).reshape(2, seq_count, share)
    gains = jnp.take(gains, blocks_of, axis=1)
    gains = total_of_all(gains, seq_count, head_count)
    red_gains = lax.dynamic_slice_in_dim(gains, device, 1, 1)[:, 0]
    squares = total_of_all(
        jnp.sum(red_inward * red_inward)
        + jnp.sum(red_outward * red_outward)
        + jnp.sum(red_expand * red_expand)
        + jnp.sum(red_contract * red_contract),
        seq_count,
        head_count,
    )
    grad_norm = jnp.sqrt(squares + jnp.sum(gains * gains))
    factor = CLIP_NORM / jnp.maximum(grad_norm, CLIP_NORM)

    in_new = adamw(
        inward, red_inward.reshape(inward.shape) * factor, moment_inward, variance_inward,
        average_inward, RATE_INWARD, DECAY_MATRIX,
    )
    out_new = adamw(
        outward, red_outward * factor, moment_outward, variance_outward, average_outward,
        RATE_OUTWARD, DECAY_MATRIX,
    )
    up_new = adamw(
        expand, red_expand * factor, moment_expand, variance_expand, average_expand,
        RATE_EXPAND, DECAY_MATRIX,
    )
    down_new = adamw(
        contract, red_contract * factor, moment_contract, variance_contract, average_contract,
        RATE_CONTRACT, DECAY_MATRIX,
    )
    gain_new = adamw(
        norm_gains, red_gains * factor, moment_gains, variance_gains, average_gains, RATE_GAINS, 0.0
    )
    return (
        (layer_output, input_grad, jnp.reshape(grad_norm, (1,)))
        + in_new + out_new + up_new + down_new + gain_new
    )


def solution(mesh):
    in_place = P("seq", None, "head")
    out_place = P("head", "seq")
    up_place = P("seq", "head")
    gain_place = P(None, "seq")
    weights = (in_place, out_place, up_place, out_place, gain_place)
    placed = (P("seq", None), P("seq", None), P(), P("seq")) + weights * 4
    results = (P("seq", None), P("seq", None), P())
    for place in weights:
        results += (place,) * 4
    return jax.shard_map(
        functools.partial(local, mesh.shape["seq"], mesh.shape["head"]),
        mesh=mesh,
        in_specs=placed,
        out_specs=results,
        check_vma=False,
    )
```

time: 1930 us -> 936 us (0.48)
  waiting for transfers between devices: 1310 us -> 359 us
  matrix products: 306 us -> 168 us
  starting transfers between devices: 0.83 us -> 103 us
  Pallas kernels: 0 us -> 84.1 us
  other arithmetic: 165 us -> 93.3 us
  blocking collectives: 62.1 us -> 22.1 us
  local copies, waits for them, and re-layouts: 45.7 us -> 84.5 us
    reduce_scatter x6 -> x0, waiting for transfers between devices: 549 us -> none  [the longest x1 150 us: local(): lax.psum_scatter(grad_contract.astype(jnp.bfloat16), 'seq', scatter_dimen...]
    all_gather x6 -> x0, waiting for transfers between devices: 395 us -> none  [the longest x1 120 us: local(): lax.all_gather(shard_copies[2], 'seq', axis=0, tiled=True)]
    ppermute x0 -> x106, waiting for transfers between devices: none -> 359 us  [the longest x15 87.1 us: scatter_sum(): falling = lax.ppermute(down_sum.astype(BF), 'seq', self.down)]
    psum x3 -> x0, waiting for transfers between devices: 304 us -> none  [the longest x2 220 us: head_total(): lax.psum(partial_sum.astype(jnp.bfloat16), 'head').astype(jnp.float32)]
    dot_general x26 -> x48, matrix products: 306 us -> 168 us  [the longest x3 23 us: up_back_part(): jnp.einsum('tf,df->td', lax.dynamic_slice_in_dim(d_up, start, size, 0), u...]
    ppermute x0 -> x106, starting transfers between devices: none -> 103 us  [the longest x15 21.2 us: gather(): from_down = lax.ppermute(from_down, 'seq', self.up)]
    pallas_call x0 -> x6, Pallas kernels: none -> 84.1 us  [the longest x1 33.9 us: attention_backward(): pl.pallas_call(body, grid_spec=pltpu.PrefetchScalarGridSpec(num_scalar_pr...]
    unnamed x17 -> x0, waiting for transfers between devices: 64.1 us -> none
  transfers between devices with their start and end apart: 16 -> 106, of which waited for: 15 -> 48; matrix products, arithmetic and copies ran while one was open for 12% -> 28% of each run, Pallas kernels for 0% -> 7%
where the time goes in v1:
time: 936 us; the launch traced here: 925 us
  waiting for transfers between devices  359 us (38%)
  matrix products  168 us (18%)
  starting transfers between devices  103 us (11%)
  other arithmetic  93.3 us (10%)
  local copies, waits for them, and re-layouts  84.5 us (9%)
  Pallas kernels  84.1 us (9%)
  blocking collectives  22.1 us (2%)
  between operations  11.7 us (1%)
    ppermute x15, waiting for transfers between devices, scatter_sum(): falling = lax.ppermute(down_sum.astype(BF), 'seq', self.down)  87.1 us
    ppermute x15, waiting for transfers between devices, gather(): from_up = lax.ppermute(from_up, 'seq', self.down)  76.1 us
    unnamed x200, local copies, waits for them, and re-layouts  68.7 us
    ppermute x5, waiting for transfers between devices, gather(): lax.ppermute(from_up[:mid], 'seq', self.down)  43.1 us
    pallas_call x1, Pallas kernels, attention_backward(): pl.pallas_call(body, grid_spec=pltpu.PrefetchScalarGridSpec(num_scalar_pr...  33.9 us
    pallas_call x4, Pallas kernels, pick_columns(): pl.pallas_call(body, grid_spec=pltpu.PrefetchScalarGridSpec(num_scalar_pr...  29.5 us
    ppermute x4, waiting for transfers between devices, scatter_sum(): lax.ppermute(chip_sum((x + k) % self.chips).astype(BF), 'head', self.shif...  28.8 us
    ppermute x5, waiting for transfers between devices, scatter_sum(): falling = lax.ppermute(far[mid:].astype(BF), 'seq', self.down)  28.5 us
  transfers between devices with their start and end apart: 106, of which 48 were waited for; matrix products, arithmetic and copies ran while one was open for 28% of the time, Pallas kernels for 7%

profile of v1, /device:TPU:0, one launch (start us, length us, event | category | flops | bytes accessed | tf_op | source)
XLA Modules:
  0.0 925.4 jit_solution(15989755114163381587)
XLA Ops:
  8.2 7.4 pick_columns.4
  15.7 22.1 %all_gather.3 = bf16[2,2048]{1,0:T(2,128)(2,1)S(1)} all-gather(bf16[2,256]{1,0:T(2,128)(2,1)S(1)} %convert_element_type.342), channel_id=1, replica_groups=mesh['seq'=8,'head'=4] {'seq'}, dimensions={1}, use_global_device_ids=true | all-gather | bytes 9216 | tf_op jit(solution)/shard_map/all_gather | solution.py:437
  44.7 4.5 fusion.4
  57.9 14.6 %collective-permute-done.16 = bf16[512,256]{1,0:T(8,128)(2,1)} collective-permute-done((bf16[512,256]{1,0:T(8,128)(2,1)S(1)}, bf16[512,256]{1,0:T(8,128)(2,1)}, u32[]{:S(2)}, u32[]{:S(2)}) %collective-permute-start.16) | collective-permute-done | bytes 262176 | tf_op jit(solution)/shard_map/ppermute | solution.py:76
  80.1 7.4 pick_columns.6
  93.6 8.9 collective-permute-done.22
  122.7 8.8 convolution_convert_fusion.q_ref.k_ref.v_ref
  135.5 11.2 %collective-permute-done.8 = bf16[2,256,512]{2,1,0:T(8,128)(2,1)S(1)} collective-permute-done((bf16[2,256,512]{2,1,0:T(8,128)(2,1)S(1)}, bf16[2,256,512]{2,1,0:T(8,128)(2,1)S(1)}, u32[]{:S(2)}, u32[]{:S(2)}) %collective-permute-start.8) | collective-permute-done | bytes 524320 | tf_op jit(solution)/shard_map/ppermute | solution.py:76
  150.6 26.8 %collective-permute-done.9 = bf16[2,256,512]{2,1,0:T(8,128)(2,1)S(1)} collective-permute-done((bf16[2,256,512]{2,1,0:T(8,128)(2,1)S(1)}, bf16[2,256,512]{2,1,0:T(8,128)(2,1)S(1)}, u32[]{:S(2)}, u32[]{:S(2)}) %collective-permute-start.9) | collective-permute-done | bytes 524320 | tf_op jit(solution)/shard_map/ppermute | solution.py:76
  181.0 11.3 %collective-permute-done.14 = bf16[2,256,512]{2,1,0:T(8,128)(2,1)S(1)} collective-permute-done((bf16[2,256,512]{2,1,0:T(8,128)(2,1)S(1)}, bf16[2,256,512]{2,1,0:T(8,128)(2,1)S(1)}, u32[]{:S(2)}, u32[]{:S(2)}) %collective-permute-start.14) | collective-permute-done | bytes 524320 | tf_op jit(solution)/shard_map/ppermute | solution.py:77
  196.7 4.9 collective-permute-done.15
  203.8 16.6 %collective-permute-done.11 = bf16[1,256,512]{2,1,0:T(8,128)(2,1)S(1)} collective-permute-done((bf16[1,256,512]{2,1,0:T(8,128)(2,1)S(1)}, bf16[1,256,512]{2,1,0:T(8,128)(2,1)S(1)}, u32[]{:S(2)}, u32[]{:S(2)}) %collective-permute-start.11) | collective-permute-done | bytes 262176 | tf_op jit(solution)/shard_map/ppermute | solution.py:83
  222.5 20.7 %attention_forward.1 = (bf16[1024,512]{1,0:T(8,128)(2,1)}, f32[4,1024,1]{2,1,0:T(8,128)}) custom-call(s32[11]{0:T(128)} %pad_add_fusion.meta_ref, bf16[1024,1536]{1,0:T(8,128)(2,1)} %copy-done.7, bf16[1024,1536]{1,0:T(8,128)(2,1)} %copy-done.7, bf16[1024,1536]{1,0:T(8,128)(2,1)} %copy-done.7, bf16[2,2048,512]{2,1,0:T(8,128)(2,1)} %copy-done.11, ...), custom_call_target="tpu_custom_call" | custom-call | tf_op jit(solution)/shard_map/attention_forward/pallas_call | solution.py:266
  243.2 3.8 convolution_convert_fusion.4
  270.3 5.4 collective-permute-done.37
  280.1 18.1 %collective-permute-done.30 = bf16[256,2048]{1,0:T(8,128)(2,1)} collective-permute-done((bf16[256,2048]{1,0:T(8,128)(2,1)}, bf16[256,2048]{1,0:T(8,128)(2,1)}, u32[]{:S(2)}, u32[]{:S(2)}) %collective-permute-start.30) | collective-permute-done | bytes 1048608 | tf_op jit(solution)/shard_map/ppermute | solution.py:76
  307.3 24.1 %collective-permute-done.31 = bf16[128,2048]{1,0:T(8,128)(2,1)S(1)} collective-permute-done((bf16[128,2048]{1,0:T(8,128)(2,1)S(1)}, bf16[128,2048]{1,0:T(8,128)(2,1)S(1)}, u32[]{:S(2)}, u32[]{:S(2)}) %collective-permute-start.31) | collective-permute-done | bytes 524320 | tf_op jit(solution)/shard_map/ppermute | solution.py:83
  345.9 4.1 collective-permute-done.43
  355.8 10.6 %collective-permute-done.26 = bf16[256,2048]{1,0:T(8,128)(2,1)S(1)} collective-permute-done((bf16[256,2048]{1,0:T(8,128)(2,1)S(1)}, bf16[256,2048]{1,0:T(8,128)(2,1)S(1)}, u32[]{:S(2)}, u32[]{:S(2)}) %collective-permute-start.26) | collective-permute-done | bytes 1048608 | tf_op jit(solution)/shard_map/ppermute | solution.py:159
  370.0 13.6 %fusion.200 = f32[1024,2048]{1,0:T(8,128)} fusion(bf16[1024,2048]{1,0:T(8,128)(2,1)S(1)} %copy-done.27, bf16[2048,2048]{1,0:T(8,128)(2,1)} %constant_dynamic-update-slice_fusion.32), kind=kOutput, calls=%fused_computation.425 | convolution fusion | flops 8589934592 | bytes 20971520 | tf_op jit(solution)/shard_map/td,fd->tf/dot_general | solution.py:499
  384.7 22.1 %fusion.11 = (bf16[1024,2048]{1,0:T(8,128)(2,1)S(1)}, bf16[1024,2048]{1,0:T(8,128)(2,1)}) fusion(f32[1024,2048]{1,0:T(8,128)} %fusion.200, bf16[2048,2048]{1,0:T(8,128)(2,1)} %constant_dynamic-update-slice_fusion.23, bf16[512,2048]{1,0:T(8,128)(2,1)S(1)} %get-tuple-element.117, bf16[512,2048]{1,0:T(8,128)(2,1)S(1)} %get-tuple-element.116), kind=kOutput, calls=%fused_computation.52 | convolution fusion | flops 8644460544 | bytes 29360128 | tf_op jit(solution)/shard_map/dot_general | solution.py:466
  406.7 9.2 convolution_convert_fusion.2
  420.8 9.3 %convolution_convert_fusion.3 = bf16[512,2048]{1,0:T(8,128)(2,1)} fusion(bf16[2048,2048]{1,0:T(8,128)(2,1)} %constant_dynamic-update-slice_fusion.32, bf16[1024,2048]{1,0:T(8,128)(2,1)S(1)} %copy-done.77, s32[]{:T(128)S(6)} %select_n.257), kind=kOutput, calls=%fused_computation.68 | convolution fusion | flops 4296015872 | bytes 12582916 | tf_op jit(solution)/shard_map/dot_general | solution.py:473
  447.4 9.2 collective-permute-done.84
  459.1 8.7 collective-permute-done.92
  472.2 18.0 %collective-permute-done.85 = bf16[256,2048]{1,0:T(8,128)(2,1)S(1)} collective-permute-done((bf16[256,2048]{1,0:T(8,128)(2,1)S(1)}, bf16[256,2048]{1,0:T(8,128)(2,1)S(1)}, u32[]{:S(2)}, u32[]{:S(2)}) %collective-permute-start.85) | collective-permute-done | bytes 1048608 | tf_op jit(solution)/shard_map/ppermute | solution.py:106
  496.6 7.0 fusion.22
  503.6 9.2 collective-permute-done.93
  518.7 18.3 %collective-permute-done.49 = bf16[256,2048]{1,0:T(8,128)(2,1)S(1)} collective-permute-done((bf16[256,2048]{1,0:T(8,128)(2,1)}, bf16[256,2048]{1,0:T(8,128)(2,1)S(1)}, u32[]{:S(2)}, u32[]{:S(2)}) %collective-permute-start.49) | collective-permute-done | bytes 1048608 | tf_op jit(solution)/shard_map/ppermute | solution.py:150
  538.3 6.8 multiply_reduce_fusion
  549.0 6.1 fusion.21
  560.5 13.1 %collective-permute-done.50 = bf16[256,2048]{1,0:T(8,128)(2,1)S(1)} collective-permute-done((bf16[256,2048]{1,0:T(8,128)(2,1)S(1)}, bf16[256,2048]{1,0:T(8,128)(2,1)S(1)}, u32[]{:S(2)}, u32[]{:S(2)}) %collective-permute-start.50) | collective-permute-done | bytes 1048608 | tf_op jit(solution)/shard_map/ppermute | solution.py:159
  579.0 3.5 fusion.25
  582.5 10.4 %collective-permute-done.45 = bf16[256,2048]{1,0:T(8,128)(2,1)S(1)} collective-permute-done((bf16[256,2048]{1,0:T(8,128)(2,1)S(1)}, bf16[256,2048]{1,0:T(8,128)(2,1)S(1)}, u32[]{:S(2)}, u32[]{:S(2)}) %collective-permute-start.45) | collective-permute-done | bytes 1048608 | tf_op jit(solution)/shard_map/ppermute | solution.py:150
  594.5 7.4 fusion.20
  607.1 3.6 multiply_reduce_fusion.1
  612.3 3.3 fusion.47.do_ref
  615.6 33.9 %attention_backward.1 = (bf16[1024,512]{1,0:T(8,128)(2,1)}, bf16[2,2048,512]{2,1,0:T(8,128)(2,1)}, bf16[2,768,512]{2,1,0:T(8,128)(2,1)}) custom-call(s32[11]{0:T(128)} %pad_add_fusion.meta_ref, bf16[1024,1536]{1,0:T(8,128)(2,1)} %copy-done.7, bf16[1024,1536]{1,0:T(8,128)(2,1)} %copy-done.7, bf16[1024,1536]{1,0:T(8,128)(2,1)} %copy-done.7, ...), custom_call_target="tpu_custom_call" | custom-call | tf_op jit(solution)/shard_map/attention_backward/pallas_call | solution.py:336
  653.0 4.9 multiply_reduce_fusion.2
  664.9 5.9 collective-permute-done.53
  674.1 5.1 collective-permute-done.57
  686.4 10.1 %collective-permute-done.58 = bf16[2,256,512]{2,1,0:T(8,128)(2,1)S(1)} collective-permute-done((bf16[2,256,512]{2,1,0:T(8,128)(2,1)S(1)}, bf16[2,256,512]{2,1,0:T(8,128)(2,1)S(1)}, u32[]{:S(2)}, u32[]{:S(2)}) %collective-permute-start.58) | collective-permute-done | bytes 524320 | tf_op jit(solution)/shard_map/ppermute | solution.py:106
  698.9 3.3 collective-permute-done.77
  702.9 9.9 %collective-permute-done.59 = bf16[2,256,512]{2,1,0:T(8,128)(2,1)S(1)} collective-permute-done((bf16[2,256,512]{2,1,0:T(8,128)(2,1)S(1)}, bf16[2,256,512]{2,1,0:T(8,128)(2,1)S(1)}, u32[]{:S(2)}, u32[]{:S(2)}) %collective-permute-start.59) | collective-permute-done | bytes 524320 | tf_op jit(solution)/shard_map/ppermute | solution.py:106
  719.9 3.6 convolution_convert_fusion.1
  725.2 10.0 %collective-permute-done.68 = bf16[128,1536]{1,0:T(8,128)(2,1)S(1)} collective-permute-done((bf16[128,1536]{1,0:T(8,128)(2,1)S(1)}, bf16[128,1536]{1,0:T(8,128)(2,1)S(1)}, u32[]{:S(2)}, u32[]{:S(2)}) %collective-permute-start.68) | collective-permute-done | bytes 393248 | tf_op jit(solution)/shard_map/ppermute | solution.py:95
  735.9 10.0 %collective-permute-done.64 = bf16[128,1536]{1,0:T(8,128)(2,1)S(1)} collective-permute-done((bf16[128,1536]{1,0:T(8,128)(2,1)S(1)}, bf16[128,1536]{1,0:T(8,128)(2,1)S(1)}, u32[]{:S(2)}, u32[]{:S(2)}) %collective-permute-start.64) | collective-permute-done | bytes 393248 | tf_op jit(solution)/shard_map/ppermute | solution.py:94
  750.5 13.7 %collective-permute-done.69 = bf16[256,1536]{1,0:T(8,128)(2,1)S(1)} collective-permute-done((bf16[256,1536]{1,0:T(8,128)(2,1)S(1)}, bf16[256,1536]{1,0:T(8,128)(2,1)S(1)}, u32[]{:S(2)}, u32[]{:S(2)}) %collective-permute-start.69) | collective-permute-done | bytes 786464 | tf_op jit(solution)/shard_map/ppermute | solution.py:106
  774.4 13.0 %collective-permute-done.70 = bf16[256,1536]{1,0:T(8,128)(2,1)S(1)} collective-permute-done((bf16[256,1536]{1,0:T(8,128)(2,1)S(1)}, bf16[256,1536]{1,0:T(8,128)(2,1)S(1)}, u32[]{:S(2)}, u32[]{:S(2)}) %collective-permute-start.70) | collective-permute-done | bytes 786464 | tf_op jit(solution)/shard_map/ppermute | solution.py:106
  794.6 5.0 fusion.39
  806.4 4.5 collective-permute-done.67
  810.9 4.3 multiply_reduce_fusion.7
  838.0 3.3 collective-permute-done.103
  842.0 3.1 collective-permute-done.104
  845.6 3.6 fusion.38
  851.4 3.3 broadcast_multiply_fusion
  854.7 3.2 copy.56
  857.9 5.9 multiply_add_fusion.5
  879.6 7.3 multiply_add_fusion.2
  886.9 6.8 multiply_add_fusion
  893.7 4.1 broadcast_select_fusion.2
  900.1 7.3 pick_columns.5
  910.0 7.4 pick_columns.7
  917.4 6.7 convert_element_type.396
  (537 shorter events, 304.6 us)
Async XLA Ops:
  2.7 46.5 %collective-permute-start = (bf16[256,1536]{0,1:T(8,128)(2,1)S(1)}, bf16[256,1536]{0,1:T(8,128)(2,1)}, u32[]{:S(2)}, u32[]{:S(2)}) collective-permute-start(bf16[256,1536]{0,1:T(8,128)(2,1)S(1)} %bitcast.86), channel_id=1, source_target_pairs={{8,0},{16,8},{24,16},{28,24},{20,28},{12,20},{4,12},{0,4},{9,1},{1... | collective-permute-start | bytes 2359304 | tf_op jit(solution)/shard_map/ppermute | solution.py:76
  5.7 46.5 %collective-permute-start.4 = (bf16[256,1536]{0,1:T(8,128)(2,1)S(1)}, bf16[256,1536]{0,1:T(8,128)(2,1)}, u32[]{:S(2)}, u32[]{:S(2)}) collective-permute-start(bf16[256,1536]{0,1:T(8,128)(2,1)S(1)} %bitcast.87), channel_id=1, source_target_pairs={{0,8},{8,16},{16,24},{24,28},{28,20},{20,12},{12,4},{4,0},{1,9},{9... | collective-permute-start | bytes 2359304 | tf_op jit(solution)/shard_map/ppermute | solution.py:77
  49.2 27.2 %collective-permute-start.1 = (bf16[256,1536]{0,1:T(8,128)(2,1)}, bf16[256,1536]{0,1:T(8,128)(2,1)}, u32[]{:S(2)}, u32[]{:S(2)}) collective-permute-start(bf16[256,1536]{0,1:T(8,128)(2,1)} %collective-permute-done), channel_id=1, source_target_pairs={{8,0},{16,8},{24,16},{28,24},{20,28},{12,20},{4,12},{0,4},{9,1},{1... | collective-permute-start | bytes 2359304 | tf_op jit(solution)/shard_map/ppermute | solution.py:76
  52.2 26.7 %collective-permute-start.5 = (bf16[256,1536]{0,1:T(8,128)(2,1)}, bf16[256,1536]{0,1:T(8,128)(2,1)}, u32[]{:S(2)}, u32[]{:S(2)}) collective-permute-start(bf16[256,1536]{0,1:T(8,128)(2,1)} %collective-permute-done.4), channel_id=1, source_target_pairs={{0,8},{8,16},{16,24},{24,28},{28,20},{20,12},{12,4},{4,0},{1,9},{9... | collective-permute-start | bytes 2359304 | tf_op jit(solution)/shard_map/ppermute | solution.py:77
  53.0 19.5 %collective-permute-start.16 = (bf16[512,256]{1,0:T(8,128)(2,1)S(1)}, bf16[512,256]{1,0:T(8,128)(2,1)}, u32[]{:S(2)}, u32[]{:S(2)}) collective-permute-start(bf16[512,256]{1,0:T(8,128)(2,1)S(1)} %get-tuple-element.99), channel_id=1, source_target_pairs={{8,0},{16,8},{24,16},{28,24},{20,28},{12,20},{4,12},{0,4},{9,1},{1... | collective-permute-start | bytes 786440 | tf_op jit(solution)/shard_map/ppermute | solution.py:76
  54.4 21.3 %collective-permute-start.20 = (bf16[512,256]{1,0:T(8,128)(2,1)S(1)}, bf16[512,256]{1,0:T(8,128)(2,1)S(1)}, u32[]{:S(2)}, u32[]{:S(2)}) collective-permute-start(bf16[512,256]{1,0:T(8,128)(2,1)S(1)} %get-tuple-element.99), channel_id=1, source_target_pairs={{0,8},{8,16},{16,24},{24,28},{28,20},{20,12},{12,4},{4,0},{1,9},{9... | collective-permute-start | bytes 786440 | tf_op jit(solution)/shard_map/ppermute | solution.py:77
  76.3 28.3 %collective-permute-start.2 = (bf16[256,1536]{0,1:T(8,128)(2,1)}, bf16[256,1536]{0,1:T(8,128)(2,1)}, u32[]{:S(2)}, u32[]{:S(2)}) collective-permute-start(bf16[256,1536]{0,1:T(8,128)(2,1)} %collective-permute-done.1), channel_id=1, source_target_pairs={{8,0},{16,8},{24,16},{28,24},{20,28},{12,20},{4,12},{0,4},{9,1},{1... | collective-permute-start | bytes 2359304 | tf_op jit(solution)/shard_map/ppermute | solution.py:76
  78.9 29.3 %collective-permute-start.6 = (bf16[256,1536]{0,1:T(8,128)(2,1)}, bf16[256,1536]{0,1:T(8,128)(2,1)S(1)}, u32[]{:S(2)}, u32[]{:S(2)}) collective-permute-start(bf16[256,1536]{0,1:T(8,128)(2,1)} %collective-permute-done.5), channel_id=1, source_target_pairs={{0,8},{8,16},{16,24},{24,28},{28,20},{20,12},{12,4},{4,0},{1,9},{9... | collective-permute-start | bytes 2359304 | tf_op jit(solution)/shard_map/ppermute | solution.py:77
  102.5 46.2 %collective-permute-start.23 = (bf16[256,256]{1,0:T(8,128)(2,1)S(1)}, bf16[256,256]{1,0:T(8,128)(2,1)S(1)}, u32[]{:S(2)}, u32[]{:S(2)}) collective-permute-start(bf16[256,256]{1,0:T(8,128)(2,1)S(1)} %slice.385), channel_id=1, source_target_pairs={{0,8},{8,16},{16,24},{24,28},{28,20},{20,12},{12,4},{4,0},{1,9},{9... | collective-permute-start | bytes 393224 | tf_op jit(solution)/shard_map/ppermute | solution.py:84
  103.7 46.8 %collective-permute-start.19 = (bf16[256,256]{1,0:T(8,128)(2,1)S(1)}, bf16[256,256]{1,0:T(8,128)(2,1)S(1)}, u32[]{:S(2)}, u32[]{:S(2)}) collective-permute-start(bf16[256,256]{1,0:T(8,128)(2,1)S(1)} %slice.384), channel_id=1, source_target_pairs={{8,0},{16,8},{24,16},{28,24},{20,28},{12,20},{4,12},{0,4},{9,1},{1... | collective-permute-start | bytes 393224 | tf_op jit(solution)/shard_map/ppermute | solution.py:83
  135.4 59.2 %collective-permute-start.28 = (bf16[256,2048]{1,0:T(8,128)(2,1)S(1)}, bf16[256,2048]{1,0:T(8,128)(2,1)}, u32[]{:S(2)}, u32[]{:S(2)}) collective-permute-start(bf16[256,2048]{1,0:T(8,128)(2,1)S(1)} %get-tuple-element.95), channel_id=1, source_target_pairs={{8,0},{16,8},{24,16},{28,24},{20,28},{12,20},{4,12},{0,4},{9,1},{1... | collective-permute-start | bytes 3145736 | tf_op jit(solution)/shard_map/ppermute | solution.py:76
  146.6 30.8 %collective-permute-start.9 = (bf16[2,256,512]{2,1,0:T(8,128)(2,1)S(1)}, bf16[2,256,512]{2,1,0:T(8,128)(2,1)S(1)}, u32[]{:S(2)}, u32[]{:S(2)}) collective-permute-start(bf16[2,256,512]{2,1,0:T(8,128)(2,1)S(1)} %collective-permute-done.8), channel_id=1, source_target_pairs={{8,0},{16,8},{24,16},{28,24},{20,28},{12,20},{4,12},{0,4},{9,1},{1... | collective-permute-start | bytes 1572872 | tf_op jit(solution)/shard_map/ppermute | solution.py:76
  146.6 30.8 %collective-permute-start.13 = (bf16[2,256,512]{2,1,0:T(8,128)(2,1)S(1)}, bf16[2,256,512]{2,1,0:T(8,128)(2,1)S(1)}, u32[]{:S(2)}, u32[]{:S(2)}) collective-permute-start(bf16[2,256,512]{2,1,0:T(8,128)(2,1)S(1)} %collective-permute-done.12), channel_id=1, source_target_pairs={{0,8},{8,16},{16,24},{24,28},{28,20},{20,12},{12,4},{4,0},{1,9},{9... | collective-permute-start | bytes 1572872 | tf_op jit(solution)/shard_map/ppermute | solution.py:77
  148.7 48.0 %collective-permute-start.32 = (bf16[256,2048]{1,0:T(8,128)(2,1)S(1)}, bf16[256,2048]{1,0:T(8,128)(2,1)S(1)}, u32[]{:S(2)}, u32[]{:S(2)}) collective-permute-start(bf16[256,2048]{1,0:T(8,128)(2,1)S(1)} %get-tuple-element.95), channel_id=1, source_target_pairs={{0,8},{8,16},{16,24},{24,28},{28,20},{20,12},{12,4},{4,0},{1,9},{9... | collective-permute-start | bytes 3145736 | tf_op jit(solution)/shard_map/ppermute | solution.py:77
  181.0 68.5 %collective-permute-start.36 = (bf16[2048,256]{1,0:T(8,128)(2,1)}, bf16[2048,256]{1,0:T(8,128)(2,1)}, u32[]{:S(2)}, u32[]{:S(2)}) collective-permute-start(bf16[2048,256]{1,0:T(8,128)(2,1)} %get-tuple-element.97), channel_id=1, source_target_pairs={{8,0},{16,8},{24,16},{28,24},{20,28},{12,20},{4,12},{0,4},{9,1},{1... | collective-permute-start | bytes 3145736 | tf_op jit(solution)/shard_map/ppermute | solution.py:76
  194.4 26.0 %collective-permute-start.11 = (bf16[1,256,512]{2,1,0:T(8,128)(2,1)S(1)}, bf16[1,256,512]{2,1,0:T(8,128)(2,1)S(1)}, u32[]{:S(2)}, u32[]{:S(2)}) collective-permute-start(bf16[1,256,512]{2,1,0:T(8,128)(2,1)S(1)} %slice.382), channel_id=1, source_target_pairs={{8,0},{16,8},{24,16},{28,24},{20,28},{12,20},{4,12},{0,4},{9,1},{1... | collective-permute-start | bytes 786440 | tf_op jit(solution)/shard_map/ppermute | solution.py:83
  194.6 54.9 %collective-permute-start.40 = (bf16[2048,256]{1,0:T(8,128)(2,1)}, bf16[2048,256]{1,0:T(8,128)(2,1)}, u32[]{:S(2)}, u32[]{:S(2)}) collective-permute-start(bf16[2048,256]{1,0:T(8,128)(2,1)} %get-tuple-element.97), channel_id=1, source_target_pairs={{0,8},{8,16},{16,24},{24,28},{28,20},{20,12},{12,4},{4,0},{1,9},{9... | collective-permute-start | bytes 3145736 | tf_op jit(solution)/shard_map/ppermute | solution.py:77
  196.7 54.8 %collective-permute-start.29 = (bf16[256,2048]{1,0:T(8,128)(2,1)}, bf16[256,2048]{1,0:T(8,128)(2,1)}, u32[]{:S(2)}, u32[]{:S(2)}) collective-permute-start(bf16[256,2048]{1,0:T(8,128)(2,1)} %collective-permute-done.28), channel_id=1, source_target_pairs={{8,0},{16,8},{24,16},{28,24},{20,28},{12,20},{4,12},{0,4},{9,1},{1... | collective-permute-start | bytes 3145736 | tf_op jit(solution)/shard_map/ppermute | solution.py:76
  201.6 50.0 %collective-permute-start.33 = (bf16[256,2048]{1,0:T(8,128)(2,1)S(1)}, bf16[256,2048]{1,0:T(8,128)(2,1)}, u32[]{:S(2)}, u32[]{:S(2)}) collective-permute-start(bf16[256,2048]{1,0:T(8,128)(2,1)S(1)} %collective-permute-done.32), channel_id=1, source_target_pairs={{0,8},{8,16},{16,24},{24,28},{28,20},{20,12},{12,4},{4,0},{1,9},{9... | collective-permute-start | bytes 3145736 | tf_op jit(solution)/shard_map/ppermute | solution.py:77
  247.0 54.5 %collective-permute-start.24 = (bf16[512,2048]{1,0:T(8,128)(2,1)}, bf16[512,2048]{1,0:T(8,128)(2,1)}, u32[]{:S(2)}, u32[]{:S(2)}) collective-permute-start(bf16[512,2048]{1,0:T(8,128)(2,1)} %convolution_convert_fusion.4), channel_id=1, source_target_pairs={{0,1},{1,0},{2,3},{3,2},{4,5},{5,4},{6,7},{7,6},{8,9},{9,8},{10,11... | collective-permute-start | bytes 6291464 | tf_op jit(solution)/shard_map/ppermute | solution.py:138
  249.4 26.3 %collective-permute-start.37 = (bf16[2048,256]{1,0:T(8,128)(2,1)}, bf16[2048,256]{1,0:T(8,128)(2,1)}, u32[]{:S(2)}, u32[]{:S(2)}) collective-permute-start(bf16[2048,256]{1,0:T(8,128)(2,1)} %collective-permute-done.36), channel_id=1, source_target_pairs={{8,0},{16,8},{24,16},{28,24},{20,28},{12,20},{4,12},{0,4},{9,1},{1... | collective-permute-start | bytes 3145736 | tf_op jit(solution)/shard_map/ppermute | solution.py:76
  249.5 26.3 %collective-permute-start.41 = (bf16[2048,256]{1,0:T(8,128)(2,1)}, bf16[2048,256]{1,0:T(8,128)(2,1)}, u32[]{:S(2)}, u32[]{:S(2)}) collective-permute-start(bf16[2048,256]{1,0:T(8,128)(2,1)} %collective-permute-done.40), channel_id=1, source_target_pairs={{0,8},{8,16},{16,24},{24,28},{28,20},{20,12},{12,4},{4,0},{1,9},{9... | collective-permute-start | bytes 3145736 | tf_op jit(solution)/shard_map/ppermute | solution.py:77
  251.5 46.7 %collective-permute-start.30 = (bf16[256,2048]{1,0:T(8,128)(2,1)}, bf16[256,2048]{1,0:T(8,128)(2,1)}, u32[]{:S(2)}, u32[]{:S(2)}) collective-permute-start(bf16[256,2048]{1,0:T(8,128)(2,1)} %collective-permute-done.29), channel_id=1, source_target_pairs={{8,0},{16,8},{24,16},{28,24},{20,28},{12,20},{4,12},{0,4},{9,1},{1... | collective-permute-start | bytes 3145736 | tf_op jit(solution)/shard_map/ppermute | solution.py:76
  251.6 47.8 %collective-permute-start.34 = (bf16[256,2048]{1,0:T(8,128)(2,1)}, bf16[256,2048]{1,0:T(8,128)(2,1)S(1)}, u32[]{:S(2)}, u32[]{:S(2)}) collective-permute-start(bf16[256,2048]{1,0:T(8,128)(2,1)} %collective-permute-done.33), channel_id=1, source_target_pairs={{0,8},{8,16},{16,24},{24,28},{28,20},{20,12},{12,4},{4,0},{1,9},{9... | collective-permute-start | bytes 3145736 | tf_op jit(solution)/shard_map/ppermute | solution.py:77
  275.7 62.1 %collective-permute-start.38 = (bf16[2048,256]{1,0:T(8,128)(2,1)}, bf16[2048,256]{1,0:T(8,128)(2,1)S(1)}, u32[]{:S(2)}, u32[]{:S(2)}) collective-permute-start(bf16[2048,256]{1,0:T(8,128)(2,1)} %collective-permute-done.37), channel_id=1, source_target_pairs={{8,0},{16,8},{24,16},{28,24},{20,28},{12,20},{4,12},{0,4},{9,1},{1... | collective-permute-start | bytes 3145736 | tf_op jit(solution)/shard_map/ppermute | solution.py:76
  275.8 60.6 %collective-permute-start.42 = (bf16[2048,256]{1,0:T(8,128)(2,1)}, bf16[2048,256]{1,0:T(8,128)(2,1)S(1)}, u32[]{:S(2)}, u32[]{:S(2)}) collective-permute-start(bf16[2048,256]{1,0:T(8,128)(2,1)} %collective-permute-done.41), channel_id=1, source_target_pairs={{0,8},{8,16},{16,24},{24,28},{28,20},{20,12},{12,4},{4,0},{1,9},{9... | collective-permute-start | bytes 3145736 | tf_op jit(solution)/shard_map/ppermute | solution.py:77
  299.3 32.1 %collective-permute-start.31 = (bf16[128,2048]{1,0:T(8,128)(2,1)S(1)}, bf16[128,2048]{1,0:T(8,128)(2,1)S(1)}, u32[]{:S(2)}, u32[]{:S(2)}) collective-permute-start(bf16[128,2048]{1,0:T(8,128)(2,1)S(1)} %slice.387), channel_id=1, source_target_pairs={{8,0},{16,8},{24,16},{28,24},{20,28},{12,20},{4,12},{0,4},{9,1},{1... | collective-permute-start | bytes 1572872 | tf_op jit(solution)/shard_map/ppermute | solution.py:83
  299.5 32.8 %collective-permute-start.35 = (bf16[128,2048]{1,0:T(8,128)(2,1)S(1)}, bf16[128,2048]{1,0:T(8,128)(2,1)S(1)}, u32[]{:S(2)}, u32[]{:S(2)}) collective-permute-start(bf16[128,2048]{1,0:T(8,128)(2,1)S(1)} %slice.388), channel_id=1, source_target_pairs={{0,8},{8,16},{16,24},{24,28},{28,20},{20,12},{12,4},{4,0},{1,9},{9... | collective-permute-start | bytes 1572872 | tf_op jit(solution)/shard_map/ppermute | solution.py:84
  303.4 35.2 %collective-permute-start.25 = (bf16[256,2048]{1,0:T(8,128)(2,1)S(1)}, bf16[256,2048]{1,0:T(8,128)(2,1)S(1)}, u32[]{:S(2)}, u32[]{:S(2)}) collective-permute-start(bf16[256,2048]{1,0:T(8,128)(2,1)S(1)} %fusion.23), channel_id=1, source_target_pairs={{0,2},{1,3},{2,0},{3,1},{4,6},{5,7},{6,4},{7,5},{8,10},{9,11},{10,... | collective-permute-start | bytes 3145736 | tf_op jit(solution)/shard_map/ppermute | solution.py:150
  342.1 24.3 %collective-permute-start.26 = (bf16[256,2048]{1,0:T(8,128)(2,1)S(1)}, bf16[256,2048]{1,0:T(8,128)(2,1)S(1)}, u32[]{:S(2)}, u32[]{:S(2)}) collective-permute-start(bf16[256,2048]{1,0:T(8,128)(2,1)S(1)} %multiply_convert_fusion.1), channel_id=1, source_target_pairs={{0,2},{1,3},{2,0},{3,1},{4,6},{5,7},{6,4},{7,5},{8,10},{9,11},{10,... | collective-permute-start | bytes 3145736 | tf_op jit(solution)/shard_map/ppermute | solution.py:159
  441.1 54.1 %collective-permute-start.48 = (bf16[512,2048]{1,0:T(8,128)(2,1)S(1)}, bf16[512,2048]{1,0:T(8,128)(2,1)}, u32[]{:S(2)}, u32[]{:S(2)}) collective-permute-start(bf16[512,2048]{1,0:T(8,128)(2,1)S(1)} %copy-done.76), channel_id=1, source_target_pairs={{0,1},{1,0},{2,3},{3,2},{4,5},{5,4},{6,7},{7,6},{8,9},{9,8},{10,11... | collective-permute-start | bytes 6291464 | tf_op jit(solution)/shard_map/ppermute | solution.py:138
  441.5 106.1 %collective-permute-start.44 = (bf16[512,2048]{1,0:T(8,128)(2,1)}, bf16[512,2048]{1,0:T(8,128)(2,1)}, u32[]{:S(2)}, u32[]{:S(2)}) collective-permute-start(bf16[512,2048]{1,0:T(8,128)(2,1)} %convolution_convert_fusion.3), channel_id=1, source_target_pairs={{0,1},{1,0},{2,3},{3,2},{4,5},{5,4},{6,7},{7,6},{8,9},{9,8},{10,11... | collective-permute-start | bytes 6291464 | tf_op jit(solution)/shard_map/ppermute | solution.py:138
  444.1 23.7 %collective-permute-start.92 = (bf16[1024,256]{1,0:T(8,128)(2,1)S(1)}, bf16[1024,256]{1,0:T(8,128)(2,1)S(1)}, u32[]{:S(2)}, u32[]{:S(2)}) collective-permute-start(bf16[1024,256]{1,0:T(8,128)(2,1)S(1)} %get-tuple-element.131), channel_id=1, source_target_pairs={{8,0},{16,8},{24,16},{28,24},{20,28},{12,20},{4,12},{0,4},{9,1},{1... | collective-permute-start | bytes 1572872 | tf_op jit(solution)/shard_map/ppermute | solution.py:95
  458.1 32.2 %collective-permute-start.85 = (bf16[256,2048]{1,0:T(8,128)(2,1)S(1)}, bf16[256,2048]{1,0:T(8,128)(2,1)S(1)}, u32[]{:S(2)}, u32[]{:S(2)}) collective-permute-start(bf16[256,2048]{1,0:T(8,128)(2,1)S(1)} %pad_maximum_fusion.15), channel_id=1, source_target_pairs={{8,0},{16,8},{24,16},{28,24},{20,28},{12,20},{4,12},{0,4},{9,1},{1... | collective-permute-start | bytes 3145736 | tf_op jit(solution)/shard_map/ppermute | solution.py:106
  467.8 25.4 %collective-permute-start.81 = (bf16[256,2048]{1,0:T(8,128)(2,1)S(1)}, bf16[256,2048]{1,0:T(8,128)(2,1)S(1)}, u32[]{:S(2)}, u32[]{:S(2)}) collective-permute-start(bf16[256,2048]{1,0:T(8,128)(2,1)S(1)} %pad_maximum_fusion.14), channel_id=1, source_target_pairs={{0,8},{8,16},{16,24},{24,28},{28,20},{20,12},{12,4},{4,0},{1,9},{9... | collective-permute-start | bytes 3145736 | tf_op jit(solution)/shard_map/ppermute | solution.py:105
  470.3 42.5 %collective-permute-start.93 = (bf16[2048,256]{1,0:T(8,128)(2,1)}, bf16[2048,256]{1,0:T(8,128)(2,1)}, u32[]{:S(2)}, u32[]{:S(2)}) collective-permute-start(bf16[2048,256]{1,0:T(8,128)(2,1)} %pad_maximum_fusion.17), channel_id=1, source_target_pairs={{8,0},{16,8},{24,16},{28,24},{20,28},{12,20},{4,12},{0,4},{9,1},{1... | collective-permute-start | bytes 3145736 | tf_op jit(solution)/shard_map/ppermute | solution.py:106
  490.2 26.7 %collective-permute-start.89 = (bf16[2048,256]{1,0:T(8,128)(2,1)}, bf16[2048,256]{1,0:T(8,128)(2,1)S(1)}, u32[]{:S(2)}, u32[]{:S(2)}) collective-permute-start(bf16[2048,256]{1,0:T(8,128)(2,1)} %pad_maximum_fusion.16), channel_id=1, source_target_pairs={{0,8},{8,16},{16,24},{24,28},{28,20},{20,12},{12,4},{4,0},{1,9},{9... | collective-permute-start | bytes 3145736 | tf_op jit(solution)/shard_map/ppermute | solution.py:105
  493.2 61.9 %collective-permute-start.86 = (bf16[256,2048]{1,0:T(8,128)(2,1)S(1)}, bf16[256,2048]{1,0:T(8,128)(2,1)S(1)}, u32[]{:S(2)}, u32[]{:S(2)}) collective-permute-start(bf16[256,2048]{1,0:T(8,128)(2,1)S(1)} %fusion.28), channel_id=1, source_target_pairs={{8,0},{16,8},{24,16},{28,24},{20,28},{12,20},{4,12},{0,4},{9,1},{1... | collective-permute-start | bytes 3145736 | tf_op jit(solution)/shard_map/ppermute | solution.py:106
  495.3 82.3 %collective-permute-start.82 = (bf16[256,2048]{1,0:T(8,128)(2,1)S(1)}, bf16[256,2048]{1,0:T(8,128)(2,1)}, u32[]{:S(2)}, u32[]{:S(2)}) collective-permute-start(bf16[256,2048]{1,0:T(8,128)(2,1)S(1)} %fusion.26), channel_id=1, source_target_pairs={{0,8},{8,16},{16,24},{24,28},{28,20},{20,12},{12,4},{4,0},{1,9},{9... | collective-permute-start | bytes 3145736 | tf_op jit(solution)/shard_map/ppermute | solution.py:105
  512.8 24.2 %collective-permute-start.49 = (bf16[256,2048]{1,0:T(8,128)(2,1)}, bf16[256,2048]{1,0:T(8,128)(2,1)S(1)}, u32[]{:S(2)}, u32[]{:S(2)}) collective-permute-start(bf16[256,2048]{1,0:T(8,128)(2,1)} %fusion.22), channel_id=1, source_target_pairs={{0,2},{1,3},{2,0},{3,1},{4,6},{5,7},{6,4},{7,5},{8,10},{9,11},{10,... | collective-permute-start | bytes 3145736 | tf_op jit(solution)/shard_map/ppermute | solution.py:150
  516.9 41.1 %collective-permute-start.94 = (bf16[2048,256]{1,0:T(8,128)(2,1)}, bf16[2048,256]{1,0:T(8,128)(2,1)}, u32[]{:S(2)}, u32[]{:S(2)}) collective-permute-start(bf16[2048,256]{1,0:T(8,128)(2,1)} %add_convert_fusion.1), channel_id=1, source_target_pairs={{8,0},{16,8},{24,16},{28,24},{20,28},{12,20},{4,12},{0,4},{9,1},{1... | collective-permute-start | bytes 3145736 | tf_op jit(solution)/shard_map/ppermute | solution.py:106
  537.0 37.8 %collective-permute-start.90 = (bf16[2048,256]{1,0:T(8,128)(2,1)}, bf16[2048,256]{1,0:T(8,128)(2,1)}, u32[]{:S(2)}, u32[]{:S(2)}) collective-permute-start(bf16[2048,256]{1,0:T(8,128)(2,1)} %add_convert_fusion.3), channel_id=1, source_target_pairs={{0,8},{8,16},{16,24},{24,28},{28,20},{20,12},{12,4},{4,0},{1,9},{9... | collective-permute-start | bytes 3145736 | tf_op jit(solution)/shard_map/ppermute | solution.py:105
  547.5 26.1 %collective-permute-start.50 = (bf16[256,2048]{1,0:T(8,128)(2,1)S(1)}, bf16[256,2048]{1,0:T(8,128)(2,1)S(1)}, u32[]{:S(2)}, u32[]{:S(2)}) collective-permute-start(bf16[256,2048]{1,0:T(8,128)(2,1)S(1)} %get-tuple-element.92), channel_id=1, source_target_pairs={{0,2},{1,3},{2,0},{3,1},{4,6},{5,7},{6,4},{7,5},{8,10},{9,11},{10,... | collective-permute-start | bytes 3145736 | tf_op jit(solution)/shard_map/ppermute | solution.py:159
  555.2 37.7 %collective-permute-start.45 = (bf16[256,2048]{1,0:T(8,128)(2,1)S(1)}, bf16[256,2048]{1,0:T(8,128)(2,1)S(1)}, u32[]{:S(2)}, u32[]{:S(2)}) collective-permute-start(bf16[256,2048]{1,0:T(8,128)(2,1)S(1)} %fusion.21), channel_id=1, source_target_pairs={{0,2},{1,3},{2,0},{3,1},{4,6},{5,7},{6,4},{7,5},{8,10},{9,11},{10,... | collective-permute-start | bytes 3145736 | tf_op jit(solution)/shard_map/ppermute | solution.py:150
  558.0 95.0 %collective-permute-start.87 = (bf16[256,2048]{1,0:T(8,128)(2,1)}, bf16[256,2048]{1,0:T(8,128)(2,1)S(1)}, u32[]{:S(2)}, u32[]{:S(2)}) collective-permute-start(bf16[256,2048]{1,0:T(8,128)(2,1)} %fusion.27), channel_id=1, source_target_pairs={{8,0},{16,8},{24,16},{28,24},{20,28},{12,20},{4,12},{0,4},{9,1},{1... | collective-permute-start | bytes 3145736 | tf_op jit(solution)/shard_map/ppermute | solution.py:106
  573.6 31.0 %collective-permute-start.95 = (bf16[2048,256]{1,0:T(8,128)(2,1)S(1)}, bf16[2048,256]{1,0:T(8,128)(2,1)S(1)}, u32[]{:S(2)}, u32[]{:S(2)}) collective-permute-start(bf16[2048,256]{1,0:T(8,128)(2,1)S(1)} %add_convert_fusion), channel_id=1, source_target_pairs={{8,0},{16,8},{24,16},{28,24},{20,28},{12,20},{4,12},{0,4},{9,1},{1... | collective-permute-start | bytes 3145736 | tf_op jit(solution)/shard_map/ppermute | solution.py:106
  574.8 35.9 %collective-permute-start.51 = (bf16[512,2048]{1,0:T(8,128)(2,1)S(1)}, bf16[512,2048]{1,0:T(8,128)(2,1)S(1)}, u32[]{:S(2)}, u32[]{:S(2)}) collective-permute-start(bf16[512,2048]{1,0:T(8,128)(2,1)S(1)} %pad_maximum_fusion.9), channel_id=1, source_target_pairs={{0,1},{1,0},{2,3},{3,2},{4,5},{5,4},{6,7},{7,6},{8,9},{9,8},{10,11... | collective-permute-start | bytes 6291464 | tf_op jit(solution)/shard_map/ppermute | solution.py:169
  577.6 28.5 %collective-permute-start.91 = (bf16[2048,256]{1,0:T(8,128)(2,1)S(1)}, bf16[2048,256]{1,0:T(8,128)(2,1)S(1)}, u32[]{:S(2)}, u32[]{:S(2)}) collective-permute-start(bf16[2048,256]{1,0:T(8,128)(2,1)S(1)} %add_convert_fusion.2), channel_id=1, source_target_pairs={{0,8},{8,16},{16,24},{24,28},{28,20},{20,12},{12,4},{4,0},{1,9},{9... | collective-permute-start | bytes 3145736 | tf_op jit(solution)/shard_map/ppermute | solution.py:105
  592.9 60.1 %collective-permute-start.83 = (bf16[256,2048]{1,0:T(8,128)(2,1)}, bf16[256,2048]{1,0:T(8,128)(2,1)}, u32[]{:S(2)}, u32[]{:S(2)}) collective-permute-start(bf16[256,2048]{1,0:T(8,128)(2,1)} %fusion.25), channel_id=1, source_target_pairs={{0,8},{8,16},{16,24},{24,28},{28,20},{20,12},{12,4},{4,0},{1,9},{9... | collective-permute-start | bytes 3145736 | tf_op jit(solution)/shard_map/ppermute | solution.py:105
  604.6 55.9 %collective-permute-start.46 = (bf16[256,2048]{1,0:T(8,128)(2,1)}, bf16[256,2048]{1,0:T(8,128)(2,1)}, u32[]{:S(2)}, u32[]{:S(2)}) collective-permute-start(bf16[256,2048]{1,0:T(8,128)(2,1)} %fusion.20), channel_id=1, source_target_pairs={{0,2},{1,3},{2,0},{3,1},{4,6},{5,7},{6,4},{7,5},{8,10},{9,11},{10,... | collective-permute-start | bytes 3145736 | tf_op jit(solution)/shard_map/ppermute | solution.py:159
  664.3 229.4 %collective-permute-start.47 = (bf16[512,2048]{1,0:T(8,128)(2,1)}, bf16[512,2048]{1,0:T(8,128)(2,1)}, u32[]{:S(2)}, u32[]{:S(2)}) collective-permute-start(bf16[512,2048]{1,0:T(8,128)(2,1)} %pad_maximum_fusion.8), channel_id=1, source_target_pairs={{0,1},{1,0},{2,3},{3,2},{4,5},{5,4},{6,7},{7,6},{8,9},{9,8},{10,11... | collective-permute-start | bytes 6291464 | tf_op jit(solution)/shard_map/ppermute | solution.py:169
  684.6 18.3 %collective-permute-start.55 = (bf16[2,256,512]{2,1,0:T(8,128)(2,1)S(1)}, bf16[2,256,512]{2,1,0:T(8,128)(2,1)S(1)}, u32[]{:S(2)}, u32[]{:S(2)}) collective-permute-start(bf16[2,256,512]{2,1,0:T(8,128)(2,1)S(1)} %get-tuple-element.104), channel_id=1, source_target_pairs={{0,8},{8,16},{16,24},{24,28},{28,20},{20,12},{12,4},{4,0},{1,9},{9... | collective-permute-start | bytes 1572872 | tf_op jit(solution)/shard_map/ppermute | solution.py:105
  697.0 49.5 %collective-permute-start.73 = (bf16[512,256]{1,0:T(8,128)(2,1)S(1)}, bf16[512,256]{1,0:T(8,128)(2,1)S(1)}, u32[]{:S(2)}, u32[]{:S(2)}) collective-permute-start(bf16[512,256]{1,0:T(8,128)(2,1)S(1)} %pad_maximum_fusion.23), channel_id=1, source_target_pairs={{0,8},{8,16},{16,24},{24,28},{28,20},{20,12},{12,4},{4,0},{1,9},{9... | collective-permute-start | bytes 786440 | tf_op jit(solution)/shard_map/ppermute | solution.py:105
  702.6 46.0 %collective-permute-start.78 = (bf16[512,256]{1,0:T(8,128)(2,1)S(1)}, bf16[512,256]{1,0:T(8,128)(2,1)S(1)}, u32[]{:S(2)}, u32[]{:S(2)}) collective-permute-start(bf16[512,256]{1,0:T(8,128)(2,1)S(1)} %fusion.52), channel_id=1, source_target_pairs={{8,0},{16,8},{24,16},{28,24},{20,28},{12,20},{4,12},{0,4},{9,1},{1... | collective-permute-start | bytes 786440 | tf_op jit(solution)/shard_map/ppermute | solution.py:106
  723.5 45.3 %collective-permute-start.60 = (bf16[512,2048]{1,0:T(8,128)(2,1)S(1)}, bf16[512,2048]{1,0:T(8,128)(2,1)S(1)}, u32[]{:S(2)}, u32[]{:S(2)}) collective-permute-start(bf16[512,2048]{1,0:T(8,128)(2,1)S(1)} %convolution_convert_fusion.1), channel_id=1, source_target_pairs={{0,1},{1,0},{2,3},{3,2},{4,5},{5,4},{6,7},{7,6},{8,9},{9,8},{10,11... | collective-permute-start | bytes 6291464 | tf_op jit(solution)/shard_map/ppermute | solution.py:138
  745.9 18.3 %collective-permute-start.69 = (bf16[256,1536]{1,0:T(8,128)(2,1)S(1)}, bf16[256,1536]{1,0:T(8,128)(2,1)S(1)}, u32[]{:S(2)}, u32[]{:S(2)}) collective-permute-start(bf16[256,1536]{1,0:T(8,128)(2,1)S(1)} %pad_maximum_fusion.19), channel_id=1, source_target_pairs={{8,0},{16,8},{24,16},{28,24},{20,28},{12,20},{4,12},{0,4},{9,1},{1... | collective-permute-start | bytes 2359304 | tf_op jit(solution)/shard_map/ppermute | solution.py:106
  746.5 20.5 %collective-permute-start.65 = (bf16[256,1536]{1,0:T(8,128)(2,1)S(1)}, bf16[256,1536]{1,0:T(8,128)(2,1)S(1)}, u32[]{:S(2)}, u32[]{:S(2)}) collective-permute-start(bf16[256,1536]{1,0:T(8,128)(2,1)S(1)} %pad_maximum_fusion.18), channel_id=1, source_target_pairs={{0,8},{8,16},{16,24},{24,28},{28,20},{20,12},{12,4},{4,0},{1,9},{9... | collective-permute-start | bytes 2359304 | tf_op jit(solution)/shard_map/ppermute | solution.py:105
  748.6 24.0 %collective-permute-start.74 = (bf16[512,256]{1,0:T(8,128)(2,1)S(1)}, bf16[512,256]{1,0:T(8,128)(2,1)S(1)}, u32[]{:S(2)}, u32[]{:S(2)}) collective-permute-start(bf16[512,256]{1,0:T(8,128)(2,1)S(1)} %fusion.50), channel_id=1, source_target_pairs={{0,8},{8,16},{16,24},{24,28},{28,20},{20,12},{12,4},{4,0},{1,9},{9... | collective-permute-start | bytes 786440 | tf_op jit(solution)/shard_map/ppermute | solution.py:105
  764.2 36.2 %collective-permute-start.79 = (bf16[512,256]{1,0:T(8,128)(2,1)}, bf16[512,256]{1,0:T(8,128)(2,1)S(1)}, u32[]{:S(2)}, u32[]{:S(2)}) collective-permute-start(bf16[512,256]{1,0:T(8,128)(2,1)} %fusion.51), channel_id=1, source_target_pairs={{8,0},{16,8},{24,16},{28,24},{20,28},{12,20},{4,12},{0,4},{9,1},{1... | collective-permute-start | bytes 786440 | tf_op jit(solution)/shard_map/ppermute | solution.py:106
  767.0 20.3 %collective-permute-start.70 = (bf16[256,1536]{1,0:T(8,128)(2,1)S(1)}, bf16[256,1536]{1,0:T(8,128)(2,1)S(1)}, u32[]{:S(2)}, u32[]{:S(2)}) collective-permute-start(bf16[256,1536]{1,0:T(8,128)(2,1)S(1)} %add_convert_fusion.5), channel_id=1, source_target_pairs={{8,0},{16,8},{24,16},{28,24},{20,28},{12,20},{4,12},{0,4},{9,1},{1... | collective-permute-start | bytes 2359304 | tf_op jit(solution)/shard_map/ppermute | solution.py:106
  768.8 21.0 %collective-permute-start.66 = (bf16[256,1536]{1,0:T(8,128)(2,1)S(1)}, bf16[256,1536]{1,0:T(8,128)(2,1)S(1)}, u32[]{:S(2)}, u32[]{:S(2)}) collective-permute-start(bf16[256,1536]{1,0:T(8,128)(2,1)S(1)} %add_convert_fusion.7), channel_id=1, source_target_pairs={{0,8},{8,16},{16,24},{24,28},{28,20},{20,12},{12,4},{4,0},{1,9},{9... | collective-permute-start | bytes 2359304 | tf_op jit(solution)/shard_map/ppermute | solution.py:105
  772.7 20.6 %collective-permute-start.61 = (bf16[256,2048]{1,0:T(8,128)(2,1)S(1)}, bf16[256,2048]{1,0:T(8,128)(2,1)S(1)}, u32[]{:S(2)}, u32[]{:S(2)}) collective-permute-start(bf16[256,2048]{1,0:T(8,128)(2,1)S(1)} %fusion.24), channel_id=1, source_target_pairs={{0,2},{1,3},{2,0},{3,1},{4,6},{5,7},{6,4},{7,5},{8,10},{9,11},{10,... | collective-permute-start | bytes 3145736 | tf_op jit(solution)/shard_map/ppermute | solution.py:150
  803.7 33.8 %collective-permute-start.102 = (f32[2,8,256]{2,0,1:T(2,128)S(1)}, f32[2,8,256]{2,0,1:T(2,128)S(1)}, u32[]{:S(2)}, u32[]{:S(2)}) collective-permute-start(f32[2,8,256]{2,0,1:T(2,128)S(1)} %fusion.243), channel_id=1, source_target_pairs={{0,2},{1,3},{2,0},{3,1},{4,6},{5,7},{6,4},{7,5},{8,10},{9,11},{10,... | collective-permute-start | bytes 49160 | tf_op jit(solution)/shard_map/ppermute | solution.py:177
  849.2 25.4 %collective-permute-start.62 = (bf16[256,2048]{1,0:T(8,128)(2,1)}, bf16[256,2048]{1,0:T(8,128)(2,1)}, u32[]{:S(2)}, u32[]{:S(2)}) collective-permute-start(bf16[256,2048]{1,0:T(8,128)(2,1)} %fusion.38), channel_id=1, source_target_pairs={{0,2},{1,3},{2,0},{3,1},{4,6},{5,7},{6,4},{7,5},{8,10},{9,11},{10,... | collective-permute-start | bytes 3145736 | tf_op jit(solution)/shard_map/ppermute | solution.py:159
  (123 other events, 1742.8 us)

commit v2 on v1

v2 whole, which is shorter than its diff:
```python
import functools

import jax
import jax.numpy as jnp
from jax import lax
from jax.experimental import pallas as pl
from jax.experimental.pallas import tpu as pltpu
from jax.sharding import PartitionSpec as P

HEAD_DIM = 128
PRE_DEV = 256
SOL_DEV = 768
STEP = 10
BLOCK = 256

EPS_NORM = 1e-05
BETA_ONE = 0.9
BETA_TWO = 0.95
ADAM_EPS = 1e-08
EMA_KEEP = 0.7
CLIP_NORM = 1.0
DECAY_MATRIX = 0.1
RATE_INWARD = 0.05
RATE_OUTWARD = 0.15
RATE_EXPAND = 0.05
RATE_CONTRACT = 0.03
RATE_GAINS = 0.5

LOG2E = 1.4426950408889634
MASKED = -1e30
BF = jnp.bfloat16
FP = jnp.float32
VMEM_LIMIT = 56 * 1024 * 1024


def ring_order(count):
    depth = 4
    if count % depth or (count // depth) % 2:
        return list(range(count))
    width = count // depth
    order = [z * width for z in range(depth)]
    across = list(range(1, width))
    for z in reversed(range(depth)):
        order += [z * width + y for y in across]
        across = across[::-1]
    return order


class Ring:
    def __init__(self, count):
        self.count = count
        self.half = count // 2
        self.order = ring_order(count)
        self.up = [(self.order[i], self.order[(i + 1) % count]) for i in range(count)]
        self.down = [(b, a) for a, b in self.up]
        inverse = [0] * count
        for i, s in enumerate(self.order):
            inverse[s] = i
        self.inverse = inverse

    def gather(self, own):
        return Gather(self, own)

    def scatter(self, far):
        return Scatter(self, far)


class Gather:
    def __init__(self, ring, own):
        self.ring = ring
        self.blocks = [None] * ring.count
        self.blocks[0] = own
        self.fresh = [own, own]
        self.done = 0
        self.advance()

    def advance(self):
        ring = self.ring
        self.done += 1
        upper, lower = self.fresh
        if self.done == ring.half:
            mid = upper.shape[0] // 2
            upper, lower = upper[:mid], lower[mid:]
        self.fresh = [
            lax.ppermute(upper, "seq", ring.down),
            lax.ppermute(lower, "seq", ring.up),
        ]
        self.waiting = True

    def complete(self):
        while True:
            if self.waiting:
                pin([self])
            if self.done == self.ring.half:
                return self.blocks
            self.advance()

    def arrive(self):
        self.waiting = False
        j, n = self.done, self.ring.count
        if j == self.ring.half:
            self.blocks[j] = jnp.concatenate(self.fresh, axis=0)
        else:
            self.blocks[j], self.blocks[n - j] = self.fresh


class Scatter:
    def __init__(self, ring, far):
        self.ring = ring
        self.mid = far.shape[0] // 2
        self.left = ring.half
        self.send(far[: self.mid].astype(BF), far[self.mid :].astype(BF))

    def send(self, rising, falling):
        self.left -= 1
        self.fresh = [
            lax.ppermute(rising, "seq", self.ring.up),
            lax.ppermute(falling, "seq", self.ring.down),
        ]

    def arrive(self):
        pass

    def advance(self, part, order):
        j, mid = self.left, self.mid
        rising, falling = self.fresh
        upper, lower = part(j), part(self.ring.count - j)
        if j == self.ring.half - 1:
            upper = jnp.concatenate([upper[:mid] + rising.astype(FP), upper[mid:]], axis=0)
            lower = jnp.concatenate([lower[:mid], lower[mid:] + falling.astype(FP)], axis=0)
        else:
            upper = upper + rising.astype(FP)
            lower = lower + falling.astype(FP)
        order.upper, order.lower = upper.astype(BF), lower.astype(BF)
        order.pin()
        self.send(order.out.upper, order.out.lower)

    def finish(self, part, order):
        while self.left:
            order.pin(self)
            self.advance(part, order)
        return part(0) + self.fresh[0].astype(FP) + self.fresh[1].astype(FP)


class Team:
    def __init__(self, count):
        self.cores = 2 if count % 2 == 0 else 1
        self.chips = count // self.cores
        self.count = count
        self.core_flip = [(i, i ^ 1) for i in range(count)]

    def quarters(self, index):
        x, c = index // self.cores, index % self.cores
        cores = [c] + [1 - c] * (self.cores - 1)
        return [k * self.chips + (x + i) % self.chips for k in cores for i in range(self.chips)]

    def shift(self, k):
        chips, cores = self.chips, self.cores
        return [
            (x * cores + c, ((x + k) % chips) * cores + c) for x in range(chips) for c in range(cores)
        ]

    def cross(self, away):
        return lax.ppermute(away, "head", self.core_flip) if self.cores == 2 else None

    def send_sums(self, kept, got):
        size = kept.shape[0] // self.chips
        arrived = []
        for k in range(1, self.chips):
            spot = slice(k * size, (k + 1) * size)
            term = kept[spot].astype(FP)
            if got is not None:
                term = term + got[spot].astype(FP)
            arrived.append(lax.ppermute(term.astype(BF), "head", self.shift(k)))
        return arrived

    def send_own(self, own):
        return [own] + [lax.ppermute(own, "head", self.shift(-k)) for k in range(1, self.chips)]

    def send_half(self, parts):
        if self.cores == 1:
            return list(parts)
        half = jnp.concatenate(parts, axis=0) if self.chips > 1 else parts[0]
        return list(parts) + [lax.ppermute(half, "head", self.core_flip)]


def total_of_all(value, seq_count, head_count):
    for axis, count in (("head", head_count), ("seq", seq_count)):
        step = 1
        while step < count:
            value = value + lax.ppermute(value, axis, [(i, i ^ step) for i in range(count)])
            step *= 2
    return value


PARAMS = pltpu.CompilerParams(vmem_limit_bytes=VMEM_LIMIT)
ANYWHERE = pl.BlockSpec(memory_space=pl.ANY)
META_IDS = 3


def dot_nt(a, b):
    return lax.dot_general(a, b, (((1,), (1,)), ((), ())), preferred_element_type=FP)


def dot_nn(a, b):
    return lax.dot_general(a, b, (((1,), (0,)), ((), ())), preferred_element_type=FP)


def dot_tn(a, b):
    return lax.dot_general(a, b, (((0,), (0,)), ((), ())), preferred_element_type=FP)


def lanes(index, size):
    return pl.ds(pl.multiple_of(index * size, size), size)


def unit_of(values):
    center = values - jnp.mean(values, axis=-1, keepdims=True)
    inverse = lax.rsqrt(jnp.mean(center * center, axis=-1, keepdims=True) + EPS_NORM)
    return center * inverse, inverse


def norm_back(incoming, unit, inverse, gain_row):
    scaled = incoming * gain_row
    inner = (
        scaled
        - jnp.mean(scaled, axis=-1, keepdims=True)
        - unit * jnp.mean(scaled * unit, axis=-1, keepdims=True)
    )
    return inner * inverse, jnp.sum(incoming * unit, axis=0, keepdims=True)


def call(body, name, meta, inputs, in_specs, out_specs, out_shape, grid=(1,), scratch=()):
    return pl.pallas_call(
        body,
        grid_spec=pltpu.PrefetchScalarGridSpec(
            num_scalar_prefetch=1,
            grid=grid,
            in_specs=in_specs,
            out_specs=out_specs,
            scratch_shapes=list(scratch),
        ),
        out_shape=out_shape,
        compiler_params=PARAMS,
        cost_estimate=pl.CostEstimate(flops=1, bytes_accessed=1, transcendentals=0),
        name=name,
    )(meta, *inputs)


def first_norm(meta, tokens, gains, rows, n):
    model = tokens.shape[1]
    share = model // n

    def body(meta_ref, in_ref, gain_ref, norm_ref, source_ref, held):
        held[...], _ = unit_of(in_ref[...].astype(FP))
        for b in range(n):
            here = pl.ds(b * share, share)
            there = lanes(meta_ref[META_IDS + b], share)
            norm_ref[:, here] = (held[:, there] * gain_ref[0:1, here]).astype(BF)
            source_ref[:, here] = in_ref[:, there]

    tile = pl.BlockSpec((BLOCK, model), lambda i, m: (i, 0))
    return call(
        body, "first_norm", meta, (tokens, gains),
        [tile, pl.BlockSpec((2, model), lambda i, m: (0, 0))], [tile, tile],
        [jax.ShapeDtypeStruct((rows, model), BF), jax.ShapeDtypeStruct((rows, model), BF)],
        grid=(rows // BLOCK,),
        scratch=[pltpu.VMEM((BLOCK, model), FP)],
    )


def mask_cotangent(meta, cotangent, n, m):
    rows, model = cotangent.shape
    share, quarter = model // n, rows // m

    def body(meta_ref, in_ref, out_ref):
        spot = meta_ref[META_IDS + n + pl.program_id(0)] * quarter
        row = lax.broadcasted_iota(jnp.int32, (quarter, share), 0) + spot
        limit = jnp.where(
            row < PRE_DEV, meta_ref[1] - meta_ref[0] * PRE_DEV, meta_ref[2] + PRE_DEV
        )
        for b in range(n):
            piece = in_ref[:, lanes(meta_ref[META_IDS + b], share)]
            out_ref[:, pl.ds(b * share, share)] = jnp.where(row < limit, piece.astype(FP), 0).astype(BF)

    return call(
        body, "mask_cotangent", meta, (cotangent,),
        [pl.BlockSpec((quarter, model), lambda i, meta: (meta[META_IDS + n + i], 0))],
        pl.BlockSpec((quarter, model), lambda i, meta: (i, 0)),
        jax.ShapeDtypeStruct((rows, model), BF),
        grid=(m,),
    )


def place_rows(meta, pieces, n, m, dtype):
    quarter, model = pieces[0].shape
    share = model // n
    count = len(pieces)
    starts = [0]
    for piece in pieces:
        starts.append(starts[-1] + piece.shape[0] // quarter)

    def body(meta_ref, *refs):
        out_ref = refs[count]
        for k in range(count):

            @pl.when((pl.program_id(0) >= starts[k]) & (pl.program_id(0) < starts[k + 1]))
            def _():
                for b in range(n):
                    out_ref[:, lanes(meta_ref[META_IDS + b], share)] = refs[k][
                        :, pl.ds(b * share, share)
                    ].astype(dtype)

    def spec(k):
        last = starts[k + 1] - starts[k] - 1
        return pl.BlockSpec(
            (quarter, model), lambda i, meta: (jnp.clip(i - starts[k], 0, last), 0)
        )

    return call(
        body, "place_rows", meta, pieces, [spec(k) for k in range(count)],
        pl.BlockSpec((quarter, model), lambda i, meta: (meta[META_IDS + n + i], 0)),
        jax.ShapeDtypeStruct((quarter * m, model), dtype),
        grid=(m,),
    )


def project_prefix(meta, normed, weights, out_shard):
    n = len(weights)
    model = normed.shape[1]
    width = weights[0].shape[1]
    share = model // n

    def body(meta_ref, x_ref, shard_ref, *refs):
        blocks, (send_ref, held, sems) = refs[:n], refs[n:]

        def copy(b):
            return pltpu.make_async_copy(
                blocks[b].at[pl.ds(share, 2 * share), :], held.at[b], sems.at[b]
            )

        for b in range(n):
            copy(b).start()
        send_ref[pl.ds(2 * PRE_DEV, share), :] = shard_ref[...]
        totals = [None, None]
        for b in range(n):
            copy(b).wait()
            for c in range(2):
                term = dot_nn(
                    x_ref[:, pl.ds(b * share, share)], held[b, pl.ds(c * share, share), :]
                )
                totals[c] = term if b == 0 else totals[c] + term
        for c in range(2):
            send_ref[pl.ds(c * PRE_DEV, PRE_DEV), :] = totals[c].astype(BF)

    sent = 2 * PRE_DEV + share
    return call(
        body, "project_prefix", meta, (normed, out_shard, *weights),
        [
            pl.BlockSpec((PRE_DEV, model), lambda i, m: (0, 0)),
            pl.BlockSpec((share, width), lambda i, m: (0, 0)),
        ]
        + [ANYWHERE] * n,
        pl.BlockSpec((sent, width), lambda i, m: (0, 0)),
        jax.ShapeDtypeStruct((sent, width), BF),
        scratch=[pltpu.VMEM((n, 2 * share, width), BF), pltpu.SemaphoreType.DMA((n,))],
    )


def project(meta, normed, weights):
    n = len(weights)
    rows, model = normed.shape
    width = weights[0].shape[1]
    share = model // n

    def body(meta_ref, x_ref, *refs):
        blocks, (out_ref, held, sems) = refs[:n], refs[n:]
        part = pl.program_id(0)

        def copy(c, b):
            return pltpu.make_async_copy(
                blocks[b].at[pl.ds(pl.multiple_of(c * share, share), share), :],
                held.at[c, pl.ds(b * share, share), :],
                sems.at[c, b],
            )

        @pl.when(part == 0)
        def _():
            for c in range(3):
                for b in range(n):
                    copy(c, b).start()

        for b in range(n):
            copy(part, b).wait()
        out_ref[0] = dot_nn(x_ref[...], held[part]).astype(BF)

    return call(
        body, "project", meta, (normed, *weights),
        [pl.BlockSpec((rows, model), lambda c, m: (0, 0))] + [ANYWHERE] * n,
        pl.BlockSpec((1, rows, width), lambda c, m: (c, 0, 0)),
        jax.ShapeDtypeStruct((3, rows, width), BF),
        grid=(3,),
        scratch=[pltpu.VMEM((3, model, width), BF), pltpu.SemaphoreType.DMA((3, n))],
    )


def rows_matmul(meta, name, x, weights, m, placed, taken, form, layer=None):
    n = len(weights)
    rows, depth = x.shape[-2:]
    quarter = rows // m
    kept = quarter * (m // 2) if m % 2 == 0 else rows
    offset, size = taken
    width = weights[0].shape[1]
    held_rows = weights[0].shape[0] if size is None else size
    column = {"nn": width, "nt": held_rows}.get(form, held_rows // 3)
    group = max(1, min(n, 512 // column))
    tile = group * column
    steps = n // group

    def body(meta_ref, x_any, *refs):
        blocks, outs = refs[:n], refs[n:-4]
        x_held, held, x_sems, sems = refs[-4:]
        step = pl.program_id(0)

        def x_copy(i):
            spot = i * quarter
            if placed:
                spot = pl.multiple_of(meta_ref[META_IDS + n + i] * quarter, quarter)
            x_rows = x_any if layer is None else x_any.at[layer]
            return pltpu.make_async_copy(
                x_rows.at[pl.ds(spot, quarter), :],
                x_held.at[pl.ds(i * quarter, quarter), :],
                x_sems.at[i],
            )

        def copies(s, g):
            block = blocks[s * group + g]
            sem = sems.at[s, g]
            if form == "three":
                return [
                    pltpu.make_async_copy(
                        block.at[pl.ds(c * column, column), :],
                        held.at[s, pl.ds(g * column, column), pl.ds(c * width, width)],
                        sems.at[s, g * 3 + c],
                    )
                    for c in range(3)
                ]
            source = block if size is None else block.at[pl.ds(offset, size), :]
            if form == "nn":
                target = held.at[s, :, pl.ds(g * column, column)]
            else:
                target = held.at[s, pl.ds(g * column, column), :]
            return [pltpu.make_async_copy(source, target, sem)]

        @pl.when(step == 0)
        def _():
            for i in range(m):
                x_copy(i).start()
            for s in range(steps):
                for g in range(group):
                    for one in copies(s, g):
                        one.start()
            for i in range(m):
                x_copy(i).wait()

        for s in range(steps):

            @pl.when(step == s)
            def _():
                for g in range(group):
                    for one in copies(s, g):
                        one.wait()

        product = (dot_nn if form == "nn" else dot_nt)(x_held[...], held[step]).astype(BF)
        outs[0][...] = product[:kept]
        if kept < rows:
            outs[1][...] = product[kept:]

    if form == "nn":
        held_shape = (steps, depth, tile)
    else:
        held_shape = (steps, tile, depth)
    sizes = [kept] + ([rows - kept] if kept < rows else [])
    return call(
        body, name, meta, (x, *weights), [ANYWHERE] * (n + 1),
        [pl.BlockSpec((size_of, tile), lambda s, m: (0, s)) for size_of in sizes],
        [jax.ShapeDtypeStruct((size_of, n * column), BF) for size_of in sizes],
        grid=(steps,),
        scratch=[
            pltpu.VMEM((rows, depth), BF),
            pltpu.VMEM(held_shape, BF),
            pltpu.SemaphoreType.DMA((m,)),
            pltpu.SemaphoreType.DMA((steps, 3 * group if form == "three" else group)),
        ],
    )


def tile_of(width):
    return min(512, width)


def feed_back(meta, out_grad, weights):
    n = len(weights)
    rows, model = out_grad.shape
    width, share = weights[0].shape
    tile = tile_of(width)
    tiles = width // tile

    def body(meta_ref, x_ref, *refs):
        blocks, (out_ref, held, sems) = refs[:n], refs[n:]
        step = pl.program_id(0)

        def copy(t, b):
            return pltpu.make_async_copy(
                blocks[b].at[pl.ds(pl.multiple_of(t * tile, tile), tile), :],
                held.at[t, :, pl.ds(b * share, share)],
                sems.at[t, b],
            )

        @pl.when(step == 0)
        def _():
            for t in range(tiles):
                for b in range(n):
                    copy(t, b).start()

        for b in range(n):
            copy(step, b).wait()
        out_ref[...] = dot_nt(x_ref[...], held[step]).astype(BF)

    part = pl.BlockSpec((rows, tile), lambda t, m: (0, t))
    return call(
        body, "feed_back", meta, (out_grad, *weights),
        [pl.BlockSpec((rows, model), lambda t, m: (0, 0))] + [ANYWHERE] * n,
        part,
        jax.ShapeDtypeStruct((rows, width), BF),
        grid=(tiles,),
        scratch=[pltpu.VMEM((tiles, tile, model), BF), pltpu.SemaphoreType.DMA((tiles, n))],
    )


def feed_up(meta, pieces, weights, d_activation):
    n, count = len(weights), len(pieces)
    rows = sum(piece.shape[0] for piece in pieces)
    model = pieces[0].shape[1]
    width = weights[0].shape[1]
    share = model // n
    tile = tile_of(width)
    tiles = width // tile
    root = 0.7978845608028654
    step_rows = 512

    def body(meta_ref, *refs):
        parts, blocks, back_ref = refs[:count], refs[count : count + n], refs[count + n]
        x_out, both_ref, held, sems, x_sems = refs[count + n + 1 :]
        step = pl.program_id(0)

        def copy(t, b):
            return pltpu.make_async_copy(
                blocks[b].at[:, lanes(t, tile)],
                held.at[t, pl.ds(b * share, share), :],
                sems.at[t, b],
            )

        def x_copies():
            at, copies = 0, []
            for k in range(count):
                size = pieces[k].shape[0]
                copies.append(
                    pltpu.make_async_copy(parts[k], x_out.at[pl.ds(at, size), :], x_sems.at[k])
                )
                at += size
            return copies

        @pl.when(step == 0)
        def _():
            for one in x_copies():
                one.start()
            for t in range(tiles):
                for b in range(n):
                    copy(t, b).start()
            for one in x_copies():
                one.wait()

        for b in range(n):
            copy(step, b).wait()

        for i in range(rows // step_rows):
            spot = pl.ds(i * step_rows, step_rows)
            v = dot_nn(x_out[spot, :], held[step])
            square = v * v
            t = jnp.tanh(root * v * (1.0 + 0.044715 * square))
            half = 0.5 * (1.0 + t)
            both_ref[0, spot, :] = (v * half).astype(BF)
            slope = half + 0.5 * v * (1.0 - t * t) * (root * (1.0 + 3.0 * 0.044715 * square))
            both_ref[1, spot, :] = (back_ref[spot, :].astype(FP) * slope).astype(BF)

    return call(
        body, "feed_up", meta, (*pieces, *weights, d_activation),
        [ANYWHERE] * (count + n) + [pl.BlockSpec((rows, tile), lambda t, m: (0, t))],
        [
            pl.BlockSpec((rows, model), lambda t, m: (0, 0)),
            pl.BlockSpec((2, rows, tile), lambda t, m: (0, 0, t)),
        ],
        [
            jax.ShapeDtypeStruct((rows, model), BF),
            jax.ShapeDtypeStruct((2, rows, width), BF),
        ],
        grid=(tiles,),
        scratch=[
            pltpu.VMEM((tiles, model, tile), BF),
            pltpu.SemaphoreType.DMA((tiles, n)),
            pltpu.SemaphoreType.DMA((count,)),
        ],
    )


def feed_terms(meta, out_grad, normed, both, blocks, received, n, dtype, cut=False):
    rows, model = out_grad.shape
    width = both.shape[2]
    share = model // n
    count = len(blocks)
    flat = [(k, array, start) for k, sums in enumerate(received) for array, start in sums]

    def body(meta_ref, grad_ref, norm_ref, both_ref, *refs):
        arrived, outs = refs[: len(flat)], refs[len(flat) :]
        matrix, block = pl.program_id(0), pl.program_id(1)
        for k in range(count):
            for which, left in ((0, grad_ref), (1, norm_ref)):

                @pl.when((matrix == which) & (block == k))
                def _():
                    term = dot_tn(left[...], both_ref[0])
                    for (at, array, start), ref in zip(flat, arrived):
                        if at == k and start <= which < start + array.shape[0] // share:
                            term = term + ref[...].astype(FP)
                    outs[which if cut else k][...] = term.astype(dtype)

    def chosen(k):
        b = blocks[0]
        for i in range(1, count):
            b = jnp.where(k == i, blocks[i], b)
        return b

    def received_spec(array, start):
        last = array.shape[0] // share - 1
        return pl.BlockSpec((share, width), lambda t, k, m: (jnp.clip(t - start, 0, last), 0))

    column = pl.BlockSpec((rows, share), lambda t, k, m: (0, chosen(k)))
    out = call(
        body, "feed_terms", meta, (out_grad, normed, both, *[array for _, array, _ in flat]),
        [column, column, pl.BlockSpec((1, rows, width), lambda t, k, m: (t, 0, 0))]
        + [received_spec(array, start) for _, array, start in flat],
        [pl.BlockSpec((share, width), lambda t, k, m: (0 if cut else t, 0))] * (2 if cut else count),
        [jax.ShapeDtypeStruct(((1 if cut else 2) * share, width), dtype)] * (2 if cut else count),
        grid=(2, count),
    )
    return out


def mixed_back(meta, pieces, weights, mixed, offset, n, m):
    count = len(pieces)
    quarter, model = pieces[0].shape
    share = model // n
    rows, width = mixed.shape

    def body(meta_ref, *refs):
        parts, blocks, mixed_ref = refs[:count], refs[count : count + n], refs[count + n]
        x_out, d_ref, mixed_out, held, sems, x_sems = refs[count + n + 1 :]
        step = pl.program_id(0)

        def copy(b):
            return pltpu.make_async_copy(
                blocks[b].at[pl.ds(offset, share), :],
                held.at[pl.ds(b * share, share), :],
                sems.at[b],
            )

        def x_copies():
            at, copies = 0, []
            for k in range(count):
                size = pieces[k].shape[0]
                copies.append(
                    pltpu.make_async_copy(parts[k], x_out.at[pl.ds(at, size), :], x_sems.at[k])
                )
                at += size
            return copies

        @pl.when(step == 0)
        def _():
            for one in x_copies() + [copy(b) for b in range(n)]:
                one.start()
            for one in x_copies() + [copy(b) for b in range(n)]:
                one.wait()

        spot = pl.ds(pl.multiple_of(step * quarter, quarter), quarter)
        d_ref[...] = dot_nn(x_out[spot, :], held[...]).astype(BF)
        mixed_out[...] = mixed_ref[...]

    placed = pl.BlockSpec((quarter, width), lambda i, meta: (meta[META_IDS + n + i], 0))
    return call(
        body, "mixed_back", meta, (*pieces, *weights, mixed),
        [ANYWHERE] * (count + n) + [placed],
        [
            pl.BlockSpec((rows, model), lambda i, meta: (0, 0)),
            placed,
            pl.BlockSpec((quarter, width), lambda i, meta: (i, 0)),
        ],
        [
            jax.ShapeDtypeStruct((rows, model), BF),
            jax.ShapeDtypeStruct((rows, width), BF),
            jax.ShapeDtypeStruct((rows, width), BF),
        ],
        grid=(m,),
        scratch=[
            pltpu.VMEM((model, width), BF),
            pltpu.SemaphoreType.DMA((n,)),
            pltpu.SemaphoreType.DMA((count,)),
        ],
    )


def own_quarter(quarter, model, step):
    steps = quarter // step
    plain = pl.BlockSpec((step, model), lambda i, meta: (i, 0))
    whole = pl.BlockSpec((2, model), lambda i, meta: (0, 0))

    def placed(n):
        return pl.BlockSpec(
            (step, model), lambda i, meta: (meta[META_IDS + n] * steps + i, 0)
        )

    return steps, plain, whole, placed


def second_norm(meta, terms, source, gains, quarter, n):
    model = source.shape[1]
    steps, plain, whole, placed = own_quarter(quarter, model, min(64, quarter))
    count = len(terms)

    def body(meta_ref, *refs):
        source_ref, gain_ref, hidden_ref, norm_ref = refs[count:]
        hidden = refs[0][...].astype(FP)
        for k in range(1, count):
            hidden = hidden + refs[k][...].astype(FP)
        hidden = source_ref[...].astype(FP) + hidden
        hidden_ref[...] = hidden
        norm_ref[...] = (unit_of(hidden)[0] * gain_ref[1:2, :]).astype(BF)

    return call(
        body, "second_norm", meta, (*terms, source, gains),
        [plain] * count + [placed(n), whole], [plain, plain],
        [jax.ShapeDtypeStruct((quarter, model), FP), jax.ShapeDtypeStruct((quarter, model), BF)],
        grid=(steps,),
    )


def second_norm_back(meta, terms, hidden, out_grad, gains):
    quarter, model = hidden.shape
    steps, plain, whole, _ = own_quarter(quarter, model, min(64, quarter))
    count = len(terms)

    def body(meta_ref, *refs):
        hidden_ref, grad_ref, gain_ref, d_ref, low_ref, dg_ref = refs[count:]
        incoming = refs[0][...].astype(FP)
        for k in range(1, count):
            incoming = incoming + refs[k][...].astype(FP)
        unit, inverse = unit_of(hidden_ref[...])
        d_norm, d_gain = norm_back(incoming, unit, inverse, gain_ref[1:2, :])
        d_hidden = grad_ref[...].astype(FP) + d_norm
        d_ref[...] = d_hidden
        low_ref[...] = d_hidden.astype(BF)

        @pl.when(pl.program_id(0) == 0)
        def _():
            dg_ref[...] = d_gain

        @pl.when(pl.program_id(0) > 0)
        def _():
            dg_ref[...] += d_gain

    return call(
        body, "second_norm_back", meta, (*terms, hidden, out_grad, gains),
        [plain] * (count + 2) + [whole],
        [plain, plain, pl.BlockSpec((1, model), lambda i, m: (0, 0))],
        [
            jax.ShapeDtypeStruct((quarter, model), FP),
            jax.ShapeDtypeStruct((quarter, model), BF),
            jax.ShapeDtypeStruct((1, model), FP),
        ],
        grid=(steps,),
    )


def first_norm_back(meta, terms, source, d_hidden, gains, n):
    quarter, model = d_hidden.shape
    steps, plain, whole, placed = own_quarter(quarter, model, min(64, quarter))
    count = len(terms)

    def body(meta_ref, *refs):
        source_ref, hidden_ref, gain_ref, low_ref, dg_ref = refs[count:]
        incoming = refs[0][...].astype(FP)
        for k in range(1, count):
            incoming = incoming + refs[k][...].astype(FP)
        unit, inverse = unit_of(source_ref[...].astype(FP))
        d_norm, d_gain = norm_back(incoming, unit, inverse, gain_ref[0:1, :])
        low_ref[...] = (hidden_ref[...] + d_norm).astype(BF)

        @pl.when(pl.program_id(0) == 0)
        def _():
            dg_ref[...] = d_gain

        @pl.when(pl.program_id(0) > 0)
        def _():
            dg_ref[...] += d_gain

    return call(
        body, "first_norm_back", meta, (*terms, source, d_hidden, gains),
        [plain] * count + [placed(n), plain, whole],
        [plain, pl.BlockSpec((1, model), lambda i, m: (0, 0))],
        [jax.ShapeDtypeStruct((quarter, model), BF), jax.ShapeDtypeStruct((1, model), FP)],
        grid=(steps,),
    )


def prefix_places(meta_ref, n):
    spot = lax.broadcasted_iota(jnp.int32, (1, PRE_DEV), 1)
    return jnp.concatenate([spot + meta_ref[META_IDS + b] * PRE_DEV for b in range(n)], axis=1)


def masked_scores(meta_ref, q_ref, k_ref, kp_ref, places, block):
    limit_prefix = meta_ref[1]
    limit_answer = meta_ref[2]
    query = q_ref[0, pl.ds(block * BLOCK, BLOCK), :]
    score_pre = dot_nt(query, kp_ref[...])
    if block < PRE_DEV // BLOCK:
        row = lax.broadcasted_iota(jnp.int32, (BLOCK, 1), 0) + block * BLOCK
        reach = jnp.minimum(meta_ref[0] * PRE_DEV + row + 1, limit_prefix)
        return query, jnp.where(places < reach, score_pre, MASKED), None
    score_pre = jnp.where(places < limit_prefix, score_pre, MASKED)
    solution_row = block * BLOCK - PRE_DEV
    width = solution_row + BLOCK
    score_own = dot_nt(query, k_ref[0, pl.ds(PRE_DEV, width), :])
    row = lax.broadcasted_iota(jnp.int32, (BLOCK, 1), 0) + solution_row
    reach = jnp.minimum(row + 1, limit_answer)
    column = lax.broadcasted_iota(jnp.int32, (1, width), 1)
    return query, score_pre, jnp.where(column < reach, score_own, MASKED)


def attention_specs(rows, n):
    part = lambda c: pl.BlockSpec((1, rows, HEAD_DIM), lambda h, m: (c, 0, h))
    pre = lambda c: pl.BlockSpec((PRE_DEV, HEAD_DIM), lambda h, m: (c, h))
    return [part(0), part(1), part(2)] + [pre(0)] * n + [pre(1)] * n


def attention_forward(meta, projected, prefix_kv):
    _, rows, width = projected.shape
    heads = width // HEAD_DIM
    n = len(prefix_kv)
    prefix = n * PRE_DEV
    scale = HEAD_DIM ** (-0.5) * LOG2E

    def body(meta_ref, q_ref, k_ref, v_ref, *refs):
        keys, values, (out_ref, log_ref, kp_ref, vp_ref) = refs[:n], refs[n : 2 * n], refs[2 * n :]
        for b in range(n):
            kp_ref[pl.ds(b * PRE_DEV, PRE_DEV), :] = keys[b][...]
            vp_ref[pl.ds(b * PRE_DEV, PRE_DEV), :] = values[b][...]
        places = prefix_places(meta_ref, n)
        for block in range(rows // BLOCK):
            _, score_pre, score_own = masked_scores(meta_ref, q_ref, k_ref, kp_ref, places, block)
            top = jnp.max(score_pre, axis=-1, keepdims=True)
            if score_own is not None:
                top = jnp.maximum(top, jnp.max(score_own, axis=-1, keepdims=True))
            e_pre = jnp.exp2((score_pre - top) * scale)
            total = jnp.sum(e_pre, axis=-1, keepdims=True)
            out = dot_nn(e_pre.astype(BF), vp_ref[...])
            if score_own is not None:
                e_own = jnp.exp2((score_own - top) * scale)
                total = total + jnp.sum(e_own, axis=-1, keepdims=True)
                out = out + dot_nn(
                    e_own.astype(BF), v_ref[0, pl.ds(PRE_DEV, score_own.shape[1]), :]
                )
            out_ref[pl.ds(block * BLOCK, BLOCK), :] = (out / total).astype(BF)
            log_ref[0, pl.ds(block * BLOCK, BLOCK), :] = top * scale + jnp.log2(total)

    return call(
        body, "attention_forward", meta, (projected,) * 3 + tuple(prefix_kv) * 2,
        attention_specs(rows, n),
        [
            pl.BlockSpec((rows, HEAD_DIM), lambda h, m: (0, h)),
            pl.BlockSpec((1, rows, 1), lambda h, m: (h, 0, 0)),
        ],
        [
            jax.ShapeDtypeStruct((rows, heads * HEAD_DIM), BF),
            jax.ShapeDtypeStruct((heads, rows, 1), FP),
        ],
        grid=(heads,),
        scratch=[pltpu.VMEM((prefix, HEAD_DIM), BF), pltpu.VMEM((prefix, HEAD_DIM), BF)],
    )


def attention_backward(meta, projected, prefix_kv, mixed, d_mixed, logs, d_out_matrix):
    _, rows, width = projected.shape
    heads = width // HEAD_DIM
    n = len(prefix_kv)
    prefix = n * PRE_DEV
    share = d_out_matrix.shape[0] // n
    scale = HEAD_DIM ** (-0.5)
    sent = 2 * PRE_DEV + share

    def body(meta_ref, q_ref, k_ref, v_ref, *refs):
        keys, values = refs[:n], refs[n : 2 * n]
        o_ref, do_ref, log_ref, matrix_ref, d_ref, send_ref = refs[2 * n : 2 * n + 6]
        kp_ref, vp_ref, dk_pre, dv_pre, dk_own, dv_own = refs[2 * n + 6 :]
        for b in range(n):
            kp_ref[pl.ds(b * PRE_DEV, PRE_DEV), :] = keys[b][...]
            vp_ref[pl.ds(b * PRE_DEV, PRE_DEV), :] = values[b][...]
            send_ref[b, pl.ds(2 * PRE_DEV, share), :] = matrix_ref[pl.ds(b * share, share), :]
        places = prefix_places(meta_ref, n)
        dk_own[...] = jnp.zeros_like(dk_own)
        dv_own[...] = jnp.zeros_like(dv_own)
        for block in range(rows // BLOCK):
            spot = pl.ds(block * BLOCK, BLOCK)
            query, score_pre, score_own = masked_scores(
                meta_ref, q_ref, k_ref, kp_ref, places, block
            )
            d_out = do_ref[spot, :]
            log = log_ref[0, spot, :]
            inner = jnp.sum(d_out.astype(FP) * o_ref[spot, :].astype(FP), axis=-1, keepdims=True)
            p = jnp.exp2(score_pre * (scale * LOG2E) - log)
            ds = (p * (dot_nt(d_out, vp_ref[...]) - inner)).astype(BF)
            p = p.astype(BF)
            dq = dot_nn(ds, kp_ref[...])
            dk_term = dot_tn(ds, query)
            dv_term = dot_tn(p, d_out)
            if block == 0:
                dk_pre[...] = dk_term
                dv_pre[...] = dv_term
            else:
                dk_pre[...] += dk_term
                dv_pre[...] += dv_term
            if score_own is not None:
                near = pl.ds(PRE_DEV, score_own.shape[1])
                p = jnp.exp2(score_own * (scale * LOG2E) - log)
                ds = (p * (dot_nt(d_out, v_ref[0, near, :]) - inner)).astype(BF)
                p = p.astype(BF)
                dq = dq + dot_nn(ds, k_ref[0, near, :])
                own = pl.ds(0, score_own.shape[1])
                dk_own[own, :] += dot_tn(ds, query)
                dv_own[own, :] += dot_tn(p, d_out)
            d_ref[0, spot, :] = (dq * scale).astype(BF)
        for b in range(n):
            here = pl.ds(b * PRE_DEV, PRE_DEV)
            send_ref[b, pl.ds(0, PRE_DEV), :] = (dk_pre[here, :] * scale).astype(BF)
            send_ref[b, pl.ds(PRE_DEV, PRE_DEV), :] = dv_pre[here, :].astype(BF)
        first, rest = pl.ds(0, PRE_DEV), pl.ds(PRE_DEV, rows - PRE_DEV)
        d_ref[1, first, :] = jnp.zeros((PRE_DEV, HEAD_DIM), BF)
        d_ref[2, first, :] = jnp.zeros((PRE_DEV, HEAD_DIM), BF)
        d_ref[1, rest, :] = (dk_own[...] * scale).astype(BF)
        d_ref[2, rest, :] = dv_own[...].astype(BF)

    sol = rows - PRE_DEV
    flat = pl.BlockSpec((rows, HEAD_DIM), lambda h, m: (0, h))
    return call(
        body, "attention_backward", meta,
        (projected,) * 3 + tuple(prefix_kv) * 2 + (mixed, d_mixed, logs, d_out_matrix),
        attention_specs(rows, n)
        + [
            flat,
            flat,
            pl.BlockSpec((1, rows, 1), lambda h, m: (h, 0, 0)),
            pl.BlockSpec((n * share, HEAD_DIM), lambda h, m: (0, h)),
        ],
        [
            pl.BlockSpec((3, rows, HEAD_DIM), lambda h, m: (0, 0, h)),
            pl.BlockSpec((n, sent, HEAD_DIM), lambda h, m: (0, 0, h)),
        ],
        [
            jax.ShapeDtypeStruct((3, rows, width), BF),
            jax.ShapeDtypeStruct((n, sent, width), BF),
        ],
        grid=(heads,),
        scratch=[
            pltpu.VMEM((prefix, HEAD_DIM), BF),
            pltpu.VMEM((prefix, HEAD_DIM), BF),
            pltpu.VMEM((prefix, HEAD_DIM), FP),
            pltpu.VMEM((prefix, HEAD_DIM), FP),
            pltpu.VMEM((sol, HEAD_DIM), FP),
            pltpu.VMEM((sol, HEAD_DIM), FP),
        ],
    )


def adamw(weight, gradient, moment, variance, average, step_rate, decay_rate):
    moment = BETA_ONE * moment + (1.0 - BETA_ONE) * gradient
    variance = BETA_TWO * variance + (1.0 - BETA_TWO) * gradient * gradient
    corrected = moment / (1.0 - BETA_ONE**STEP)
    scaled_root = jnp.sqrt(variance / (1.0 - BETA_TWO**STEP)) + ADAM_EPS
    weight_new = weight - step_rate * corrected / scaled_root - step_rate * decay_rate * weight
    average = EMA_KEEP * average + (1.0 - EMA_KEEP) * weight_new
    return (moment, variance, weight_new, average)


def update_matrices(factor, groups, rates, steps):
    def spec(shape):
        if len(shape) == 3:
            return pl.BlockSpec((3, shape[1] // steps, shape[2]), lambda i: (0, i, 0))
        return pl.BlockSpec((shape[0] // steps, shape[1]), lambda i: (i, 0))

    flat = [array for group in groups for array in group]
    count = len(groups)
    shapes = [group[1].shape for group in groups]
    turned = [False, True, False, True]
    wide = [shape[0] // steps % 128 == 0 for shape in shapes]

    def body(factor_ref, *refs):
        scale = factor_ref[0]
        ins, outs, held = refs[: 5 * count], refs[5 * count : -1], refs[-1]
        for g in range(count):
            grad_ref, *old = ins[5 * g : 5 * g + 5]
            new = outs[4 * g : 4 * g + 4]
            if turned[g] and wide[g]:
                grad = jnp.transpose(grad_ref[...])
            elif turned[g]:
                size = shapes[g][0] // steps

                @pl.when(pl.program_id(0) == 0)
                def _():
                    held[...] = jnp.transpose(grad_ref[...])

                grad = held[pl.ds(pl.multiple_of(pl.program_id(0) * size, size), size), :]
            elif len(old[0].shape) < 3:
                grad = grad_ref[...]
            if len(old[0].shape) == 3:
                width = old[0].shape[2]
                for c in range(3):
                    grad = grad_ref[:, pl.ds(c * width, width)] * scale
                    results = adamw(
                        old[0][c], grad, old[1][c], old[2][c], old[3][c], rates[g], DECAY_MATRIX
                    )
                    for ref, value in zip(new, results):
                        ref[c] = value
            else:
                results = adamw(
                    old[0][...], grad * scale, old[1][...], old[2][...], old[3][...],
                    rates[g], DECAY_MATRIX,
                )
                for ref, value in zip(new, results):
                    ref[...] = value

    def gradient_spec(g):
        rows, columns = shapes[g]
        if g == 2:
            return pl.BlockSpec((rows // steps, columns), lambda i: (i + steps, 0))
        if wide[g]:
            return pl.BlockSpec((columns, rows // steps), lambda i: (0, i))
        return pl.BlockSpec((columns, rows), lambda i: (0, 0))

    results = [group[1] for group in groups for _ in range(4)]
    return pl.pallas_call(
        body,
        grid=(steps,),
        in_specs=[pl.BlockSpec(memory_space=pltpu.SMEM)]
        + [
            gradient_spec(g) if k == 0 and g > 0 else spec(a.shape)
            for g, group in enumerate(groups)
            for k, a in enumerate(group)
        ],
        out_specs=[spec(a.shape) for a in results],
        out_shape=[jax.ShapeDtypeStruct(a.shape, FP) for a in results],
        scratch_shapes=[pltpu.VMEM(shapes[1], FP)],
        compiler_params=PARAMS,
        name="update_matrices",
    )(factor, *flat)


class FeedScatter(Scatter):
    def __init__(self, ring, terms):
        self.terms = terms
        self.ring = ring
        self.left = ring.half
        self.send(*terms([ring.half], [[]], BF, True))

    def sums(self, order):
        j, n = self.left, self.ring.count
        rising, falling = self.fresh
        first = j == self.ring.half - 1
        return self.terms([j, n - j], [[(rising, 0)], [(falling, 1 if first else 0)]], BF)

    def advance(self, order):
        order.sums = self.sums(order)
        order.pin()
        self.send(*order.out.sums)

    def finish(self, order):
        while self.left:
            order.pin(self)
            self.advance(order)
        rising, falling = self.fresh
        return self.terms([0], [[(rising, 0), (falling, 0)]], FP)[0]


def pin(streams, *arrays):
    flat = [array for stream in streams for array in stream.fresh] + list(arrays)
    flat = list(lax.optimization_barrier(tuple(flat)))
    for stream in streams:
        stream.fresh = [flat.pop(0), flat.pop(0)]
        stream.arrive()
    return flat


class Taken:
    def __init__(self, arrays):
        self.__dict__["arrays"] = arrays

    def __getattr__(self, name):
        return self.arrays.pop(name)


class Order:
    def __init__(self, meta):
        self.meta = meta

    @property
    def out(self):
        return Taken(self.__dict__)

    def pin(self, *streams):
        arrays = self.__dict__
        names = sorted(arrays)
        leaves, tree = jax.tree.flatten([arrays[name] for name in names])
        arrays.update(zip(names, jax.tree.unflatten(tree, pin(streams, *leaves))))


def local(
    seq_count,
    head_count,
    tokens,
    cotangent,
    prefix_length,
    answer_lengths,
    inward,
    outward,
    expand,
    contract,
    norm_gains,
    moment_inward,
    moment_outward,
    moment_expand,
    moment_contract,
    moment_gains,
    variance_inward,
    variance_outward,
    variance_expand,
    variance_contract,
    variance_gains,
    average_inward,
    average_outward,
    average_expand,
    average_contract,
    average_gains,
):
    n, m = seq_count, head_count
    rows, model = tokens.shape
    share = model // n
    quarter = rows // m
    width = outward.shape[0]
    ring, team = Ring(n), Team(m)
    chips = team.chips

    device = lax.axis_index("seq")
    seq_table = []
    for s in range(n):
        place = ring.inverse[s]
        seq_table.append(
            [s] + [ring.order[(place + b) % n] for b in range(n)]
            + [(ring.inverse[t] - place) % n for t in range(n)]
        )
    seq_row = jnp.asarray(seq_table, jnp.int32)[device]
    head_row = jnp.asarray([team.quarters(h) for h in range(m)], jnp.int32)[lax.axis_index("head")]
    meta = jnp.concatenate(
        [seq_row[:1], prefix_length, answer_lengths, seq_row[1 : n + 1], head_row]
    ).astype(jnp.int32)
    blocks_of = seq_row[n + 1 :]
    places = META_IDS + n

    def flat_inward(array):
        return jnp.transpose(array, (1, 0, 2))

    def column_block(array, b):
        return array[:, b * share : (b + 1) * share]

    o = Order(meta)
    gain_row = norm_gains.astype(BF).reshape(-1, width)
    gain_row = jnp.pad(gain_row, ((0, 32 - gain_row.shape[0]), (0, 0)))
    gather_in = ring.gather(
        jnp.concatenate([flat_inward(inward).astype(BF).reshape(3 * share, width), gain_row], axis=0)
    )
    o.out_grad = mask_cotangent(meta, cotangent, n, m)
    o.up_shard = expand.astype(BF)
    o.down_shard = contract.astype(BF)
    o.out_shard = jnp.transpose(outward).astype(BF)
    o.pin(gather_in)
    gather_in.advance()
    o.pin(gather_in)
    gather_in.advance()
    o.pin(gather_in)
    gather_in.advance()
    o.pin(gather_in)
    in_blocks = gather_in.complete()
    gains = jnp.stack([block[3 * share : 3 * share + 2 * share // width] for block in in_blocks])
    gains = gains.reshape(n, 2, share).transpose(1, 0, 2).reshape(2, model).astype(FP)
    normed_prefix, _ = first_norm(o.meta, tokens, gains, PRE_DEV, n)
    o.kv_send = project_prefix(o.meta, normed_prefix, in_blocks, o.out.out_shard)
    o.pin()
    gather_kv = ring.gather(o.out.kv_send)
    gather_down = ring.gather(o.out.down_shard)
    o.normed_one, o.source = first_norm(o.meta, tokens, gains, rows, n)
    o.pin(gather_kv)
    gather_kv.advance()
    o.projected = project(o.meta, o.normed_one, in_blocks)
    o.pin(gather_kv, gather_down)
    gather_kv.advance()
    gather_down.advance()
    o.pin(gather_kv)
    gather_kv.advance()
    o.pin(gather_kv)
    kv_blocks = gather_kv.complete()
    gather_up = ring.gather(o.out.up_shard)

    o.mixed, o.logs = attention_forward(o.meta, o.projected, kv_blocks)
    o.pin(gather_down)
    gather_down.advance()
    out_rows = (2 * PRE_DEV, share)
    o.kept, o.away = rows_matmul(
        o.meta, "out_part", o.mixed, kv_blocks, m, True, out_rows, "nt"
    )
    o.pin(gather_up)
    gather_up.advance()
    o.got = team.cross(o.out.away)
    o.pin()
    o.arrived = team.send_sums(o.kept, o.got)
    o.pin(gather_down)
    kept, got, arrived = o.out.kept, o.out.got, o.out.arrived
    o.hidden, o.own = second_norm(
        o.meta, [kept, got] + arrived, o.source, gains, quarter, n
    )
    o.pin()
    o.parts = team.send_own(o.out.own)
    parts = o.out.parts
    o.pin(gather_up)
    gather_up.advance()
    gather_down.advance()
    o.parts = parts
    o.pin(gather_up)
    gather_up.advance()
    parts = team.send_half(o.out.parts)
    o.pin(gather_down)
    o.d_activation = feed_back(o.meta, o.out_grad, gather_down.complete())
    o.parts = parts
    o.pin(gather_up)
    o.normed_two, o.both = feed_up(
        o.meta, o.out.parts, gather_up.complete(), o.out.d_activation
    )

    def terms(blocks, received, dtype, cut=False):
        return feed_terms(
            o.meta, o.out_grad, o.normed_two, o.both, blocks, received, n, dtype, cut
        )

    sum_feed = FeedScatter(ring, terms)
    o.pin()
    o.kept, o.away = rows_matmul(
        o.meta, "up_back", o.both, gather_up.blocks, m, False, (0, None), "nt", 1
    )
    o.pin(sum_feed)
    o.got = team.cross(o.out.away)
    o.pin()
    kept, got = o.out.kept, o.out.got
    arrived = team.send_sums(kept, got)
    sum_feed.advance(o)
    o.terms = [kept, got] + arrived
    o.pin()
    o.d_hidden, o.own, o.gain_two = second_norm_back(
        o.meta, o.out.terms, o.hidden, o.out_grad, gains
    )
    o.pin()
    o.parts = team.send_own(o.out.own)

    o.kept, o.away = rows_matmul(
        o.meta, "down_part", o.both, gather_down.blocks, m, False, (0, None), "nn", 0
    )
    o.pin(sum_feed)
    parts = team.send_half(o.out.parts)
    kept, got = o.out.kept, team.cross(o.out.away)
    sum_feed.advance(o)
    o.parts, o.kept, o.got = parts, kept, got
    o.pin()

    o.d_attention, o.d_mixed, o.mixed_order = mixed_back(
        o.meta, o.out.parts, kv_blocks, o.mixed, 2 * PRE_DEV, n, m
    )
    o.d_out_matrix = jnp.einsum(
        "td,tn->dn", o.out.d_attention, o.out.mixed_order, preferred_element_type=FP
    ).astype(BF)
    o.pin()
    kept, got = o.out.kept, o.out.got
    arrived = team.send_sums(kept, got)
    o.d_parts, o.d_send = attention_backward(
        o.meta, o.projected, kv_blocks, o.out.mixed, o.out.d_mixed, o.out.logs,
        o.out.d_out_matrix,
    )
    o.terms = [kept, got] + arrived
    o.pin()

    def part_kv(b):
        return o.d_send[b].astype(FP)

    sum_kv = ring.scatter(part_kv(ring.half))
    result = o.hidden
    for term in o.out.terms:
        result = result + term[:quarter].astype(FP)
    o.own = result.astype(BF)
    o.pin()
    parts = team.send_own(o.out.own)
    o.pin(sum_kv)
    sum_kv.advance(part_kv, o)
    o.pin(sum_feed)
    o.sums = sum_feed.sums(o)
    o.parts = parts
    o.pin(sum_kv)
    sum_kv.advance(part_kv, o)
    parts = team.send_half(o.out.parts)
    o.parts = parts
    o.pin(sum_kv)
    sum_kv.advance(part_kv, o)
    sum_feed.send(*o.out.sums)
    o.layer_output = place_rows(o.meta, o.out.parts, n, m, BF)
    o.pin(sum_kv)

    red_kv_out = sum_kv.finish(part_kv, o)
    o.red_outward = red_kv_out[2 * PRE_DEV :]
    d_prefix = red_kv_out[: 2 * PRE_DEV].astype(BF).reshape(2, PRE_DEV, width)
    d_parts = lax.dynamic_update_slice(o.out.d_parts, d_prefix, (1, 0, 0))
    o.d_projected = jnp.concatenate([d_parts[0], d_parts[1], d_parts[2]], axis=1)
    o.out.d_send

    def part_inward(b):
        return jnp.einsum(
            "td,tn->dn", column_block(o.normed_one, b), o.d_projected, preferred_element_type=FP
        )

    o.far = part_inward(ring.half)
    o.pin()
    sum_inward = ring.scatter(o.out.far)
    o.kept, o.away = rows_matmul(
        o.meta, "in_back", o.d_projected, in_blocks, m, True, (0, 3 * share), "three"
    )
    o.pin(sum_inward)
    kept, got = o.out.kept, team.cross(o.out.away)
    sum_inward.advance(part_inward, o)
    o.kept, o.got = kept, got
    o.pin()
    kept, got = o.out.kept, o.out.got
    arrived = team.send_sums(kept, got)
    o.pin(sum_inward)
    sum_inward.advance(part_inward, o)
    o.terms = [kept, got] + arrived
    o.pin()
    o.own, o.gain_one = first_norm_back(
        o.meta, o.out.terms, o.source, o.d_hidden, gains, n
    )
    o.pin()
    parts = team.send_own(o.out.own)
    o.pin(sum_inward)
    sum_inward.advance(part_inward, o)
    o.parts = parts
    o.pin(sum_feed)
    o.parts = team.send_half(o.parts)
    o.red_feed = sum_feed.finish(o)
    o.out.both
    gain_parts = jnp.concatenate([o.out.gain_one, o.out.gain_two], axis=0).reshape(2, n, share)
    o.gain_parts = jnp.take(gain_parts, blocks_of, axis=1).reshape(2, model)
    red_feed, red_outward = o.out.red_feed, o.out.red_outward
    o.squares = jnp.sum(red_outward * red_outward) + jnp.sum(red_feed * red_feed)
    o.pin()
    o.input_grad = place_rows(o.meta, o.out.parts, n, m, FP)
    o.pin(sum_inward)
    red_inward = sum_inward.finish(part_inward, o)
    layer_output, input_grad, gain_parts = o.out.layer_output, o.out.input_grad, o.out.gain_parts

    squares = jnp.sum(red_inward * red_inward) + o.out.squares
    sums = jnp.concatenate([gain_parts, jnp.full((1, model), squares, FP)], axis=0)
    sums = total_of_all(sums, n, m)
    gain_sums = sums[:2]
    grad_norm = jnp.sqrt(sums[2, 0] + jnp.sum(gain_sums * gain_sums))
    factor = CLIP_NORM / jnp.maximum(grad_norm, CLIP_NORM)
    red_gains = lax.dynamic_slice(gain_sums, (0, device * share), (2, share))

    new = update_matrices(
        jnp.reshape(factor, (1,)),
        (
            (
                red_inward, flat_inward(inward), flat_inward(moment_inward),
                flat_inward(variance_inward), flat_inward(average_inward),
            ),
            (red_outward, outward, moment_outward, variance_outward, average_outward),
            (red_feed, expand, moment_expand, variance_expand, average_expand),
            (red_feed, contract, moment_contract, variance_contract, average_contract),
        ),
        (RATE_INWARD, RATE_OUTWARD, RATE_EXPAND, RATE_CONTRACT),
        4,
    )
    in_new = tuple(jnp.transpose(array, (1, 0, 2)) for array in new[:4])
    gain_new = adamw(
        norm_gains, red_gains * factor, moment_gains, variance_gains, average_gains, RATE_GAINS, 0.0
    )
    return (
        (layer_output, input_grad, jnp.reshape(grad_norm, (1,)))
        + in_new + tuple(new[4:]) + gain_new
    )


def solution(mesh):
    in_place = P("seq", None, "head")
    out_place = P("head", "seq")
    up_place = P("seq", "head")
    gain_place = P(None, "seq")
    weights = (in_place, out_place, up_place, out_place, gain_place)
    placed = (P("seq", None), P("seq", None), P(), P("seq")) + weights * 4
    results = (P("seq", None), P("seq", None), P())
    for place in weights:
        results += (place,) * 4
    return jax.shard_map(
        functools.partial(local, mesh.shape["seq"], mesh.shape["head"]),
        mesh=mesh,
        in_specs=placed,
        out_specs=results,
        check_vma=False,
    )
```

time: 936 us -> 804 us (0.86)
  Pallas kernels: 84.1 us -> 296 us
  matrix products: 168 us -> 23.6 us
  local copies, waits for them, and re-layouts: 84.5 us -> 23.4 us
  other arithmetic: 93.3 us -> 36.9 us
  waiting for transfers between devices: 359 us -> 331 us
  starting transfers between devices: 103 us -> 78.7 us
  blocking collectives: 22.1 us -> 0 us
    pallas_call x6 -> x25, Pallas kernels: 84.1 us -> 296 us  [the longest x24 276 us: call(): pl.pallas_call(body, grid_spec=pltpu.PrefetchScalarGridSpec(num_scalar_pr...]
    dot_general x48 -> x9, matrix products: 168 us -> 23.6 us  [the longest x8 17.3 us: part_inward(): jnp.einsum('td,tn->dn', column_block(o.normed_one, b), o.d_projected, pre...]
    unnamed x200 -> x140, local copies, waits for them, and re-layouts: 68.7 us -> 10.7 us
    ppermute x96 -> x72, waiting for transfers between devices: 345 us -> 319 us  [the longest x16 155 us: advance(): lax.ppermute(upper, 'seq', ring.down)]
    add x5 -> x1, other arithmetic: 23.4 us -> 0.62 us  [adamw(): average = EMA_KEEP * average + (1.0 - EMA_KEEP) * weight_new]
    all_gather x1 -> x0, blocking collectives: 22.1 us -> none  [local(): gain_rows = lax.all_gather(norm_gains.astype(BF), 'seq', axis=1, tiled=True)]
    ppermute x96 -> x72, starting transfers between devices: 92.6 us -> 72.3 us  [the longest x16 18.8 us: advance(): lax.ppermute(lower, 'seq', ring.up)]
    select_n x13 -> x2, other arithmetic: 13.9 us -> 0.09 us  [local(): o.gain_parts = jnp.take(gain_parts, blocks_of, axis=1).reshape(2, model)]
  transfers between devices with their start and end apart: 106 -> 77, of which waited for: 48 -> 55; matrix products, arithmetic and copies ran while one was open for 28% -> 4% of each run, Pallas kernels for 7% -> 29%
where the time goes in v2:
time: 804 us; the launch traced here: 797 us
  waiting for transfers between devices  331 us (41%)
  Pallas kernels  296 us (37%)
  starting transfers between devices  78.7 us (10%)
  other arithmetic  36.9 us (5%)
  matrix products  23.6 us (3%)
  local copies, waits for them, and re-layouts  23.4 us (3%)
    pallas_call x24, Pallas kernels, call(): pl.pallas_call(body, grid_spec=pltpu.PrefetchScalarGridSpec(num_scalar_pr...  276 us
    ppermute x16, waiting for transfers between devices, advance(): lax.ppermute(upper, 'seq', ring.down)  155 us
    ppermute x12, waiting for transfers between devices, send(): lax.ppermute(rising, 'seq', self.ring.up)  119 us
    pallas_call x1, Pallas kernels, update_matrices(): pl.pallas_call(body, grid=(steps,), in_specs=[pl.BlockSpec(memory_space=p...  19.9 us
    ppermute x16, starting transfers between devices, advance(): lax.ppermute(lower, 'seq', ring.up)  18.8 us
    dot_general x8, matrix products, part_inward(): jnp.einsum('td,tn->dn', column_block(o.normed_one, b), o.d_projected, pre...  17.3 us
    ppermute x4, waiting for transfers between devices, send_sums(): arrived.append(lax.ppermute(term.astype(BF), 'head', self.shift(k)))  16.5 us
  transfers between devices with their start and end apart: 77, of which 55 were waited for; matrix products, arithmetic and copies ran while one was open for 4% of the time, Pallas kernels for 29%

profile of v2, /device:TPU:0, one launch (start us, length us, event | category | flops | bytes accessed | tf_op | source)
XLA Modules:
  0.0 796.7 jit_solution(3233060817061956407)
XLA Ops:
  2.3 3.0 collective-permute-start
  8.8 5.9 mask_cotangent.1.x_ref.grad_ref.refs_4_
  18.6 5.0 collective-permute-done.refs_1_
  27.0 16.9 %collective-permute-done.2.refs_2_ = bf16[800,512]{1,0:T(8,128)(2,1)} collective-permute-done((bf16[800,512]{1,0:T(8,128)(2,1)S(1)}, bf16[800,512]{1,0:T(8,128)(2,1)}, u32[]{:S(2)}, u32[]{:S(2)}) %collective-permute-start.2) | collective-permute-done | bytes 819232 | tf_op jit(solution)/shard_map/ppermute | solution.py:85
  47.3 15.7 %collective-permute-done.4.refs_3_ = bf16[800,512]{1,0:T(8,128)(2,1)S(1)} collective-permute-done((bf16[800,512]{1,0:T(8,128)(2,1)}, bf16[800,512]{1,0:T(8,128)(2,1)S(1)}, u32[]{:S(2)}, u32[]{:S(2)}) %collective-permute-start.4) | collective-permute-done | bytes 819232 | tf_op jit(solution)/shard_map/ppermute | solution.py:85
  68.8 4.6 collective-permute-done.6
  79.3 4.1 first_norm.2
  83.4 5.8 project_prefix.1.refs_0_.refs_8_.refs_3_
  93.4 8.2 %first_norm.3 = (bf16[1024,2048]{1,0:T(8,128)(2,1)}, bf16[1024,2048]{1,0:T(8,128)(2,1)}) custom-call(s32[15]{0:T(128)} %concatenate.57.meta_ref, bf16[1024,2048]{1,0:T(8,128)(2,1)} %in_ref.5, f32[2,2048]{1,0:T(2,128)} %bitcast.96), custom_call_target="tpu_custom_call" | custom-call | flops 1 | bytes 1 | tf_op jit(solution)/shard_map/first_norm/pallas_call | solution.py:234
  101.5 8.5 %collective-permute-done.8.refs_1_.refs_9_.refs_4_ = bf16[768,512]{1,0:T(8,128)(2,1)S(1)} collective-permute-done((bf16[768,512]{1,0:T(8,128)(2,1)}, bf16[768,512]{1,0:T(8,128)(2,1)S(1)}, u32[]{:S(2)}, u32[]{:S(2)}) %collective-permute-start.8) | collective-permute-done | bytes 786464 | tf_op jit(solution)/shard_map/ppermute | solution.py:85
  112.8 12.7 %project.1.q_ref.k_ref.v_ref = bf16[3,1024,512]{2,1,0:T(8,128)(2,1)} custom-call(s32[15]{0:T(128)} %concatenate.57.meta_ref, bf16[1024,2048]{1,0:T(8,128)(2,1)} %get-tuple-element.1334.x_ref, bf16[800,512]{1,0:T(8,128)(2,1)} %copy-done.8, bf16[800,512]{1,0:T(8,128)(2,1)} %copy-done.18, bf16[800,512]{1,0:T(8,128)(2,1)} %collective-permute-done.2.refs_2_, ...), custom_call_target="tpu_custom_call" | custom-call | flops 1 | bytes 1 | tf_op jit(solution)/shard_map/project/pallas_call | solution.py:234
  125.5 7.0 collective-permute-done.12.refs_1_
  133.2 12.8 %collective-permute-done.10.refs_2_.refs_10_.refs_5_ = bf16[768,512]{1,0:T(8,128)(2,1)S(1)} collective-permute-done((bf16[768,512]{1,0:T(8,128)(2,1)S(1)}, bf16[768,512]{1,0:T(8,128)(2,1)S(1)}, u32[]{:S(2)}, u32[]{:S(2)}) %collective-permute-start.10) | collective-permute-done | bytes 786464 | tf_op jit(solution)/shard_map/ppermute | solution.py:85
  148.9 14.7 %collective-permute-done.14.refs_3_.refs_11_.refs_6_ = bf16[768,512]{1,0:T(8,128)(2,1)S(1)} collective-permute-done((bf16[768,512]{1,0:T(8,128)(2,1)S(1)}, bf16[768,512]{1,0:T(8,128)(2,1)S(1)}, u32[]{:S(2)}, u32[]{:S(2)}) %collective-permute-start.14) | collective-permute-done | bytes 786464 | tf_op jit(solution)/shard_map/ppermute | solution.py:85
  168.8 7.9 collective-permute-done.16
  180.6 20.8 %attention_forward.1 = (bf16[1024,512]{1,0:T(8,128)(2,1)}, f32[4,1024,1]{2,1,0:T(8,128)}) custom-call(s32[15]{0:T(128)} %concatenate.57.meta_ref, bf16[3,1024,512]{2,1,0:T(8,128)(2,1)} %project.1.q_ref.k_ref.v_ref, bf16[3,1024,512]{2,1,0:T(8,128)(2,1)} %project.1.q_ref.k_ref.v_ref, bf16[3,1024,512]{2,1,0:T(8,128)(2,1)} %project.1.q_ref.k_ref.v_ref, ...), custom_call_target="tpu_custom_call" | custom-call | flops 1 | bytes 1 | tf_op jit(solution)/shard_map/attention_forward/pallas_call | solution.py:234
  201.5 6.5 out_part.1
  208.0 5.8 collective-permute-done.18.refs_4_.refs_1_
  218.7 2.4 add_convert_fusion.4
  224.7 15.8 %collective-permute-done.24.refs_3_ = bf16[2048,256]{1,0:T(8,128)(2,1)S(1)} collective-permute-done((bf16[2048,256]{1,0:T(8,128)(2,1)}, bf16[2048,256]{1,0:T(8,128)(2,1)S(1)}, u32[]{:S(2)}, u32[]{:S(2)}) %collective-permute-start.24) | collective-permute-done | bytes 1048608 | tf_op jit(solution)/shard_map/ppermute | solution.py:85
  241.2 5.2 collective-permute-done.27.refs_2_
  247.4 5.4 second_norm.1
  252.8 9.8 %collective-permute-done.22.refs_5_.refs_2_ = bf16[256,2048]{1,0:T(8,128)(2,1)S(1)} collective-permute-done((bf16[256,2048]{1,0:T(8,128)(2,1)}, bf16[256,2048]{1,0:T(8,128)(2,1)S(1)}, u32[]{:S(2)}, u32[]{:S(2)}) %collective-permute-start.22) | collective-permute-done | bytes 1048608 | tf_op jit(solution)/shard_map/ppermute | solution.py:85
  266.5 21.0 %collective-permute-done.28.refs_6_.refs_3_ = bf16[256,2048]{1,0:T(8,128)(2,1)S(1)} collective-permute-done((bf16[256,2048]{1,0:T(8,128)(2,1)S(1)}, bf16[256,2048]{1,0:T(8,128)(2,1)S(1)}, u32[]{:S(2)}, u32[]{:S(2)}) %collective-permute-start.28) | collective-permute-done | bytes 1048608 | tf_op jit(solution)/shard_map/ppermute | solution.py:85
  289.1 3.2 pad_maximum_fusion.1
  297.3 9.9 %collective-permute-done.33 = bf16[1024,256]{1,0:T(8,128)(2,1)S(1)} collective-permute-done((bf16[1024,256]{1,0:T(8,128)(2,1)S(1)}, bf16[1024,256]{1,0:T(8,128)(2,1)S(1)}, u32[]{:S(2)}, u32[]{:S(2)}) %collective-permute-start.33) | collective-permute-done | bytes 524320 | tf_op jit(solution)/shard_map/ppermute | solution.py:85
  309.1 15.3 %feed_back.1.refs_11_ = bf16[1024,2048]{1,0:T(8,128)(2,1)} custom-call(s32[15]{0:T(128)} %concatenate.57.meta_ref, bf16[1024,2048]{1,0:T(8,128)(2,1)} %mask_cotangent.1.x_ref.grad_ref.refs_4_, bf16[2048,256]{1,0:T(8,128)(2,1)} %convert_element_type.203.refs_0_, bf16[2048,256]{1,0:T(8,128)(2,1)} %copy-done.32, ...), custom_call_target="tpu_custom_call" | custom-call | flops 1 | bytes 1 | tf_op jit(solution)/shard_map/feed_back/pallas_call | solution.py:234
  325.5 22.4 %feed_up.1 = (bf16[1024,2048]{1,0:T(8,128)(2,1)}, bf16[2,1024,2048]{2,1,0:T(8,128)(2,1)}) custom-call(s32[15]{0:T(128)} %concatenate.57.meta_ref, bf16[256,2048]{1,0:T(8,128)(2,1)} %get-tuple-element.848.refs_0_, bf16[256,2048]{1,0:T(8,128)(2,1)} %copy-done.38, bf16[512,2048]{1,0:T(8,128)(2,1)} %collective-permute-done.35.refs_2_, ...), custom_call_target="tpu_custom_call" | custom-call | flops 1 | bytes 1 | tf_op jit(solution)/shard_map/feed_up/pallas_call | solution.py:234
  347.9 7.1 feed_terms.5
  357.2 15.5 %up_back.1 = (bf16[512,2048]{1,0:T(8,128)(2,1)}, bf16[512,2048]{1,0:T(8,128)(2,1)}) custom-call(s32[15]{0:T(128)} %concatenate.57.meta_ref, bf16[2,1024,2048]{2,1,0:T(8,128)(2,1)} %get-tuple-element.1319.both_ref.x_any, bf16[256,2048]{1,0:T(8,128)(2,1)} %convert_element_type.206.refs_3_.refs_0_, bf16[256,2048]{1,0:T(8,128)(2,1)} %collective-permute-done.18.refs_4_.refs_1_, ...), custom_call_target="tpu_custom_call" | custom-call | flops 1 | bytes 1 | tf_op jit(solution)/shard_map/up_back/pallas_call | solution.py:234
  372.7 6.3 collective-permute-done.36.refs_0_
  380.1 4.4 collective-permute-done.38.refs_1_
  384.5 3.3 add_convert_fusion.3
  389.4 12.2 %feed_terms.6 = (bf16[512,2048]{1,0:T(8,128)(2,1)}, bf16[512,2048]{1,0:T(8,128)(2,1)}) custom-call(s32[15]{0:T(128)} %concatenate.57.meta_ref, bf16[1024,2048]{1,0:T(8,128)(2,1)} %mask_cotangent.1.x_ref.grad_ref.refs_4_, bf16[1024,2048]{1,0:T(8,128)(2,1)} %get-tuple-element.1314.norm_ref, bf16[2,1024,2048]{2,1,0:T(8,128)(2,1)} %get-tuple-element.1319.both_ref.x_any, ...), custom_call_target="tpu_custom_call" | custom-call | flops 1 | bytes 1 | tf_op jit(solution)/shard_map/feed_terms/pallas_call | solution.py:234
  403.8 9.5 %collective-permute-done.41.refs_2_ = bf16[256,2048]{1,0:T(8,128)(2,1)S(1)} collective-permute-done((bf16[256,2048]{1,0:T(8,128)(2,1)}, bf16[256,2048]{1,0:T(8,128)(2,1)S(1)}, u32[]{:S(2)}, u32[]{:S(2)}) %collective-permute-start.41) | collective-permute-done | bytes 1048608 | tf_op jit(solution)/shard_map/ppermute | solution.py:174
  414.2 6.6 second_norm_back.1
  422.4 15.3 %down_part.1 = (bf16[512,2048]{1,0:T(8,128)(2,1)}, bf16[512,2048]{1,0:T(8,128)(2,1)}) custom-call(s32[15]{0:T(128)} %concatenate.57.meta_ref, bf16[2,1024,2048]{2,1,0:T(8,128)(2,1)} %get-tuple-element.1319.both_ref.x_any, bf16[2048,256]{1,0:T(8,128)(2,1)} %convert_element_type.203.refs_0_, bf16[2048,256]{1,0:T(8,128)(2,1)} %copy-done.32, ...), custom_call_target="tpu_custom_call" | custom-call | flops 1 | bytes 1 | tf_op jit(solution)/shard_map/down_part/pallas_call | solution.py:234
  437.7 11.4 %collective-permute-done.39.refs_0_ = bf16[512,2048]{1,0:T(8,128)(2,1)S(1)} collective-permute-done((bf16[512,2048]{1,0:T(8,128)(2,1)}, bf16[512,2048]{1,0:T(8,128)(2,1)S(1)}, u32[]{:S(2)}, u32[]{:S(2)}) %collective-permute-start.39) | collective-permute-done | bytes 2097184 | tf_op jit(solution)/shard_map/ppermute | solution.py:117
  452.7 13.2 %feed_terms.7 = (bf16[512,2048]{1,0:T(8,128)(2,1)}, bf16[512,2048]{1,0:T(8,128)(2,1)}) custom-call(s32[15]{0:T(128)} %concatenate.57.meta_ref, bf16[1024,2048]{1,0:T(8,128)(2,1)} %mask_cotangent.1.x_ref.grad_ref.refs_4_, bf16[1024,2048]{1,0:T(8,128)(2,1)} %get-tuple-element.1314.norm_ref, bf16[2,1024,2048]{2,1,0:T(8,128)(2,1)} %get-tuple-element.1319.both_ref.x_any, ...), custom_call_target="tpu_custom_call" | custom-call | flops 1 | bytes 1 | tf_op jit(solution)/shard_map/feed_terms/pallas_call | solution.py:234
  465.9 9.4 %mixed_back.1 = (bf16[1024,2048]{1,0:T(8,128)(2,1)}, bf16[1024,512]{1,0:T(8,128)(2,1)}, bf16[1024,512]{1,0:T(8,128)(2,1)}) custom-call(s32[15]{0:T(128)} %concatenate.57.meta_ref, bf16[256,2048]{1,0:T(8,128)(2,1)} %get-tuple-element.982.refs_0_, bf16[256,2048]{1,0:T(8,128)(2,1)} %copy-done.40, bf16[512,2048]{1,0:T(8,128)(2,1)} %collective-permute-done.44.refs_2_, ...), custom_call_target="tpu_custom_call" | custom-call | flops 1 | bytes 1 | tf_op jit(solution)/shard_map/mixed_back/pallas_call | solution.py:234
  475.2 6.3 convolution_convert_fusion.refs_19_
  485.7 35.5 %attention_backward.1 = (bf16[3,1024,512]{2,1,0:T(8,128)(2,1)}, bf16[8,768,512]{2,1,0:T(8,128)(2,1)}) custom-call(s32[15]{0:T(128)} %concatenate.57.meta_ref, bf16[3,1024,512]{2,1,0:T(8,128)(2,1)} %project.1.q_ref.k_ref.v_ref, bf16[3,1024,512]{2,1,0:T(8,128)(2,1)} %project.1.q_ref.k_ref.v_ref, bf16[3,1024,512]{2,1,0:T(8,128)(2,1)} %project.1.q_ref.k_ref.v_ref, ...), custom_call_target="tpu_custom_call" | custom-call | flops 1 | bytes 1 | tf_op jit(solution)/shard_map/attention_backward/pallas_call | solution.py:234
  528.4 11.1 %collective-permute-done.46 = bf16[384,512]{1,0:T(8,128)(2,1)S(1)} collective-permute-done((bf16[384,512]{1,0:T(8,128)(2,1)S(1)}, bf16[384,512]{1,0:T(8,128)(2,1)S(1)}, u32[]{:S(2)}, u32[]{:S(2)}) %collective-permute-start.46) | collective-permute-done | bytes 393248 | tf_op jit(solution)/shard_map/ppermute | solution.py:117
  547.3 13.1 %feed_terms.8 = (bf16[512,2048]{1,0:T(8,128)(2,1)}, bf16[512,2048]{1,0:T(8,128)(2,1)}) custom-call(s32[15]{0:T(128)} %concatenate.57.meta_ref, bf16[1024,2048]{1,0:T(8,128)(2,1)} %mask_cotangent.1.x_ref.grad_ref.refs_4_, bf16[1024,2048]{1,0:T(8,128)(2,1)} %get-tuple-element.1314.norm_ref, bf16[2,1024,2048]{2,1,0:T(8,128)(2,1)} %get-tuple-element.1319.both_ref.x_any, ...), custom_call_target="tpu_custom_call" | custom-call | flops 1 | bytes 1 | tf_op jit(solution)/shard_map/feed_terms/pallas_call | solution.py:234
  560.5 2.7 collective-permute-done.48
  569.3 17.9 %collective-permute-done.53 = bf16[768,512]{1,0:T(8,128)(2,1)S(1)} collective-permute-done((bf16[768,512]{1,0:T(8,128)(2,1)S(1)}, bf16[768,512]{1,0:T(8,128)(2,1)S(1)}, u32[]{:S(2)}, u32[]{:S(2)}) %collective-permute-start.53) | collective-permute-done | bytes 786464 | tf_op jit(solution)/shard_map/ppermute | solution.py:117
  589.8 6.4 place_rows.2
  596.2 10.7 %collective-permute-done.56 = bf16[768,512]{1,0:T(8,128)(2,1)} collective-permute-done((bf16[768,512]{1,0:T(8,128)(2,1)S(1)}, bf16[768,512]{1,0:T(8,128)(2,1)}, u32[]{:S(2)}, u32[]{:S(2)}) %collective-permute-start.56) | collective-permute-done | bytes 786464 | tf_op jit(solution)/shard_map/ppermute | solution.py:117
  617.2 13.0 %in_back.1 = (bf16[512,2048]{1,0:T(8,128)(2,1)}, bf16[512,2048]{1,0:T(8,128)(2,1)}) custom-call(s32[15]{0:T(128)} %concatenate.57.meta_ref, bf16[1024,1536]{1,0:T(8,128)(2,1)} %pad_maximum_fusion.x_any, bf16[800,512]{1,0:T(8,128)(2,1)} %copy-done.8, bf16[800,512]{1,0:T(8,128)(2,1)} %copy-done.18, bf16[800,512]{1,0:T(8,128)(2,1)} %collective-permute-done.2.refs_2_, ...), custom_call_target="tpu_custom_call" | custom-call | flops 1 | bytes 1 | tf_op jit(solution)/shard_map/in_back/pallas_call | solution.py:234
  640.2 14.1 %collective-permute-done.60 = bf16[256,1536]{1,0:T(8,128)(2,1)S(1)} collective-permute-done((bf16[256,1536]{1,0:T(8,128)(2,1)S(1)}, bf16[256,1536]{1,0:T(8,128)(2,1)S(1)}, u32[]{:S(2)}, u32[]{:S(2)}) %collective-permute-start.60) | collective-permute-done | bytes 786464 | tf_op jit(solution)/shard_map/ppermute | solution.py:117
  663.2 6.1 first_norm_back.1
  670.8 45.0 %collective-permute-done.63 = bf16[256,1536]{1,0:T(8,128)(2,1)} collective-permute-done((bf16[256,1536]{1,0:T(8,128)(2,1)}, bf16[256,1536]{1,0:T(8,128)(2,1)}, u32[]{:S(2)}, u32[]{:S(2)}) %collective-permute-start.63) | collective-permute-done | bytes 786464 | tf_op jit(solution)/shard_map/ppermute | solution.py:117
  716.8 3.0 fusion.4
  719.8 3.1 fusion.3
  726.9 8.2 %feed_terms.9.refs_10_.refs_15_ = f32[512,2048]{1,0:T(8,128)} custom-call(s32[15]{0:T(128)} %concatenate.57.meta_ref, bf16[1024,2048]{1,0:T(8,128)(2,1)} %mask_cotangent.1.x_ref.grad_ref.refs_4_, bf16[1024,2048]{1,0:T(8,128)(2,1)} %get-tuple-element.1314.norm_ref, bf16[2,1024,2048]{2,1,0:T(8,128)(2,1)} %get-tuple-element.1319.both_ref.x_any, ...), custom_call_target="tpu_custom_call" | custom-call | flops 1 | bytes 1 | tf_op jit(solution)/shard_map/feed_terms/pallas_call | solution.py:234
  735.1 3.9 multiply_reduce_fusion
  741.7 7.3 place_rows.3
  749.1 4.4 multiply_reduce_fusion.1
  757.0 2.5 collective-permute-done.73
  760.3 3.1 collective-permute-done.74
  764.9 2.5 collective-permute-done.75
  767.4 2.5 collective-permute-start.76
  769.9 2.4 collective-permute-done.76
  775.5 19.9 %update_matrices.1 = (f32[3,256,512]{2,1,0:T(8,128)}, f32[3,256,512]{2,1,0:T(8,128)}, f32[3,256,512]{2,1,0:T(8,128)}, f32[3,256,512]{2,1,0:T(8,128)}, f32[512,25...) custom-call(f32[1]{0:T(128)} %bitcast.33.factor_ref, ...), custom_call_target="tpu_custom_call" | custom-call | tf_op jit(solution)/shard_map/update_matrices/pallas_call | solution.py:1059
  (348 shorter events, 154.3 us)
Async XLA Ops:
  2.3 21.3 %collective-permute-start = (bf16[800,512]{1,0:T(8,128)(2,1)S(1)}, bf16[800,512]{1,0:T(8,128)(2,1)S(1)}, u32[]{:S(2)}, u32[]{:S(2)}) collective-permute-start(bf16[800,512]{1,0:T(8,128)(2,1)S(1)} %fusion.11.refs_0_), channel_id=1, source_target_pairs={{8,0},{16,8},{24,16},{28,24},{20,28},{12,20},{4,12},{0,4},{9,1},{1... | collective-permute-start | bytes 2457608 | tf_op jit(solution)/shard_map/ppermute | solution.py:85
  5.3 19.7 %collective-permute-start.1 = (bf16[800,512]{1,0:T(8,128)(2,1)S(1)}, bf16[800,512]{1,0:T(8,128)(2,1)S(1)}, u32[]{:S(2)}, u32[]{:S(2)}) collective-permute-start(bf16[800,512]{1,0:T(8,128)(2,1)S(1)} %fusion.11.refs_0_), channel_id=1, source_target_pairs={{0,8},{8,16},{16,24},{24,28},{28,20},{20,12},{12,4},{4,0},{1,9},{9... | collective-permute-start | bytes 2457608 | tf_op jit(solution)/shard_map/ppermute | solution.py:86
  25.0 18.9 %collective-permute-start.2 = (bf16[800,512]{1,0:T(8,128)(2,1)S(1)}, bf16[800,512]{1,0:T(8,128)(2,1)}, u32[]{:S(2)}, u32[]{:S(2)}) collective-permute-start(bf16[800,512]{1,0:T(8,128)(2,1)S(1)} %collective-permute-done.refs_1_), channel_id=1, source_target_pairs={{8,0},{16,8},{24,16},{28,24},{20,28},{12,20},{4,12},{0,4},{9,1},{1... | collective-permute-start | bytes 2457608 | tf_op jit(solution)/shard_map/ppermute | solution.py:85
  26.6 18.6 %collective-permute-start.3 = (bf16[800,512]{1,0:T(8,128)(2,1)S(1)}, bf16[800,512]{1,0:T(8,128)(2,1)}, u32[]{:S(2)}, u32[]{:S(2)}) collective-permute-start(bf16[800,512]{1,0:T(8,128)(2,1)S(1)} %collective-permute-done.1.refs_7_), channel_id=1, source_target_pairs={{0,8},{8,16},{16,24},{24,28},{28,20},{20,12},{12,4},{4,0},{1,9},{9... | collective-permute-start | bytes 2457608 | tf_op jit(solution)/shard_map/ppermute | solution.py:86
  45.2 17.8 %collective-permute-start.4 = (bf16[800,512]{1,0:T(8,128)(2,1)}, bf16[800,512]{1,0:T(8,128)(2,1)S(1)}, u32[]{:S(2)}, u32[]{:S(2)}) collective-permute-start(bf16[800,512]{1,0:T(8,128)(2,1)} %collective-permute-done.2.refs_2_), channel_id=1, source_target_pairs={{8,0},{16,8},{24,16},{28,24},{20,28},{12,20},{4,12},{0,4},{9,1},{1... | collective-permute-start | bytes 2457608 | tf_op jit(solution)/shard_map/ppermute | solution.py:85
  46.8 17.5 %collective-permute-start.5 = (bf16[800,512]{1,0:T(8,128)(2,1)}, bf16[800,512]{1,0:T(8,128)(2,1)S(1)}, u32[]{:S(2)}, u32[]{:S(2)}) collective-permute-start(bf16[800,512]{1,0:T(8,128)(2,1)} %collective-permute-done.3.refs_6_), channel_id=1, source_target_pairs={{0,8},{8,16},{16,24},{24,28},{28,20},{20,12},{12,4},{4,0},{1,9},{9... | collective-permute-start | bytes 2457608 | tf_op jit(solution)/shard_map/ppermute | solution.py:86
  89.2 20.7 %collective-permute-start.8 = (bf16[768,512]{1,0:T(8,128)(2,1)}, bf16[768,512]{1,0:T(8,128)(2,1)S(1)}, u32[]{:S(2)}, u32[]{:S(2)}) collective-permute-start(bf16[768,512]{1,0:T(8,128)(2,1)} %project_prefix.1.refs_0_.refs_8_.refs_3_), channel_id=1, source_target_pairs={{8,0},{16,8},{24,16},{28,24},{20,28},{12,20},{4,12},{0,4},{9,1},{1... | collective-permute-start | bytes 2359304 | tf_op jit(solution)/shard_map/ppermute | solution.py:85
  90.1 20.7 %collective-permute-start.9 = (bf16[768,512]{1,0:T(8,128)(2,1)}, bf16[768,512]{1,0:T(8,128)(2,1)S(1)}, u32[]{:S(2)}, u32[]{:S(2)}) collective-permute-start(bf16[768,512]{1,0:T(8,128)(2,1)} %project_prefix.1.refs_0_.refs_8_.refs_3_), channel_id=1, source_target_pairs={{0,8},{8,16},{16,24},{24,28},{28,20},{20,12},{12,4},{4,0},{1,9},{9... | collective-permute-start | bytes 2359304 | tf_op jit(solution)/shard_map/ppermute | solution.py:86
  91.3 41.1 %collective-permute-start.12 = (bf16[2048,256]{1,0:T(8,128)(2,1)S(1)}, bf16[2048,256]{1,0:T(8,128)(2,1)S(1)}, u32[]{:S(2)}, u32[]{:S(2)}) collective-permute-start(bf16[2048,256]{1,0:T(8,128)(2,1)S(1)} %copy-done.12), channel_id=1, source_target_pairs={{8,0},{16,8},{24,16},{28,24},{20,28},{12,20},{4,12},{0,4},{9,1},{1... | collective-permute-start | bytes 3145736 | tf_op jit(solution)/shard_map/ppermute | solution.py:85
  92.1 41.1 %collective-permute-start.13 = (bf16[2048,256]{1,0:T(8,128)(2,1)S(1)}, bf16[2048,256]{1,0:T(8,128)(2,1)S(1)}, u32[]{:S(2)}, u32[]{:S(2)}) collective-permute-start(bf16[2048,256]{1,0:T(8,128)(2,1)S(1)} %copy-done.12), channel_id=1, source_target_pairs={{0,8},{8,16},{16,24},{24,28},{28,20},{20,12},{12,4},{4,0},{1,9},{9... | collective-permute-start | bytes 3145736 | tf_op jit(solution)/shard_map/ppermute | solution.py:86
  110.8 35.2 %collective-permute-start.10 = (bf16[768,512]{1,0:T(8,128)(2,1)S(1)}, bf16[768,512]{1,0:T(8,128)(2,1)S(1)}, u32[]{:S(2)}, u32[]{:S(2)}) collective-permute-start(bf16[768,512]{1,0:T(8,128)(2,1)S(1)} %collective-permute-done.8.refs_1_.refs_9_.refs_4_), channel_id=1, source_target_pairs={{8,0},{16,8},{24,16},{28,24},{20,28},{12,20},{4,12},{0,4},{9,1},{1... | collective-permute-start | bytes 2359304 | tf_op jit(solution)/shard_map/ppermute | solution.py:85
  111.4 35.5 %collective-permute-start.11 = (bf16[768,512]{1,0:T(8,128)(2,1)S(1)}, bf16[768,512]{1,0:T(8,128)(2,1)S(1)}, u32[]{:S(2)}, u32[]{:S(2)}) collective-permute-start(bf16[768,512]{1,0:T(8,128)(2,1)S(1)} %collective-permute-done.9.refs_7_.refs_15_.refs_10_), channel_id=1, source_target_pairs={{0,8},{8,16},{16,24},{24,28},{28,20},{20,12},{12,4},{4,0},{1,9},{9... | collective-permute-start | bytes 2359304 | tf_op jit(solution)/shard_map/ppermute | solution.py:86
  146.9 16.7 %collective-permute-start.14 = (bf16[768,512]{1,0:T(8,128)(2,1)S(1)}, bf16[768,512]{1,0:T(8,128)(2,1)S(1)}, u32[]{:S(2)}, u32[]{:S(2)}) collective-permute-start(bf16[768,512]{1,0:T(8,128)(2,1)S(1)} %collective-permute-done.10.refs_2_.refs_10_.refs_5_), channel_id=1, source_target_pairs={{8,0},{16,8},{24,16},{28,24},{20,28},{12,20},{4,12},{0,4},{9,1},{1... | collective-permute-start | bytes 2359304 | tf_op jit(solution)/shard_map/ppermute | solution.py:85
  147.3 17.3 %collective-permute-start.15 = (bf16[768,512]{1,0:T(8,128)(2,1)S(1)}, bf16[768,512]{1,0:T(8,128)(2,1)S(1)}, u32[]{:S(2)}, u32[]{:S(2)}) collective-permute-start(bf16[768,512]{1,0:T(8,128)(2,1)S(1)} %collective-permute-done.11.refs_6_.refs_14_.refs_9_), channel_id=1, source_target_pairs={{0,8},{8,16},{16,24},{24,28},{28,20},{20,12},{12,4},{4,0},{1,9},{9... | collective-permute-start | bytes 2359304 | tf_op jit(solution)/shard_map/ppermute | solution.py:86
  166.7 34.7 %collective-permute-start.20 = (bf16[2048,256]{1,0:T(8,128)(2,1)S(1)}, bf16[2048,256]{1,0:T(8,128)(2,1)}, u32[]{:S(2)}, u32[]{:S(2)}) collective-permute-start(bf16[2048,256]{1,0:T(8,128)(2,1)S(1)} %collective-permute-done.12.refs_1_), channel_id=1, source_target_pairs={{8,0},{16,8},{24,16},{28,24},{20,28},{12,20},{4,12},{0,4},{9,1},{1... | collective-permute-start | bytes 3145736 | tf_op jit(solution)/shard_map/ppermute | solution.py:85
  167.3 34.2 %collective-permute-start.21 = (bf16[2048,256]{1,0:T(8,128)(2,1)S(1)}, bf16[2048,256]{1,0:T(8,128)(2,1)}, u32[]{:S(2)}, u32[]{:S(2)}) collective-permute-start(bf16[2048,256]{1,0:T(8,128)(2,1)S(1)} %collective-permute-done.13.refs_7_), channel_id=1, source_target_pairs={{0,8},{8,16},{16,24},{24,28},{28,20},{20,12},{12,4},{4,0},{1,9},{9... | collective-permute-start | bytes 3145736 | tf_op jit(solution)/shard_map/ppermute | solution.py:86
  177.3 36.4 %collective-permute-start.18 = (bf16[256,2048]{1,0:T(8,128)(2,1)S(1)}, bf16[256,2048]{1,0:T(8,128)(2,1)}, u32[]{:S(2)}, u32[]{:S(2)}) collective-permute-start(bf16[256,2048]{1,0:T(8,128)(2,1)S(1)} %copy-done.13), channel_id=1, source_target_pairs={{8,0},{16,8},{24,16},{28,24},{20,28},{12,20},{4,12},{0,4},{9,1},{1... | collective-permute-start | bytes 3145736 | tf_op jit(solution)/shard_map/ppermute | solution.py:85
  178.1 36.2 %collective-permute-start.19 = (bf16[256,2048]{1,0:T(8,128)(2,1)S(1)}, bf16[256,2048]{1,0:T(8,128)(2,1)}, u32[]{:S(2)}, u32[]{:S(2)}) collective-permute-start(bf16[256,2048]{1,0:T(8,128)(2,1)S(1)} %copy-done.13), channel_id=1, source_target_pairs={{0,8},{8,16},{16,24},{24,28},{28,20},{20,12},{12,4},{4,0},{1,9},{9... | collective-permute-start | bytes 3145736 | tf_op jit(solution)/shard_map/ppermute | solution.py:86
  214.4 26.2 %collective-permute-start.24 = (bf16[2048,256]{1,0:T(8,128)(2,1)}, bf16[2048,256]{1,0:T(8,128)(2,1)S(1)}, u32[]{:S(2)}, u32[]{:S(2)}) collective-permute-start(bf16[2048,256]{1,0:T(8,128)(2,1)} %collective-permute-done.20.refs_2_), channel_id=1, source_target_pairs={{8,0},{16,8},{24,16},{28,24},{20,28},{12,20},{4,12},{0,4},{9,1},{1... | collective-permute-start | bytes 3145736 | tf_op jit(solution)/shard_map/ppermute | solution.py:85
  215.0 26.2 %collective-permute-start.25 = (bf16[2048,256]{1,0:T(8,128)(2,1)}, bf16[2048,256]{1,0:T(8,128)(2,1)S(1)}, u32[]{:S(2)}, u32[]{:S(2)}) collective-permute-start(bf16[2048,256]{1,0:T(8,128)(2,1)} %collective-permute-done.21.refs_6_), channel_id=1, source_target_pairs={{0,8},{8,16},{16,24},{24,28},{28,20},{20,12},{12,4},{4,0},{1,9},{9... | collective-permute-start | bytes 3145736 | tf_op jit(solution)/shard_map/ppermute | solution.py:86
  221.1 25.3 %collective-permute-start.27 = (bf16[256,2048]{1,0:T(8,128)(2,1)S(1)}, bf16[256,2048]{1,0:T(8,128)(2,1)S(1)}, u32[]{:S(2)}, u32[]{:S(2)}) collective-permute-start(bf16[256,2048]{1,0:T(8,128)(2,1)S(1)} %add_convert_fusion.4), channel_id=1, source_target_pairs={{0,2},{1,3},{2,0},{3,1},{4,6},{5,7},{6,4},{7,5},{8,10},{9,11},{10,... | collective-permute-start | bytes 3145736 | tf_op jit(solution)/shard_map/ppermute | solution.py:174
  222.7 39.9 %collective-permute-start.22 = (bf16[256,2048]{1,0:T(8,128)(2,1)}, bf16[256,2048]{1,0:T(8,128)(2,1)S(1)}, u32[]{:S(2)}, u32[]{:S(2)}) collective-permute-start(bf16[256,2048]{1,0:T(8,128)(2,1)} %collective-permute-done.18.refs_4_.refs_1_), channel_id=1, source_target_pairs={{8,0},{16,8},{24,16},{28,24},{20,28},{12,20},{4,12},{0,4},{9,1},{1... | collective-permute-start | bytes 3145736 | tf_op jit(solution)/shard_map/ppermute | solution.py:85
  223.3 39.7 %collective-permute-start.23 = (bf16[256,2048]{1,0:T(8,128)(2,1)}, bf16[256,2048]{1,0:T(8,128)(2,1)S(1)}, u32[]{:S(2)}, u32[]{:S(2)}) collective-permute-start(bf16[256,2048]{1,0:T(8,128)(2,1)} %collective-permute-done.19.refs_10_.refs_7_), channel_id=1, source_target_pairs={{0,8},{8,16},{16,24},{24,28},{28,20},{20,12},{12,4},{4,0},{1,9},{9... | collective-permute-start | bytes 3145736 | tf_op jit(solution)/shard_map/ppermute | solution.py:86
  263.0 24.5 %collective-permute-start.28 = (bf16[256,2048]{1,0:T(8,128)(2,1)S(1)}, bf16[256,2048]{1,0:T(8,128)(2,1)S(1)}, u32[]{:S(2)}, u32[]{:S(2)}) collective-permute-start(bf16[256,2048]{1,0:T(8,128)(2,1)S(1)} %collective-permute-done.22.refs_5_.refs_2_), channel_id=1, source_target_pairs={{8,0},{16,8},{24,16},{28,24},{20,28},{12,20},{4,12},{0,4},{9,1},{1... | collective-permute-start | bytes 3145736 | tf_op jit(solution)/shard_map/ppermute | solution.py:85
  263.7 24.2 %collective-permute-start.29 = (bf16[256,2048]{1,0:T(8,128)(2,1)S(1)}, bf16[256,2048]{1,0:T(8,128)(2,1)S(1)}, u32[]{:S(2)}, u32[]{:S(2)}) collective-permute-start(bf16[256,2048]{1,0:T(8,128)(2,1)S(1)} %collective-permute-done.23.refs_9_.refs_6_), channel_id=1, source_target_pairs={{0,8},{8,16},{16,24},{24,28},{28,20},{20,12},{12,4},{4,0},{1,9},{9... | collective-permute-start | bytes 3145736 | tf_op jit(solution)/shard_map/ppermute | solution.py:86
  265.0 24.1 %collective-permute-start.30 = (bf16[256,2048]{1,0:T(8,128)(2,1)}, bf16[256,2048]{1,0:T(8,128)(2,1)S(1)}, u32[]{:S(2)}, u32[]{:S(2)}) collective-permute-start(bf16[256,2048]{1,0:T(8,128)(2,1)} %get-tuple-element.848.refs_0_), channel_id=1, source_target_pairs={{0,2},{1,3},{2,0},{3,1},{4,6},{5,7},{6,4},{7,5},{8,10},{9,11},{10,... | collective-permute-start | bytes 3145736 | tf_op jit(solution)/shard_map/ppermute | solution.py:178
  292.3 32.1 %collective-permute-start.35 = (bf16[512,2048]{1,0:T(8,128)(2,1)}, bf16[512,2048]{1,0:T(8,128)(2,1)}, u32[]{:S(2)}, u32[]{:S(2)}) collective-permute-start(bf16[512,2048]{1,0:T(8,128)(2,1)} %pad_maximum_fusion.1), channel_id=1, source_target_pairs={{0,1},{1,0},{2,3},{3,2},{4,5},{5,4},{6,7},{7,6},{8,9},{9,8},{10,11... | collective-permute-start | bytes 6291464 | tf_op jit(solution)/shard_map/ppermute | solution.py:184
  292.4 14.8 %collective-permute-start.33 = (bf16[1024,256]{1,0:T(8,128)(2,1)S(1)}, bf16[1024,256]{1,0:T(8,128)(2,1)S(1)}, u32[]{:S(2)}, u32[]{:S(2)}) collective-permute-start(bf16[1024,256]{1,0:T(8,128)(2,1)S(1)} %slice.249), channel_id=1, source_target_pairs={{8,0},{16,8},{24,16},{28,24},{20,28},{12,20},{4,12},{0,4},{9,1},{1... | collective-permute-start | bytes 1572872 | tf_op jit(solution)/shard_map/ppermute | solution.py:85
  293.2 14.8 %collective-permute-start.34 = (bf16[1024,256]{1,0:T(8,128)(2,1)S(1)}, bf16[1024,256]{1,0:T(8,128)(2,1)S(1)}, u32[]{:S(2)}, u32[]{:S(2)}) collective-permute-start(bf16[1024,256]{1,0:T(8,128)(2,1)S(1)} %slice.250), channel_id=1, source_target_pairs={{0,8},{8,16},{16,24},{24,28},{28,20},{20,12},{12,4},{4,0},{1,9},{9... | collective-permute-start | bytes 1572872 | tf_op jit(solution)/shard_map/ppermute | solution.py:86
  294.6 29.8 %collective-permute-start.31 = (bf16[128,2048]{1,0:T(8,128)(2,1)S(1)}, bf16[128,2048]{1,0:T(8,128)(2,1)S(1)}, u32[]{:S(2)}, u32[]{:S(2)}) collective-permute-start(bf16[128,2048]{1,0:T(8,128)(2,1)S(1)} %slice.247), channel_id=1, source_target_pairs={{8,0},{16,8},{24,16},{28,24},{20,28},{12,20},{4,12},{0,4},{9,1},{1... | collective-permute-start | bytes 1572872 | tf_op jit(solution)/shard_map/ppermute | solution.py:85
  295.4 29.0 %collective-permute-start.32 = (bf16[128,2048]{1,0:T(8,128)(2,1)S(1)}, bf16[128,2048]{1,0:T(8,128)(2,1)S(1)}, u32[]{:S(2)}, u32[]{:S(2)}) collective-permute-start(bf16[128,2048]{1,0:T(8,128)(2,1)S(1)} %slice.248), channel_id=1, source_target_pairs={{0,8},{8,16},{16,24},{24,28},{28,20},{20,12},{12,4},{4,0},{1,9},{9... | collective-permute-start | bytes 1572872 | tf_op jit(solution)/shard_map/ppermute | solution.py:86
  355.0 23.9 %collective-permute-start.36 = (bf16[256,2048]{1,0:T(8,128)(2,1)}, bf16[256,2048]{1,0:T(8,128)(2,1)S(1)}, u32[]{:S(2)}, u32[]{:S(2)}) collective-permute-start(bf16[256,2048]{1,0:T(8,128)(2,1)} %get-tuple-element.856), channel_id=1, source_target_pairs={{0,8},{8,16},{16,24},{24,28},{28,20},{20,12},{12,4},{4,0},{1,9},{9... | collective-permute-start | bytes 3145736 | tf_op jit(solution)/shard_map/ppermute | solution.py:117
  356.3 23.8 %collective-permute-start.37 = (bf16[256,2048]{1,0:T(8,128)(2,1)}, bf16[256,2048]{1,0:T(8,128)(2,1)S(1)}, u32[]{:S(2)}, u32[]{:S(2)}) collective-permute-start(bf16[256,2048]{1,0:T(8,128)(2,1)} %get-tuple-element.857), channel_id=1, source_target_pairs={{8,0},{16,8},{24,16},{28,24},{20,28},{12,20},{4,12},{0,4},{9,1},{1... | collective-permute-start | bytes 3145736 | tf_op jit(solution)/shard_map/ppermute | solution.py:118
  387.9 25.4 %collective-permute-start.41 = (bf16[256,2048]{1,0:T(8,128)(2,1)}, bf16[256,2048]{1,0:T(8,128)(2,1)S(1)}, u32[]{:S(2)}, u32[]{:S(2)}) collective-permute-start(bf16[256,2048]{1,0:T(8,128)(2,1)} %add_convert_fusion.3), channel_id=1, source_target_pairs={{0,2},{1,3},{2,0},{3,1},{4,6},{5,7},{6,4},{7,5},{8,10},{9,11},{10,... | collective-permute-start | bytes 3145736 | tf_op jit(solution)/shard_map/ppermute | solution.py:174
  401.5 47.6 %collective-permute-start.39 = (bf16[512,2048]{1,0:T(8,128)(2,1)}, bf16[512,2048]{1,0:T(8,128)(2,1)S(1)}, u32[]{:S(2)}, u32[]{:S(2)}) collective-permute-start(bf16[512,2048]{1,0:T(8,128)(2,1)} %get-tuple-element.902), channel_id=1, source_target_pairs={{0,8},{8,16},{16,24},{24,28},{28,20},{20,12},{12,4},{4,0},{1,9},{9... | collective-permute-start | bytes 6291464 | tf_op jit(solution)/shard_map/ppermute | solution.py:117
  402.9 47.5 %collective-permute-start.40 = (bf16[512,2048]{1,0:T(8,128)(2,1)}, bf16[512,2048]{1,0:T(8,128)(2,1)S(1)}, u32[]{:S(2)}, u32[]{:S(2)}) collective-permute-start(bf16[512,2048]{1,0:T(8,128)(2,1)} %get-tuple-element.903), channel_id=1, source_target_pairs={{8,0},{16,8},{24,16},{28,24},{20,28},{12,20},{4,12},{0,4},{9,1},{1... | collective-permute-start | bytes 6291464 | tf_op jit(solution)/shard_map/ppermute | solution.py:118
  420.9 29.5 %collective-permute-start.42 = (bf16[256,2048]{1,0:T(8,128)(2,1)}, bf16[256,2048]{1,0:T(8,128)(2,1)S(1)}, u32[]{:S(2)}, u32[]{:S(2)}) collective-permute-start(bf16[256,2048]{1,0:T(8,128)(2,1)} %get-tuple-element.982.refs_0_), channel_id=1, source_target_pairs={{0,2},{1,3},{2,0},{3,1},{4,6},{5,7},{6,4},{7,5},{8,10},{9,11},{10,... | collective-permute-start | bytes 3145736 | tf_op jit(solution)/shard_map/ppermute | solution.py:178
  452.2 13.7 %collective-permute-start.44 = (bf16[512,2048]{1,0:T(8,128)(2,1)}, bf16[512,2048]{1,0:T(8,128)(2,1)}, u32[]{:S(2)}, u32[]{:S(2)}) collective-permute-start(bf16[512,2048]{1,0:T(8,128)(2,1)} %pad_maximum_fusion.2), channel_id=1, source_target_pairs={{0,1},{1,0},{2,3},{3,2},{4,5},{5,4},{6,7},{7,6},{8,9},{9,8},{10,11... | collective-permute-start | bytes 6291464 | tf_op jit(solution)/shard_map/ppermute | solution.py:184
  482.9 38.3 %collective-permute-start.45 = (bf16[256,2048]{1,0:T(8,128)(2,1)}, bf16[256,2048]{1,0:T(8,128)(2,1)S(1)}, u32[]{:S(2)}, u32[]{:S(2)}) collective-permute-start(bf16[256,2048]{1,0:T(8,128)(2,1)} %add_convert_fusion.2), channel_id=1, source_target_pairs={{0,2},{1,3},{2,0},{3,1},{4,6},{5,7},{6,4},{7,5},{8,10},{9,11},{10,... | collective-permute-start | bytes 3145736 | tf_op jit(solution)/shard_map/ppermute | solution.py:174
  483.5 63.9 %collective-permute-start.50 = (bf16[512,2048]{1,0:T(8,128)(2,1)}, bf16[512,2048]{1,0:T(8,128)(2,1)}, u32[]{:S(2)}, u32[]{:S(2)}) collective-permute-start(bf16[512,2048]{1,0:T(8,128)(2,1)} %get-tuple-element.1060), channel_id=1, source_target_pairs={{0,8},{8,16},{16,24},{24,28},{28,20},{20,12},{12,4},{4,0},{1,9},{9... | collective-permute-start | bytes 6291464 | tf_op jit(solution)/shard_map/ppermute | solution.py:117
  484.6 62.8 %collective-permute-start.51 = (bf16[512,2048]{1,0:T(8,128)(2,1)}, bf16[512,2048]{1,0:T(8,128)(2,1)}, u32[]{:S(2)}, u32[]{:S(2)}) collective-permute-start(bf16[512,2048]{1,0:T(8,128)(2,1)} %get-tuple-element.1061), channel_id=1, source_target_pairs={{8,0},{16,8},{24,16},{28,24},{20,28},{12,20},{4,12},{0,4},{9,1},{1... | collective-permute-start | bytes 6291464 | tf_op jit(solution)/shard_map/ppermute | solution.py:118
  522.8 16.6 %collective-permute-start.46 = (bf16[384,512]{1,0:T(8,128)(2,1)S(1)}, bf16[384,512]{1,0:T(8,128)(2,1)S(1)}, u32[]{:S(2)}, u32[]{:S(2)}) collective-permute-start(bf16[384,512]{1,0:T(8,128)(2,1)S(1)} %get-tuple-element.1368), channel_id=1, source_target_pairs={{0,8},{8,16},{16,24},{24,28},{28,20},{20,12},{12,4},{4,0},{1,9},{9... | collective-permute-start | bytes 1179656 | tf_op jit(solution)/shard_map/ppermute | solution.py:117
  524.0 16.5 %collective-permute-start.47 = (bf16[384,512]{1,0:T(8,128)(2,1)S(1)}, bf16[384,512]{1,0:T(8,128)(2,1)S(1)}, u32[]{:S(2)}, u32[]{:S(2)}) collective-permute-start(bf16[384,512]{1,0:T(8,128)(2,1)S(1)} %get-tuple-element.1367), channel_id=1, source_target_pairs={{8,0},{16,8},{24,16},{28,24},{20,28},{12,20},{4,12},{0,4},{9,1},{1... | collective-permute-start | bytes 1179656 | tf_op jit(solution)/shard_map/ppermute | solution.py:118
  526.8 33.7 %collective-permute-start.52 = (bf16[256,2048]{1,0:T(8,128)(2,1)S(1)}, bf16[256,2048]{1,0:T(8,128)(2,1)}, u32[]{:S(2)}, u32[]{:S(2)}) collective-permute-start(bf16[256,2048]{1,0:T(8,128)(2,1)S(1)} %add_convert_fusion.1.refs_0_), channel_id=1, source_target_pairs={{0,2},{1,3},{2,0},{3,1},{4,6},{5,7},{6,4},{7,5},{8,10},{9,11},{10,... | collective-permute-start | bytes 3145736 | tf_op jit(solution)/shard_map/ppermute | solution.py:178
  544.9 18.3 %collective-permute-start.48 = (bf16[768,512]{1,0:T(8,128)(2,1)}, bf16[768,512]{1,0:T(8,128)(2,1)S(1)}, u32[]{:S(2)}, u32[]{:S(2)}) collective-permute-start(bf16[768,512]{1,0:T(8,128)(2,1)} %pad_maximum_fusion.6), channel_id=1, source_target_pairs={{0,8},{8,16},{16,24},{24,28},{28,20},{20,12},{12,4},{4,0},{1,9},{9... | collective-permute-start | bytes 2359304 | tf_op jit(solution)/shard_map/ppermute | solution.py:117
  545.6 18.5 %collective-permute-start.49 = (bf16[768,512]{1,0:T(8,128)(2,1)}, bf16[768,512]{1,0:T(8,128)(2,1)}, u32[]{:S(2)}, u32[]{:S(2)}) collective-permute-start(bf16[768,512]{1,0:T(8,128)(2,1)} %pad_maximum_fusion.5), channel_id=1, source_target_pairs={{8,0},{16,8},{24,16},{28,24},{20,28},{12,20},{4,12},{0,4},{9,1},{1... | collective-permute-start | bytes 2359304 | tf_op jit(solution)/shard_map/ppermute | solution.py:118
  567.1 20.2 %collective-permute-start.55 = (bf16[512,2048]{1,0:T(8,128)(2,1)S(1)}, bf16[512,2048]{1,0:T(8,128)(2,1)}, u32[]{:S(2)}, u32[]{:S(2)}) collective-permute-start(bf16[512,2048]{1,0:T(8,128)(2,1)S(1)} %pad_maximum_fusion.3), channel_id=1, source_target_pairs={{0,1},{1,0},{2,3},{3,2},{4,5},{5,4},{6,7},{7,6},{8,9},{9,8},{10,11... | collective-permute-start | bytes 6291464 | tf_op jit(solution)/shard_map/ppermute | solution.py:184
  567.2 19.9 %collective-permute-start.53 = (bf16[768,512]{1,0:T(8,128)(2,1)S(1)}, bf16[768,512]{1,0:T(8,128)(2,1)S(1)}, u32[]{:S(2)}, u32[]{:S(2)}) collective-permute-start(bf16[768,512]{1,0:T(8,128)(2,1)S(1)} %get-tuple-element.1109), channel_id=1, source_target_pairs={{0,8},{8,16},{16,24},{24,28},{28,20},{20,12},{12,4},{4,0},{1,9},{9... | collective-permute-start | bytes 2359304 | tf_op jit(solution)/shard_map/ppermute | solution.py:117
  567.7 19.6 %collective-permute-start.54 = (bf16[768,512]{1,0:T(8,128)(2,1)S(1)}, bf16[768,512]{1,0:T(8,128)(2,1)S(1)}, u32[]{:S(2)}, u32[]{:S(2)}) collective-permute-start(bf16[768,512]{1,0:T(8,128)(2,1)S(1)} %get-tuple-element.1110), channel_id=1, source_target_pairs={{8,0},{16,8},{24,16},{28,24},{20,28},{12,20},{4,12},{0,4},{9,1},{1... | collective-permute-start | bytes 2359304 | tf_op jit(solution)/shard_map/ppermute | solution.py:118
  587.7 19.1 %collective-permute-start.56 = (bf16[768,512]{1,0:T(8,128)(2,1)S(1)}, bf16[768,512]{1,0:T(8,128)(2,1)}, u32[]{:S(2)}, u32[]{:S(2)}) collective-permute-start(bf16[768,512]{1,0:T(8,128)(2,1)S(1)} %get-tuple-element.1146), channel_id=1, source_target_pairs={{0,8},{8,16},{16,24},{24,28},{28,20},{20,12},{12,4},{4,0},{1,9},{9... | collective-permute-start | bytes 2359304 | tf_op jit(solution)/shard_map/ppermute | solution.py:117
  588.4 18.6 %collective-permute-start.57 = (bf16[768,512]{1,0:T(8,128)(2,1)S(1)}, bf16[768,512]{1,0:T(8,128)(2,1)}, u32[]{:S(2)}, u32[]{:S(2)}) collective-permute-start(bf16[768,512]{1,0:T(8,128)(2,1)S(1)} %get-tuple-element.1147), channel_id=1, source_target_pairs={{8,0},{16,8},{24,16},{28,24},{20,28},{12,20},{4,12},{0,4},{9,1},{1... | collective-permute-start | bytes 2359304 | tf_op jit(solution)/shard_map/ppermute | solution.py:118
  615.2 15.0 %collective-permute-start.58 = (bf16[128,1536]{1,0:T(8,128)(2,1)}, bf16[128,1536]{1,0:T(8,128)(2,1)S(1)}, u32[]{:S(2)}, u32[]{:S(2)}) collective-permute-start(bf16[128,1536]{1,0:T(8,128)(2,1)} %get-tuple-element.1373), channel_id=1, source_target_pairs={{0,8},{8,16},{16,24},{24,28},{28,20},{20,12},{12,4},{4,0},{1,9},{9... | collective-permute-start | bytes 1179656 | tf_op jit(solution)/shard_map/ppermute | solution.py:117
  616.4 13.8 %collective-permute-start.59 = (bf16[128,1536]{1,0:T(8,128)(2,1)}, bf16[128,1536]{1,0:T(8,128)(2,1)S(1)}, u32[]{:S(2)}, u32[]{:S(2)}) collective-permute-start(bf16[128,1536]{1,0:T(8,128)(2,1)} %get-tuple-element.1372), channel_id=1, source_target_pairs={{8,0},{16,8},{24,16},{28,24},{20,28},{12,20},{4,12},{0,4},{9,1},{1... | collective-permute-start | bytes 1179656 | tf_op jit(solution)/shard_map/ppermute | solution.py:118
  633.9 20.4 %collective-permute-start.60 = (bf16[256,1536]{1,0:T(8,128)(2,1)S(1)}, bf16[256,1536]{1,0:T(8,128)(2,1)S(1)}, u32[]{:S(2)}, u32[]{:S(2)}) collective-permute-start(bf16[256,1536]{1,0:T(8,128)(2,1)S(1)} %pad_maximum_fusion.8), channel_id=1, source_target_pairs={{0,8},{8,16},{16,24},{24,28},{28,20},{20,12},{12,4},{4,0},{1,9},{9... | collective-permute-start | bytes 2359304 | tf_op jit(solution)/shard_map/ppermute | solution.py:117
  635.2 20.4 %collective-permute-start.61 = (bf16[256,1536]{1,0:T(8,128)(2,1)S(1)}, bf16[256,1536]{1,0:T(8,128)(2,1)S(1)}, u32[]{:S(2)}, u32[]{:S(2)}) collective-permute-start(bf16[256,1536]{1,0:T(8,128)(2,1)S(1)} %pad_maximum_fusion.7), channel_id=1, source_target_pairs={{8,0},{16,8},{24,16},{28,24},{20,28},{12,20},{4,12},{0,4},{9,1},{1... | collective-permute-start | bytes 2359304 | tf_op jit(solution)/shard_map/ppermute | solution.py:118
  636.0 86.9 %collective-permute-start.68 = (bf16[512,2048]{1,0:T(8,128)(2,1)}, bf16[512,2048]{1,0:T(8,128)(2,1)}, u32[]{:S(2)}, u32[]{:S(2)}) collective-permute-start(bf16[512,2048]{1,0:T(8,128)(2,1)} %get-tuple-element.1295), channel_id=1, source_target_pairs={{0,8},{8,16},{16,24},{24,28},{28,20},{20,12},{12,4},{4,0},{1,9},{9... | collective-permute-start | bytes 6291464 | tf_op jit(solution)/shard_map/ppermute | solution.py:117
  637.2 85.7 %collective-permute-start.69 = (bf16[512,2048]{1,0:T(8,128)(2,1)}, bf16[512,2048]{1,0:T(8,128)(2,1)}, u32[]{:S(2)}, u32[]{:S(2)}) collective-permute-start(bf16[512,2048]{1,0:T(8,128)(2,1)} %get-tuple-element.1296), channel_id=1, source_target_pairs={{8,0},{16,8},{24,16},{28,24},{20,28},{12,20},{4,12},{0,4},{9,1},{1... | collective-permute-start | bytes 6291464 | tf_op jit(solution)/shard_map/ppermute | solution.py:118
  638.6 24.6 %collective-permute-start.65 = (bf16[256,2048]{1,0:T(8,128)(2,1)S(1)}, bf16[256,2048]{1,0:T(8,128)(2,1)}, u32[]{:S(2)}, u32[]{:S(2)}) collective-permute-start(bf16[256,2048]{1,0:T(8,128)(2,1)S(1)} %add_convert_fusion), channel_id=1, source_target_pairs={{0,2},{1,3},{2,0},{3,1},{4,6},{5,7},{6,4},{7,5},{8,10},{9,11},{10,... | collective-permute-start | bytes 3145736 | tf_op jit(solution)/shard_map/ppermute | solution.py:174
  659.3 56.5 %collective-permute-start.63 = (bf16[256,1536]{1,0:T(8,128)(2,1)}, bf16[256,1536]{1,0:T(8,128)(2,1)}, u32[]{:S(2)}, u32[]{:S(2)}) collective-permute-start(bf16[256,1536]{1,0:T(8,128)(2,1)} %fusion.2), channel_id=1, source_target_pairs={{0,8},{8,16},{16,24},{24,28},{28,20},{20,12},{12,4},{4,0},{1,9},{9... | collective-permute-start | bytes 2359304 | tf_op jit(solution)/shard_map/ppermute | solution.py:117
  660.8 56.0 %collective-permute-start.64 = (bf16[256,1536]{1,0:T(8,128)(2,1)}, bf16[256,1536]{1,0:T(8,128)(2,1)}, u32[]{:S(2)}, u32[]{:S(2)}) collective-permute-start(bf16[256,1536]{1,0:T(8,128)(2,1)} %fusion.1), channel_id=1, source_target_pairs={{8,0},{16,8},{24,16},{28,24},{20,28},{12,20},{4,12},{0,4},{9,1},{1... | collective-permute-start | bytes 2359304 | tf_op jit(solution)/shard_map/ppermute | solution.py:118
  669.3 53.6 %collective-permute-start.70 = (bf16[256,2048]{1,0:T(8,128)(2,1)}, bf16[256,2048]{1,0:T(8,128)(2,1)S(1)}, u32[]{:S(2)}, u32[]{:S(2)}) collective-permute-start(bf16[256,2048]{1,0:T(8,128)(2,1)} %get-tuple-element.1325.refs_0_), channel_id=1, source_target_pairs={{0,2},{1,3},{2,0},{3,1},{4,6},{5,7},{6,4},{7,5},{8,10},{9,11},{10,... | collective-permute-start | bytes 3145736 | tf_op jit(solution)/shard_map/ppermute | solution.py:178
  724.6 17.1 %collective-permute-start.71 = (bf16[512,2048]{1,0:T(8,128)(2,1)}, bf16[512,2048]{1,0:T(8,128)(2,1)}, u32[]{:S(2)}, u32[]{:S(2)}) collective-permute-start(bf16[512,2048]{1,0:T(8,128)(2,1)} %pad_maximum_fusion.4), channel_id=1, source_target_pairs={{0,1},{1,0},{2,3},{3,2},{4,5},{5,4},{6,7},{7,6},{8,9},{9,8},{10,11... | collective-permute-start | bytes 6291464 | tf_op jit(solution)/shard_map/ppermute | solution.py:184
  724.8 24.2 %collective-permute-start.66 = (bf16[256,1536]{1,0:T(8,128)(2,1)}, bf16[256,1536]{1,0:T(8,128)(2,1)}, u32[]{:S(2)}, u32[]{:S(2)}) collective-permute-start(bf16[256,1536]{1,0:T(8,128)(2,1)} %fusion.4), channel_id=1, source_target_pairs={{0,8},{8,16},{16,24},{24,28},{28,20},{20,12},{12,4},{4,0},{1,9},{9... | collective-permute-start | bytes 2359304 | tf_op jit(solution)/shard_map/ppermute | solution.py:117
  726.3 22.8 %collective-permute-start.67 = (bf16[256,1536]{1,0:T(8,128)(2,1)}, bf16[256,1536]{1,0:T(8,128)(2,1)}, u32[]{:S(2)}, u32[]{:S(2)}) collective-permute-start(bf16[256,1536]{1,0:T(8,128)(2,1)} %fusion.3), channel_id=1, source_target_pairs={{8,0},{16,8},{24,16},{28,24},{20,28},{12,20},{4,12},{0,4},{9,1},{1... | collective-permute-start | bytes 2359304 | tf_op jit(solution)/shard_map/ppermute | solution.py:118
  (77 other events, 1258.0 us)

commit v3 on v2

--- a/solution.py
+++ b/solution.py
@@ -1086,6 +1086,14 @@
         first = j == self.ring.half - 1
         return self.terms([j, n - j], [[(rising, 0)], [(falling, 1 if first else 0)]], BF)
 
+    def raw(self):
+        return self.terms([self.left, self.ring.count - self.left], [[], []], BF)
+
+    def added(self, raw):
+        return [
+            (term.astype(FP) + got.astype(FP)).astype(BF) for term, got in zip(raw, self.fresh)
+        ]
+
     def advance(self, order):
         order.sums = self.sums(order)
         order.pin()
@@ -1289,10 +1297,13 @@
     o.kept, o.away = rows_matmul(
         o.meta, "down_part", o.both, gather_down.blocks, m, False, (0, None), "nn", 0
     )
+    o.raw = sum_feed.raw()
     o.pin(sum_feed)
     parts = team.send_half(o.out.parts)
     kept, got = o.out.kept, team.cross(o.out.away)
-    sum_feed.advance(o)
+    o.sums = sum_feed.added(o.out.raw)
+    o.pin()
+    sum_feed.send(*o.out.sums)
     o.parts, o.kept, o.got = parts, kept, got
     o.pin()
 
@@ -1310,7 +1321,7 @@
         o.out.d_out_matrix,
     )
     o.terms = [kept, got] + arrived
-    o.pin()
+    o.pin(sum_feed)
 
     def part_kv(b):
         return o.d_send[b].astype(FP)

time: 804 us -> 790 us (0.983)
  waiting for transfers between devices: 331 us -> 312 us
    ppermute x12, waiting for transfers between devices: 119 us -> 100 us  [send(): lax.ppermute(rising, 'seq', self.ring.up)]
  transfers between devices with their start and end apart: 77 -> 77, of which waited for: 55 -> 54; matrix products, arithmetic and copies ran while one was open for 4% -> 6% of each run, Pallas kernels for 29% -> 30%
where the time goes in v3:
time: 790 us; the launch traced here: 782 us
  waiting for transfers between devices  312 us (39%)
  Pallas kernels  294 us (37%)
  starting transfers between devices  77.4 us (10%)
  other arithmetic  40.2 us (5%)
  local copies, waits for them, and re-layouts  27.3 us (3%)
  matrix products  23.6 us (3%)
    pallas_call x24, Pallas kernels, call(): pl.pallas_call(body, grid_spec=pltpu.PrefetchScalarGridSpec(num_scalar_pr...  274 us
    ppermute x16, waiting for transfers between devices, advance(): lax.ppermute(upper, 'seq', ring.down)  156 us
    ppermute x12, waiting for transfers between devices, send(): lax.ppermute(rising, 'seq', self.ring.up)  100 us
    pallas_call x1, Pallas kernels, update_matrices(): pl.pallas_call(body, grid=(steps,), in_specs=[pl.BlockSpec(memory_space=p...  19.9 us
    ppermute x16, starting transfers between devices, advance(): lax.ppermute(lower, 'seq', ring.up)  18.4 us
    dot_general x8, matrix products, part_inward(): jnp.einsum('td,tn->dn', column_block(o.normed_one, b), o.d_projected, pre...  17.3 us
    ppermute x4, waiting for transfers between devices, send_sums(): arrived.append(lax.ppermute(term.astype(BF), 'head', self.shift(k)))  16 us
    ppermute x16, starting transfers between devices, advance(): lax.ppermute(upper, 'seq', ring.down)  15.9 us
  transfers between devices with their start and end apart: 77, of which 54 were waited for; matrix products, arithmetic and copies ran while one was open for 6% of the time, Pallas kernels for 30%

profile of v3, /device:TPU:0, one launch (start us, length us, event | category | flops | bytes accessed | tf_op | source)
XLA Modules:
  0.0 782.1 jit_solution(12403293544117855834)
XLA Ops:
  2.3 3.0 collective-permute-start
  8.8 5.9 mask_cotangent.1.x_ref.grad_ref.refs_4_
  18.6 5.0 collective-permute-done.refs_1_
  27.0 16.9 %collective-permute-done.2.refs_2_ = bf16[800,512]{1,0:T(8,128)(2,1)} collective-permute-done((bf16[800,512]{1,0:T(8,128)(2,1)S(1)}, bf16[800,512]{1,0:T(8,128)(2,1)}, u32[]{:S(2)}, u32[]{:S(2)}) %collective-permute-start.2) | collective-permute-done | bytes 819232 | tf_op jit(solution)/shard_map/ppermute | solution.py:85
  47.3 15.7 %collective-permute-done.4.refs_3_ = bf16[800,512]{1,0:T(8,128)(2,1)S(1)} collective-permute-done((bf16[800,512]{1,0:T(8,128)(2,1)}, bf16[800,512]{1,0:T(8,128)(2,1)S(1)}, u32[]{:S(2)}, u32[]{:S(2)}) %collective-permute-start.4) | collective-permute-done | bytes 819232 | tf_op jit(solution)/shard_map/ppermute | solution.py:85
  68.8 4.6 collective-permute-done.6
  79.4 4.1 first_norm.2
  83.5 5.8 project_prefix.1.refs_0_.refs_8_.refs_3_
  93.4 8.2 %first_norm.3 = (bf16[1024,2048]{1,0:T(8,128)(2,1)}, bf16[1024,2048]{1,0:T(8,128)(2,1)}) custom-call(s32[15]{0:T(128)} %concatenate.57.meta_ref, bf16[1024,2048]{1,0:T(8,128)(2,1)} %in_ref.5, f32[2,2048]{1,0:T(2,128)} %bitcast.96), custom_call_target="tpu_custom_call" | custom-call | flops 1 | bytes 1 | tf_op jit(solution)/shard_map/first_norm/pallas_call | solution.py:234
  101.5 8.4 %collective-permute-done.8.refs_1_.refs_9_.refs_4_ = bf16[768,512]{1,0:T(8,128)(2,1)S(1)} collective-permute-done((bf16[768,512]{1,0:T(8,128)(2,1)}, bf16[768,512]{1,0:T(8,128)(2,1)S(1)}, u32[]{:S(2)}, u32[]{:S(2)}) %collective-permute-start.8) | collective-permute-done | bytes 786464 | tf_op jit(solution)/shard_map/ppermute | solution.py:85
  112.8 12.7 %project.1.q_ref.k_ref.v_ref = bf16[3,1024,512]{2,1,0:T(8,128)(2,1)} custom-call(s32[15]{0:T(128)} %concatenate.57.meta_ref, bf16[1024,2048]{1,0:T(8,128)(2,1)} %get-tuple-element.1342.x_ref, bf16[800,512]{1,0:T(8,128)(2,1)} %copy-done.8, bf16[800,512]{1,0:T(8,128)(2,1)} %copy-done.18, bf16[800,512]{1,0:T(8,128)(2,1)} %collective-permute-done.2.refs_2_, ...), custom_call_target="tpu_custom_call" | custom-call | flops 1 | bytes 1 | tf_op jit(solution)/shard_map/project/pallas_call | solution.py:234
  125.5 7.0 collective-permute-done.12.refs_1_
  133.3 12.8 %collective-permute-done.10.refs_2_.refs_10_.refs_5_ = bf16[768,512]{1,0:T(8,128)(2,1)S(1)} collective-permute-done((bf16[768,512]{1,0:T(8,128)(2,1)S(1)}, bf16[768,512]{1,0:T(8,128)(2,1)S(1)}, u32[]{:S(2)}, u32[]{:S(2)}) %collective-permute-start.10) | collective-permute-done | bytes 786464 | tf_op jit(solution)/shard_map/ppermute | solution.py:85
  148.8 14.9 %collective-permute-done.14.refs_3_.refs_11_.refs_6_ = bf16[768,512]{1,0:T(8,128)(2,1)S(1)} collective-permute-done((bf16[768,512]{1,0:T(8,128)(2,1)S(1)}, bf16[768,512]{1,0:T(8,128)(2,1)S(1)}, u32[]{:S(2)}, u32[]{:S(2)}) %collective-permute-start.14) | collective-permute-done | bytes 786464 | tf_op jit(solution)/shard_map/ppermute | solution.py:85
  168.8 7.9 %collective-permute-done.16 = bf16[384,512]{1,0:T(8,128)(2,1)S(1)} collective-permute-done((bf16[384,512]{1,0:T(8,128)(2,1)S(1)}, bf16[384,512]{1,0:T(8,128)(2,1)S(1)}, u32[]{:S(2)}, u32[]{:S(2)}) %collective-permute-start.16) | collective-permute-done | bytes 393248 | tf_op jit(solution)/shard_map/ppermute | solution.py:85
  180.5 20.8 %attention_forward.1 = (bf16[1024,512]{1,0:T(8,128)(2,1)}, f32[4,1024,1]{2,1,0:T(8,128)}) custom-call(s32[15]{0:T(128)} %concatenate.57.meta_ref, bf16[3,1024,512]{2,1,0:T(8,128)(2,1)} %project.1.q_ref.k_ref.v_ref, bf16[3,1024,512]{2,1,0:T(8,128)(2,1)} %project.1.q_ref.k_ref.v_ref, bf16[3,1024,512]{2,1,0:T(8,128)(2,1)} %project.1.q_ref.k_ref.v_ref, ...), custom_call_target="tpu_custom_call" | custom-call | flops 1 | bytes 1 | tf_op jit(solution)/shard_map/attention_forward/pallas_call | solution.py:234
  201.4 6.5 out_part.1
  207.9 5.8 collective-permute-done.18.refs_4_.refs_1_
  218.7 2.4 add_convert_fusion.6
  224.7 15.8 %collective-permute-done.24.refs_3_ = bf16[2048,256]{1,0:T(8,128)(2,1)S(1)} collective-permute-done((bf16[2048,256]{1,0:T(8,128)(2,1)}, bf16[2048,256]{1,0:T(8,128)(2,1)S(1)}, u32[]{:S(2)}, u32[]{:S(2)}) %collective-permute-start.24) | collective-permute-done | bytes 1048608 | tf_op jit(solution)/shard_map/ppermute | solution.py:85
  241.3 5.1 collective-permute-done.27.refs_2_
  247.4 5.5 second_norm.1
  252.8 9.8 %collective-permute-done.22.refs_5_.refs_2_ = bf16[256,2048]{1,0:T(8,128)(2,1)S(1)} collective-permute-done((bf16[256,2048]{1,0:T(8,128)(2,1)}, bf16[256,2048]{1,0:T(8,128)(2,1)S(1)}, u32[]{:S(2)}, u32[]{:S(2)}) %collective-permute-start.22) | collective-permute-done | bytes 1048608 | tf_op jit(solution)/shard_map/ppermute | solution.py:85
  266.6 21.0 %collective-permute-done.28.refs_6_.refs_3_ = bf16[256,2048]{1,0:T(8,128)(2,1)S(1)} collective-permute-done((bf16[256,2048]{1,0:T(8,128)(2,1)S(1)}, bf16[256,2048]{1,0:T(8,128)(2,1)S(1)}, u32[]{:S(2)}, u32[]{:S(2)}) %collective-permute-start.28) | collective-permute-done | bytes 1048608 | tf_op jit(solution)/shard_map/ppermute | solution.py:85
  289.2 3.2 pad_maximum_fusion.1
  297.0 10.2 %collective-permute-done.33 = bf16[1024,256]{1,0:T(8,128)(2,1)S(1)} collective-permute-done((bf16[1024,256]{1,0:T(8,128)(2,1)S(1)}, bf16[1024,256]{1,0:T(8,128)(2,1)S(1)}, u32[]{:S(2)}, u32[]{:S(2)}) %collective-permute-start.33) | collective-permute-done | bytes 524320 | tf_op jit(solution)/shard_map/ppermute | solution.py:85
  309.1 15.3 %feed_back.1.refs_11_ = bf16[1024,2048]{1,0:T(8,128)(2,1)} custom-call(s32[15]{0:T(128)} %concatenate.57.meta_ref, bf16[1024,2048]{1,0:T(8,128)(2,1)} %mask_cotangent.1.x_ref.grad_ref.refs_4_, bf16[2048,256]{1,0:T(8,128)(2,1)} %convert_element_type.221.refs_0_, bf16[2048,256]{1,0:T(8,128)(2,1)} %copy-done.32, ...), custom_call_target="tpu_custom_call" | custom-call | flops 1 | bytes 1 | tf_op jit(solution)/shard_map/feed_back/pallas_call | solution.py:234
  325.5 22.4 %feed_up.1 = (bf16[1024,2048]{1,0:T(8,128)(2,1)}, bf16[2,1024,2048]{2,1,0:T(8,128)(2,1)}) custom-call(s32[15]{0:T(128)} %concatenate.57.meta_ref, bf16[256,2048]{1,0:T(8,128)(2,1)} %get-tuple-element.852.refs_0_, bf16[256,2048]{1,0:T(8,128)(2,1)} %copy-done.39, bf16[512,2048]{1,0:T(8,128)(2,1)} %collective-permute-done.35.refs_2_, ...), custom_call_target="tpu_custom_call" | custom-call | flops 1 | bytes 1 | tf_op jit(solution)/shard_map/feed_up/pallas_call | solution.py:234
  348.0 7.1 feed_terms.5
  357.3 15.5 %up_back.1 = (bf16[512,2048]{1,0:T(8,128)(2,1)}, bf16[512,2048]{1,0:T(8,128)(2,1)}) custom-call(s32[15]{0:T(128)} %concatenate.57.meta_ref, bf16[2,1024,2048]{2,1,0:T(8,128)(2,1)} %get-tuple-element.1327.both_ref.x_any, bf16[256,2048]{1,0:T(8,128)(2,1)} %convert_element_type.224.refs_3_.refs_0_, bf16[256,2048]{1,0:T(8,128)(2,1)} %collective-permute-done.18.refs_4_.refs_1_, ...), custom_call_target="tpu_custom_call" | custom-call | flops 1 | bytes 1 | tf_op jit(solution)/shard_map/up_back/pallas_call | solution.py:234
  372.8 6.2 collective-permute-done.36.refs_0_
  380.3 4.4 collective-permute-done.38.refs_1_
  384.6 3.3 add_convert_fusion.5
  389.5 12.2 %feed_terms.6 = (bf16[512,2048]{1,0:T(8,128)(2,1)}, bf16[512,2048]{1,0:T(8,128)(2,1)}) custom-call(s32[15]{0:T(128)} %concatenate.57.meta_ref, bf16[1024,2048]{1,0:T(8,128)(2,1)} %mask_cotangent.1.x_ref.grad_ref.refs_4_, bf16[1024,2048]{1,0:T(8,128)(2,1)} %get-tuple-element.1322.norm_ref, bf16[2,1024,2048]{2,1,0:T(8,128)(2,1)} %get-tuple-element.1327.both_ref.x_any, ...), custom_call_target="tpu_custom_call" | custom-call | flops 1 | bytes 1 | tf_op jit(solution)/shard_map/feed_terms/pallas_call | solution.py:234
  404.1 9.3 %collective-permute-done.41.refs_2_ = bf16[256,2048]{1,0:T(8,128)(2,1)S(1)} collective-permute-done((bf16[256,2048]{1,0:T(8,128)(2,1)}, bf16[256,2048]{1,0:T(8,128)(2,1)S(1)}, u32[]{:S(2)}, u32[]{:S(2)}) %collective-permute-start.41) | collective-permute-done | bytes 1048608 | tf_op jit(solution)/shard_map/ppermute | solution.py:174
  414.4 6.6 second_norm_back.1
  422.6 15.3 %down_part.1 = (bf16[512,2048]{1,0:T(8,128)(2,1)}, bf16[512,2048]{1,0:T(8,128)(2,1)}) custom-call(s32[15]{0:T(128)} %concatenate.57.meta_ref, bf16[2,1024,2048]{2,1,0:T(8,128)(2,1)} %get-tuple-element.1327.both_ref.x_any, bf16[2048,256]{1,0:T(8,128)(2,1)} %convert_element_type.221.refs_0_, bf16[2048,256]{1,0:T(8,128)(2,1)} %copy-done.32, ...), custom_call_target="tpu_custom_call" | custom-call | flops 1 | bytes 1 | tf_op jit(solution)/shard_map/down_part/pallas_call | solution.py:234
  437.9 11.8 %feed_terms.7 = (bf16[512,2048]{1,0:T(8,128)(2,1)}, bf16[512,2048]{1,0:T(8,128)(2,1)}) custom-call(s32[15]{0:T(128)} %concatenate.57.meta_ref, bf16[1024,2048]{1,0:T(8,128)(2,1)} %mask_cotangent.1.x_ref.grad_ref.refs_4_, bf16[1024,2048]{1,0:T(8,128)(2,1)} %get-tuple-element.1322.norm_ref, bf16[2,1024,2048]{2,1,0:T(8,128)(2,1)} %get-tuple-element.1327.both_ref.x_any), custom_call_target="tpu_custom_call" | custom-call | flops 1 | bytes 1 | tf_op jit(solution)/shard_map/feed_terms/pallas_call | solution.py:234
  461.1 9.4 %mixed_back.1 = (bf16[1024,2048]{1,0:T(8,128)(2,1)}, bf16[1024,512]{1,0:T(8,128)(2,1)}, bf16[1024,512]{1,0:T(8,128)(2,1)}) custom-call(s32[15]{0:T(128)} %concatenate.57.meta_ref, bf16[256,2048]{1,0:T(8,128)(2,1)} %get-tuple-element.990.refs_0_, bf16[256,2048]{1,0:T(8,128)(2,1)} %copy-done.40, bf16[512,2048]{1,0:T(8,128)(2,1)} %copy-done.49, ...), custom_call_target="tpu_custom_call" | custom-call | flops 1 | bytes 1 | tf_op jit(solution)/shard_map/mixed_back/pallas_call | solution.py:234
  470.4 6.3 convolution_convert_fusion.refs_19_
  478.7 35.1 %attention_backward.1 = (bf16[3,1024,512]{2,1,0:T(8,128)(2,1)}, bf16[8,768,512]{2,1,0:T(8,128)(2,1)}) custom-call(s32[15]{0:T(128)} %concatenate.57.meta_ref, bf16[3,1024,512]{2,1,0:T(8,128)(2,1)} %project.1.q_ref.k_ref.v_ref, bf16[3,1024,512]{2,1,0:T(8,128)(2,1)} %project.1.q_ref.k_ref.v_ref, bf16[3,1024,512]{2,1,0:T(8,128)(2,1)} %project.1.q_ref.k_ref.v_ref, ...), custom_call_target="tpu_custom_call" | custom-call | flops 1 | bytes 1 | tf_op jit(solution)/shard_map/attention_backward/pallas_call | solution.py:234
  517.9 2.5 add_convert_fusion.3.refs_0_
  522.0 3.8 collective-permute-done.48
  533.1 13.1 %feed_terms.8 = (bf16[512,2048]{1,0:T(8,128)(2,1)}, bf16[512,2048]{1,0:T(8,128)(2,1)}) custom-call(s32[15]{0:T(128)} %concatenate.57.meta_ref, bf16[1024,2048]{1,0:T(8,128)(2,1)} %mask_cotangent.1.x_ref.grad_ref.refs_4_, bf16[1024,2048]{1,0:T(8,128)(2,1)} %get-tuple-element.1322.norm_ref, bf16[2,1024,2048]{2,1,0:T(8,128)(2,1)} %get-tuple-element.1327.both_ref.x_any, ...), custom_call_target="tpu_custom_call" | custom-call | flops 1 | bytes 1 | tf_op jit(solution)/shard_map/feed_terms/pallas_call | solution.py:234
  546.3 2.4 collective-permute-done.50
  554.1 17.9 %collective-permute-done.53 = bf16[768,512]{1,0:T(8,128)(2,1)S(1)} collective-permute-done((bf16[768,512]{1,0:T(8,128)(2,1)S(1)}, bf16[768,512]{1,0:T(8,128)(2,1)S(1)}, u32[]{:S(2)}, u32[]{:S(2)}) %collective-permute-start.53) | collective-permute-done | bytes 786464 | tf_op jit(solution)/shard_map/ppermute | solution.py:117
  574.7 6.4 place_rows.2
  581.1 10.6 %collective-permute-done.56 = bf16[768,512]{1,0:T(8,128)(2,1)} collective-permute-done((bf16[768,512]{1,0:T(8,128)(2,1)S(1)}, bf16[768,512]{1,0:T(8,128)(2,1)}, u32[]{:S(2)}, u32[]{:S(2)}) %collective-permute-start.56) | collective-permute-done | bytes 786464 | tf_op jit(solution)/shard_map/ppermute | solution.py:117
  602.1 13.0 %in_back.1 = (bf16[512,2048]{1,0:T(8,128)(2,1)}, bf16[512,2048]{1,0:T(8,128)(2,1)}) custom-call(s32[15]{0:T(128)} %concatenate.57.meta_ref, bf16[1024,1536]{1,0:T(8,128)(2,1)} %pad_maximum_fusion.x_any, bf16[800,512]{1,0:T(8,128)(2,1)} %copy-done.8, bf16[800,512]{1,0:T(8,128)(2,1)} %copy-done.18, bf16[800,512]{1,0:T(8,128)(2,1)} %collective-permute-done.2.refs_2_, ...), custom_call_target="tpu_custom_call" | custom-call | flops 1 | bytes 1 | tf_op jit(solution)/shard_map/in_back/pallas_call | solution.py:234
  625.1 14.1 %collective-permute-done.60 = bf16[256,1536]{1,0:T(8,128)(2,1)S(1)} collective-permute-done((bf16[256,1536]{1,0:T(8,128)(2,1)S(1)}, bf16[256,1536]{1,0:T(8,128)(2,1)S(1)}, u32[]{:S(2)}, u32[]{:S(2)}) %collective-permute-start.60) | collective-permute-done | bytes 786464 | tf_op jit(solution)/shard_map/ppermute | solution.py:117
  648.2 6.0 first_norm_back.1
  655.7 45.0 %collective-permute-done.63 = bf16[256,1536]{1,0:T(8,128)(2,1)} collective-permute-done((bf16[256,1536]{1,0:T(8,128)(2,1)}, bf16[256,1536]{1,0:T(8,128)(2,1)}, u32[]{:S(2)}, u32[]{:S(2)}) %collective-permute-start.63) | collective-permute-done | bytes 786464 | tf_op jit(solution)/shard_map/ppermute | solution.py:117
  701.9 3.0 fusion.4
  705.0 3.1 fusion.3
  712.0 8.2 %feed_terms.9.refs_10_.refs_15_ = f32[512,2048]{1,0:T(8,128)} custom-call(s32[15]{0:T(128)} %concatenate.57.meta_ref, bf16[1024,2048]{1,0:T(8,128)(2,1)} %mask_cotangent.1.x_ref.grad_ref.refs_4_, bf16[1024,2048]{1,0:T(8,128)(2,1)} %get-tuple-element.1322.norm_ref, bf16[2,1024,2048]{2,1,0:T(8,128)(2,1)} %get-tuple-element.1327.both_ref.x_any, ...), custom_call_target="tpu_custom_call" | custom-call | flops 1 | bytes 1 | tf_op jit(solution)/shard_map/feed_terms/pallas_call | solution.py:234
  720.3 3.9 multiply_reduce_fusion
  726.9 7.3 place_rows.3
  734.3 4.4 multiply_reduce_fusion.1
  742.2 2.4 collective-permute-done.73
  745.2 3.4 collective-permute-done.74
  750.1 2.5 collective-permute-done.75
  752.6 2.4 collective-permute-start.76
  755.1 2.4 collective-permute-done.76
  760.7 19.9 %update_matrices.1 = (f32[3,256,512]{2,1,0:T(8,128)}, f32[3,256,512]{2,1,0:T(8,128)}, f32[3,256,512]{2,1,0:T(8,128)}, f32[3,256,512]{2,1,0:T(8,128)}, f32[512,25...) custom-call(f32[1]{0:T(128)} %bitcast.33.factor_ref, ...), custom_call_target="tpu_custom_call" | custom-call | tf_op jit(solution)/shard_map/update_matrices/pallas_call | solution.py:1059
  (356 shorter events, 157.4 us)
Async XLA Ops:
  2.3 21.3 %collective-permute-start = (bf16[800,512]{1,0:T(8,128)(2,1)S(1)}, bf16[800,512]{1,0:T(8,128)(2,1)S(1)}, u32[]{:S(2)}, u32[]{:S(2)}) collective-permute-start(bf16[800,512]{1,0:T(8,128)(2,1)S(1)} %fusion.11.refs_0_), channel_id=1, source_target_pairs={{8,0},{16,8},{24,16},{28,24},{20,28},{12,20},{4,12},{0,4},{9,1},{1... | collective-permute-start | bytes 2457608 | tf_op jit(solution)/shard_map/ppermute | solution.py:85
  5.3 19.7 %collective-permute-start.1 = (bf16[800,512]{1,0:T(8,128)(2,1)S(1)}, bf16[800,512]{1,0:T(8,128)(2,1)S(1)}, u32[]{:S(2)}, u32[]{:S(2)}) collective-permute-start(bf16[800,512]{1,0:T(8,128)(2,1)S(1)} %fusion.11.refs_0_), channel_id=1, source_target_pairs={{0,8},{8,16},{16,24},{24,28},{28,20},{20,12},{12,4},{4,0},{1,9},{9... | collective-permute-start | bytes 2457608 | tf_op jit(solution)/shard_map/ppermute | solution.py:86
  25.0 18.9 %collective-permute-start.2 = (bf16[800,512]{1,0:T(8,128)(2,1)S(1)}, bf16[800,512]{1,0:T(8,128)(2,1)}, u32[]{:S(2)}, u32[]{:S(2)}) collective-permute-start(bf16[800,512]{1,0:T(8,128)(2,1)S(1)} %collective-permute-done.refs_1_), channel_id=1, source_target_pairs={{8,0},{16,8},{24,16},{28,24},{20,28},{12,20},{4,12},{0,4},{9,1},{1... | collective-permute-start | bytes 2457608 | tf_op jit(solution)/shard_map/ppermute | solution.py:85
  26.6 18.6 %collective-permute-start.3 = (bf16[800,512]{1,0:T(8,128)(2,1)S(1)}, bf16[800,512]{1,0:T(8,128)(2,1)}, u32[]{:S(2)}, u32[]{:S(2)}) collective-permute-start(bf16[800,512]{1,0:T(8,128)(2,1)S(1)} %collective-permute-done.1.refs_7_), channel_id=1, source_target_pairs={{0,8},{8,16},{16,24},{24,28},{28,20},{20,12},{12,4},{4,0},{1,9},{9... | collective-permute-start | bytes 2457608 | tf_op jit(solution)/shard_map/ppermute | solution.py:86
  45.2 17.8 %collective-permute-start.4 = (bf16[800,512]{1,0:T(8,128)(2,1)}, bf16[800,512]{1,0:T(8,128)(2,1)S(1)}, u32[]{:S(2)}, u32[]{:S(2)}) collective-permute-start(bf16[800,512]{1,0:T(8,128)(2,1)} %collective-permute-done.2.refs_2_), channel_id=1, source_target_pairs={{8,0},{16,8},{24,16},{28,24},{20,28},{12,20},{4,12},{0,4},{9,1},{1... | collective-permute-start | bytes 2457608 | tf_op jit(solution)/shard_map/ppermute | solution.py:85
  46.8 17.5 %collective-permute-start.5 = (bf16[800,512]{1,0:T(8,128)(2,1)}, bf16[800,512]{1,0:T(8,128)(2,1)S(1)}, u32[]{:S(2)}, u32[]{:S(2)}) collective-permute-start(bf16[800,512]{1,0:T(8,128)(2,1)} %collective-permute-done.3.refs_6_), channel_id=1, source_target_pairs={{0,8},{8,16},{16,24},{24,28},{28,20},{20,12},{12,4},{4,0},{1,9},{9... | collective-permute-start | bytes 2457608 | tf_op jit(solution)/shard_map/ppermute | solution.py:86
  89.3 20.7 %collective-permute-start.8 = (bf16[768,512]{1,0:T(8,128)(2,1)}, bf16[768,512]{1,0:T(8,128)(2,1)S(1)}, u32[]{:S(2)}, u32[]{:S(2)}) collective-permute-start(bf16[768,512]{1,0:T(8,128)(2,1)} %project_prefix.1.refs_0_.refs_8_.refs_3_), channel_id=1, source_target_pairs={{8,0},{16,8},{24,16},{28,24},{20,28},{12,20},{4,12},{0,4},{9,1},{1... | collective-permute-start | bytes 2359304 | tf_op jit(solution)/shard_map/ppermute | solution.py:85
  90.1 20.7 %collective-permute-start.9 = (bf16[768,512]{1,0:T(8,128)(2,1)}, bf16[768,512]{1,0:T(8,128)(2,1)S(1)}, u32[]{:S(2)}, u32[]{:S(2)}) collective-permute-start(bf16[768,512]{1,0:T(8,128)(2,1)} %project_prefix.1.refs_0_.refs_8_.refs_3_), channel_id=1, source_target_pairs={{0,8},{8,16},{16,24},{24,28},{28,20},{20,12},{12,4},{4,0},{1,9},{9... | collective-permute-start | bytes 2359304 | tf_op jit(solution)/shard_map/ppermute | solution.py:86
  91.3 41.1 %collective-permute-start.12 = (bf16[2048,256]{1,0:T(8,128)(2,1)S(1)}, bf16[2048,256]{1,0:T(8,128)(2,1)S(1)}, u32[]{:S(2)}, u32[]{:S(2)}) collective-permute-start(bf16[2048,256]{1,0:T(8,128)(2,1)S(1)} %copy-done.12), channel_id=1, source_target_pairs={{8,0},{16,8},{24,16},{28,24},{20,28},{12,20},{4,12},{0,4},{9,1},{1... | collective-permute-start | bytes 3145736 | tf_op jit(solution)/shard_map/ppermute | solution.py:85
  92.1 41.1 %collective-permute-start.13 = (bf16[2048,256]{1,0:T(8,128)(2,1)S(1)}, bf16[2048,256]{1,0:T(8,128)(2,1)S(1)}, u32[]{:S(2)}, u32[]{:S(2)}) collective-permute-start(bf16[2048,256]{1,0:T(8,128)(2,1)S(1)} %copy-done.12), channel_id=1, source_target_pairs={{0,8},{8,16},{16,24},{24,28},{28,20},{20,12},{12,4},{4,0},{1,9},{9... | collective-permute-start | bytes 3145736 | tf_op jit(solution)/shard_map/ppermute | solution.py:86
  110.8 35.2 %collective-permute-start.10 = (bf16[768,512]{1,0:T(8,128)(2,1)S(1)}, bf16[768,512]{1,0:T(8,128)(2,1)S(1)}, u32[]{:S(2)}, u32[]{:S(2)}) collective-permute-start(bf16[768,512]{1,0:T(8,128)(2,1)S(1)} %collective-permute-done.8.refs_1_.refs_9_.refs_4_), channel_id=1, source_target_pairs={{8,0},{16,8},{24,16},{28,24},{20,28},{12,20},{4,12},{0,4},{9,1},{1... | collective-permute-start | bytes 2359304 | tf_op jit(solution)/shard_map/ppermute | solution.py:85
  111.4 35.5 %collective-permute-start.11 = (bf16[768,512]{1,0:T(8,128)(2,1)S(1)}, bf16[768,512]{1,0:T(8,128)(2,1)S(1)}, u32[]{:S(2)}, u32[]{:S(2)}) collective-permute-start(bf16[768,512]{1,0:T(8,128)(2,1)S(1)} %collective-permute-done.9.refs_7_.refs_15_.refs_10_), channel_id=1, source_target_pairs={{0,8},{8,16},{16,24},{24,28},{28,20},{20,12},{12,4},{4,0},{1,9},{9... | collective-permute-start | bytes 2359304 | tf_op jit(solution)/shard_map/ppermute | solution.py:86
  146.8 16.9 %collective-permute-start.14 = (bf16[768,512]{1,0:T(8,128)(2,1)S(1)}, bf16[768,512]{1,0:T(8,128)(2,1)S(1)}, u32[]{:S(2)}, u32[]{:S(2)}) collective-permute-start(bf16[768,512]{1,0:T(8,128)(2,1)S(1)} %collective-permute-done.10.refs_2_.refs_10_.refs_5_), channel_id=1, source_target_pairs={{8,0},{16,8},{24,16},{28,24},{20,28},{12,20},{4,12},{0,4},{9,1},{1... | collective-permute-start | bytes 2359304 | tf_op jit(solution)/shard_map/ppermute | solution.py:85
  147.4 17.2 %collective-permute-start.15 = (bf16[768,512]{1,0:T(8,128)(2,1)S(1)}, bf16[768,512]{1,0:T(8,128)(2,1)S(1)}, u32[]{:S(2)}, u32[]{:S(2)}) collective-permute-start(bf16[768,512]{1,0:T(8,128)(2,1)S(1)} %collective-permute-done.11.refs_6_.refs_14_.refs_9_), channel_id=1, source_target_pairs={{0,8},{8,16},{16,24},{24,28},{28,20},{20,12},{12,4},{4,0},{1,9},{9... | collective-permute-start | bytes 2359304 | tf_op jit(solution)/shard_map/ppermute | solution.py:86
  164.6 12.1 %collective-permute-start.16 = (bf16[384,512]{1,0:T(8,128)(2,1)S(1)}, bf16[384,512]{1,0:T(8,128)(2,1)S(1)}, u32[]{:S(2)}, u32[]{:S(2)}) collective-permute-start(bf16[384,512]{1,0:T(8,128)(2,1)S(1)} %slice.243), channel_id=1, source_target_pairs={{8,0},{16,8},{24,16},{28,24},{20,28},{12,20},{4,12},{0,4},{9,1},{1... | collective-permute-start | bytes 1179656 | tf_op jit(solution)/shard_map/ppermute | solution.py:85
  165.3 12.1 %collective-permute-start.17 = (bf16[384,512]{1,0:T(8,128)(2,1)S(1)}, bf16[384,512]{1,0:T(8,128)(2,1)S(1)}, u32[]{:S(2)}, u32[]{:S(2)}) collective-permute-start(bf16[384,512]{1,0:T(8,128)(2,1)S(1)} %slice.244), channel_id=1, source_target_pairs={{0,8},{8,16},{16,24},{24,28},{28,20},{20,12},{12,4},{4,0},{1,9},{9... | collective-permute-start | bytes 1179656 | tf_op jit(solution)/shard_map/ppermute | solution.py:86
  166.8 34.6 %collective-permute-start.20 = (bf16[2048,256]{1,0:T(8,128)(2,1)S(1)}, bf16[2048,256]{1,0:T(8,128)(2,1)}, u32[]{:S(2)}, u32[]{:S(2)}) collective-permute-start(bf16[2048,256]{1,0:T(8,128)(2,1)S(1)} %collective-permute-done.12.refs_1_), channel_id=1, source_target_pairs={{8,0},{16,8},{24,16},{28,24},{20,28},{12,20},{4,12},{0,4},{9,1},{1... | collective-permute-start | bytes 3145736 | tf_op jit(solution)/shard_map/ppermute | solution.py:85
  167.3 34.1 %collective-permute-start.21 = (bf16[2048,256]{1,0:T(8,128)(2,1)S(1)}, bf16[2048,256]{1,0:T(8,128)(2,1)}, u32[]{:S(2)}, u32[]{:S(2)}) collective-permute-start(bf16[2048,256]{1,0:T(8,128)(2,1)S(1)} %collective-permute-done.13.refs_7_), channel_id=1, source_target_pairs={{0,8},{8,16},{16,24},{24,28},{28,20},{20,12},{12,4},{4,0},{1,9},{9... | collective-permute-start | bytes 3145736 | tf_op jit(solution)/shard_map/ppermute | solution.py:86
  177.4 36.4 %collective-permute-start.18 = (bf16[256,2048]{1,0:T(8,128)(2,1)S(1)}, bf16[256,2048]{1,0:T(8,128)(2,1)}, u32[]{:S(2)}, u32[]{:S(2)}) collective-permute-start(bf16[256,2048]{1,0:T(8,128)(2,1)S(1)} %copy-done.13), channel_id=1, source_target_pairs={{8,0},{16,8},{24,16},{28,24},{20,28},{12,20},{4,12},{0,4},{9,1},{1... | collective-permute-start | bytes 3145736 | tf_op jit(solution)/shard_map/ppermute | solution.py:85
  178.0 36.3 %collective-permute-start.19 = (bf16[256,2048]{1,0:T(8,128)(2,1)S(1)}, bf16[256,2048]{1,0:T(8,128)(2,1)}, u32[]{:S(2)}, u32[]{:S(2)}) collective-permute-start(bf16[256,2048]{1,0:T(8,128)(2,1)S(1)} %copy-done.13), channel_id=1, source_target_pairs={{0,8},{8,16},{16,24},{24,28},{28,20},{20,12},{12,4},{4,0},{1,9},{9... | collective-permute-start | bytes 3145736 | tf_op jit(solution)/shard_map/ppermute | solution.py:86
  214.4 26.2 %collective-permute-start.24 = (bf16[2048,256]{1,0:T(8,128)(2,1)}, bf16[2048,256]{1,0:T(8,128)(2,1)S(1)}, u32[]{:S(2)}, u32[]{:S(2)}) collective-permute-start(bf16[2048,256]{1,0:T(8,128)(2,1)} %collective-permute-done.20.refs_2_), channel_id=1, source_target_pairs={{8,0},{16,8},{24,16},{28,24},{20,28},{12,20},{4,12},{0,4},{9,1},{1... | collective-permute-start | bytes 3145736 | tf_op jit(solution)/shard_map/ppermute | solution.py:85
  215.1 26.2 %collective-permute-start.25 = (bf16[2048,256]{1,0:T(8,128)(2,1)}, bf16[2048,256]{1,0:T(8,128)(2,1)S(1)}, u32[]{:S(2)}, u32[]{:S(2)}) collective-permute-start(bf16[2048,256]{1,0:T(8,128)(2,1)} %collective-permute-done.21.refs_6_), channel_id=1, source_target_pairs={{0,8},{8,16},{16,24},{24,28},{28,20},{20,12},{12,4},{4,0},{1,9},{9... | collective-permute-start | bytes 3145736 | tf_op jit(solution)/shard_map/ppermute | solution.py:86
  221.1 25.3 %collective-permute-start.27 = (bf16[256,2048]{1,0:T(8,128)(2,1)S(1)}, bf16[256,2048]{1,0:T(8,128)(2,1)S(1)}, u32[]{:S(2)}, u32[]{:S(2)}) collective-permute-start(bf16[256,2048]{1,0:T(8,128)(2,1)S(1)} %add_convert_fusion.6), channel_id=1, source_target_pairs={{0,2},{1,3},{2,0},{3,1},{4,6},{5,7},{6,4},{7,5},{8,10},{9,11},{10,... | collective-permute-start | bytes 3145736 | tf_op jit(solution)/shard_map/ppermute | solution.py:174
  222.7 40.0 %collective-permute-start.22 = (bf16[256,2048]{1,0:T(8,128)(2,1)}, bf16[256,2048]{1,0:T(8,128)(2,1)S(1)}, u32[]{:S(2)}, u32[]{:S(2)}) collective-permute-start(bf16[256,2048]{1,0:T(8,128)(2,1)} %collective-permute-done.18.refs_4_.refs_1_), channel_id=1, source_target_pairs={{8,0},{16,8},{24,16},{28,24},{20,28},{12,20},{4,12},{0,4},{9,1},{1... | collective-permute-start | bytes 3145736 | tf_op jit(solution)/shard_map/ppermute | solution.py:85
  223.4 39.7 %collective-permute-start.23 = (bf16[256,2048]{1,0:T(8,128)(2,1)}, bf16[256,2048]{1,0:T(8,128)(2,1)S(1)}, u32[]{:S(2)}, u32[]{:S(2)}) collective-permute-start(bf16[256,2048]{1,0:T(8,128)(2,1)} %collective-permute-done.19.refs_10_.refs_7_), channel_id=1, source_target_pairs={{0,8},{8,16},{16,24},{24,28},{28,20},{20,12},{12,4},{4,0},{1,9},{9... | collective-permute-start | bytes 3145736 | tf_op jit(solution)/shard_map/ppermute | solution.py:86
  263.0 24.5 %collective-permute-start.28 = (bf16[256,2048]{1,0:T(8,128)(2,1)S(1)}, bf16[256,2048]{1,0:T(8,128)(2,1)S(1)}, u32[]{:S(2)}, u32[]{:S(2)}) collective-permute-start(bf16[256,2048]{1,0:T(8,128)(2,1)S(1)} %collective-permute-done.22.refs_5_.refs_2_), channel_id=1, source_target_pairs={{8,0},{16,8},{24,16},{28,24},{20,28},{12,20},{4,12},{0,4},{9,1},{1... | collective-permute-start | bytes 3145736 | tf_op jit(solution)/shard_map/ppermute | solution.py:85
  263.7 24.2 %collective-permute-start.29 = (bf16[256,2048]{1,0:T(8,128)(2,1)S(1)}, bf16[256,2048]{1,0:T(8,128)(2,1)S(1)}, u32[]{:S(2)}, u32[]{:S(2)}) collective-permute-start(bf16[256,2048]{1,0:T(8,128)(2,1)S(1)} %collective-permute-done.23.refs_9_.refs_6_), channel_id=1, source_target_pairs={{0,8},{8,16},{16,24},{24,28},{28,20},{20,12},{12,4},{4,0},{1,9},{9... | collective-permute-start | bytes 3145736 | tf_op jit(solution)/shard_map/ppermute | solution.py:86
  265.1 24.1 %collective-permute-start.30 = (bf16[256,2048]{1,0:T(8,128)(2,1)}, bf16[256,2048]{1,0:T(8,128)(2,1)S(1)}, u32[]{:S(2)}, u32[]{:S(2)}) collective-permute-start(bf16[256,2048]{1,0:T(8,128)(2,1)} %get-tuple-element.852.refs_0_), channel_id=1, source_target_pairs={{0,2},{1,3},{2,0},{3,1},{4,6},{5,7},{6,4},{7,5},{8,10},{9,11},{10,... | collective-permute-start | bytes 3145736 | tf_op jit(solution)/shard_map/ppermute | solution.py:178
  292.4 32.1 %collective-permute-start.35 = (bf16[512,2048]{1,0:T(8,128)(2,1)}, bf16[512,2048]{1,0:T(8,128)(2,1)}, u32[]{:S(2)}, u32[]{:S(2)}) collective-permute-start(bf16[512,2048]{1,0:T(8,128)(2,1)} %pad_maximum_fusion.1), channel_id=1, source_target_pairs={{0,1},{1,0},{2,3},{3,2},{4,5},{5,4},{6,7},{7,6},{8,9},{9,8},{10,11... | collective-permute-start | bytes 6291464 | tf_op jit(solution)/shard_map/ppermute | solution.py:184
  292.4 14.8 %collective-permute-start.33 = (bf16[1024,256]{1,0:T(8,128)(2,1)S(1)}, bf16[1024,256]{1,0:T(8,128)(2,1)S(1)}, u32[]{:S(2)}, u32[]{:S(2)}) collective-permute-start(bf16[1024,256]{1,0:T(8,128)(2,1)S(1)} %slice.249), channel_id=1, source_target_pairs={{8,0},{16,8},{24,16},{28,24},{20,28},{12,20},{4,12},{0,4},{9,1},{1... | collective-permute-start | bytes 1572872 | tf_op jit(solution)/shard_map/ppermute | solution.py:85
  293.2 14.8 %collective-permute-start.34 = (bf16[1024,256]{1,0:T(8,128)(2,1)S(1)}, bf16[1024,256]{1,0:T(8,128)(2,1)S(1)}, u32[]{:S(2)}, u32[]{:S(2)}) collective-permute-start(bf16[1024,256]{1,0:T(8,128)(2,1)S(1)} %slice.250), channel_id=1, source_target_pairs={{0,8},{8,16},{16,24},{24,28},{28,20},{20,12},{12,4},{4,0},{1,9},{9... | collective-permute-start | bytes 1572872 | tf_op jit(solution)/shard_map/ppermute | solution.py:86
  294.6 29.8 %collective-permute-start.31 = (bf16[128,2048]{1,0:T(8,128)(2,1)S(1)}, bf16[128,2048]{1,0:T(8,128)(2,1)S(1)}, u32[]{:S(2)}, u32[]{:S(2)}) collective-permute-start(bf16[128,2048]{1,0:T(8,128)(2,1)S(1)} %slice.247), channel_id=1, source_target_pairs={{8,0},{16,8},{24,16},{28,24},{20,28},{12,20},{4,12},{0,4},{9,1},{1... | collective-permute-start | bytes 1572872 | tf_op jit(solution)/shard_map/ppermute | solution.py:85
  295.4 29.0 %collective-permute-start.32 = (bf16[128,2048]{1,0:T(8,128)(2,1)S(1)}, bf16[128,2048]{1,0:T(8,128)(2,1)S(1)}, u32[]{:S(2)}, u32[]{:S(2)}) collective-permute-start(bf16[128,2048]{1,0:T(8,128)(2,1)S(1)} %slice.248), channel_id=1, source_target_pairs={{0,8},{8,16},{16,24},{24,28},{28,20},{20,12},{12,4},{4,0},{1,9},{9... | collective-permute-start | bytes 1572872 | tf_op jit(solution)/shard_map/ppermute | solution.py:86
  355.0 23.9 %collective-permute-start.36 = (bf16[256,2048]{1,0:T(8,128)(2,1)}, bf16[256,2048]{1,0:T(8,128)(2,1)S(1)}, u32[]{:S(2)}, u32[]{:S(2)}) collective-permute-start(bf16[256,2048]{1,0:T(8,128)(2,1)} %get-tuple-element.860), channel_id=1, source_target_pairs={{0,8},{8,16},{16,24},{24,28},{28,20},{20,12},{12,4},{4,0},{1,9},{9... | collective-permute-start | bytes 3145736 | tf_op jit(solution)/shard_map/ppermute | solution.py:117
  356.4 23.9 %collective-permute-start.37 = (bf16[256,2048]{1,0:T(8,128)(2,1)}, bf16[256,2048]{1,0:T(8,128)(2,1)S(1)}, u32[]{:S(2)}, u32[]{:S(2)}) collective-permute-start(bf16[256,2048]{1,0:T(8,128)(2,1)} %get-tuple-element.861), channel_id=1, source_target_pairs={{8,0},{16,8},{24,16},{28,24},{20,28},{12,20},{4,12},{0,4},{9,1},{1... | collective-permute-start | bytes 3145736 | tf_op jit(solution)/shard_map/ppermute | solution.py:118
  388.0 25.4 %collective-permute-start.41 = (bf16[256,2048]{1,0:T(8,128)(2,1)}, bf16[256,2048]{1,0:T(8,128)(2,1)S(1)}, u32[]{:S(2)}, u32[]{:S(2)}) collective-permute-start(bf16[256,2048]{1,0:T(8,128)(2,1)} %add_convert_fusion.5), channel_id=1, source_target_pairs={{0,2},{1,3},{2,0},{3,1},{4,6},{5,7},{6,4},{7,5},{8,10},{9,11},{10,... | collective-permute-start | bytes 3145736 | tf_op jit(solution)/shard_map/ppermute | solution.py:174
  401.7 48.0 %collective-permute-start.39 = (bf16[512,2048]{1,0:T(8,128)(2,1)}, bf16[512,2048]{1,0:T(8,128)(2,1)S(1)}, u32[]{:S(2)}, u32[]{:S(2)}) collective-permute-start(bf16[512,2048]{1,0:T(8,128)(2,1)} %get-tuple-element.906), channel_id=1, source_target_pairs={{0,8},{8,16},{16,24},{24,28},{28,20},{20,12},{12,4},{4,0},{1,9},{9... | collective-permute-start | bytes 6291464 | tf_op jit(solution)/shard_map/ppermute | solution.py:117
  403.0 47.8 %collective-permute-start.40 = (bf16[512,2048]{1,0:T(8,128)(2,1)}, bf16[512,2048]{1,0:T(8,128)(2,1)S(1)}, u32[]{:S(2)}, u32[]{:S(2)}) collective-permute-start(bf16[512,2048]{1,0:T(8,128)(2,1)} %get-tuple-element.907), channel_id=1, source_target_pairs={{8,0},{16,8},{24,16},{28,24},{20,28},{12,20},{4,12},{0,4},{9,1},{1... | collective-permute-start | bytes 6291464 | tf_op jit(solution)/shard_map/ppermute | solution.py:118
  421.0 29.7 %collective-permute-start.42 = (bf16[256,2048]{1,0:T(8,128)(2,1)}, bf16[256,2048]{1,0:T(8,128)(2,1)S(1)}, u32[]{:S(2)}, u32[]{:S(2)}) collective-permute-start(bf16[256,2048]{1,0:T(8,128)(2,1)} %get-tuple-element.990.refs_0_), channel_id=1, source_target_pairs={{0,2},{1,3},{2,0},{3,1},{4,6},{5,7},{6,4},{7,5},{8,10},{9,11},{10,... | collective-permute-start | bytes 3145736 | tf_op jit(solution)/shard_map/ppermute | solution.py:178
  457.6 56.3 %collective-permute-start.43 = (bf16[512,2048]{1,0:T(8,128)(2,1)}, bf16[512,2048]{1,0:T(8,128)(2,1)S(1)}, u32[]{:S(2)}, u32[]{:S(2)}) collective-permute-start(bf16[512,2048]{1,0:T(8,128)(2,1)} %add_convert_fusion.1), channel_id=1, source_target_pairs={{0,8},{8,16},{16,24},{24,28},{28,20},{20,12},{12,4},{4,0},{1,9},{9... | collective-permute-start | bytes 6291464 | tf_op jit(solution)/shard_map/ppermute | solution.py:117
  458.7 55.2 %collective-permute-start.44 = (bf16[512,2048]{1,0:T(8,128)(2,1)}, bf16[512,2048]{1,0:T(8,128)(2,1)S(1)}, u32[]{:S(2)}, u32[]{:S(2)}) collective-permute-start(bf16[512,2048]{1,0:T(8,128)(2,1)} %add_convert_fusion), channel_id=1, source_target_pairs={{8,0},{16,8},{24,16},{28,24},{20,28},{12,20},{4,12},{0,4},{9,1},{1... | collective-permute-start | bytes 6291464 | tf_op jit(solution)/shard_map/ppermute | solution.py:118
  478.1 35.7 %collective-permute-start.47 = (bf16[256,2048]{1,0:T(8,128)(2,1)}, bf16[256,2048]{1,0:T(8,128)(2,1)S(1)}, u32[]{:S(2)}, u32[]{:S(2)}) collective-permute-start(bf16[256,2048]{1,0:T(8,128)(2,1)} %add_convert_fusion.4), channel_id=1, source_target_pairs={{0,2},{1,3},{2,0},{3,1},{4,6},{5,7},{6,4},{7,5},{8,10},{9,11},{10,... | collective-permute-start | bytes 3145736 | tf_op jit(solution)/shard_map/ppermute | solution.py:174
  515.6 10.1 %collective-permute-start.48 = (bf16[384,512]{1,0:T(8,128)(2,1)S(1)}, bf16[384,512]{1,0:T(8,128)(2,1)S(1)}, u32[]{:S(2)}, u32[]{:S(2)}) collective-permute-start(bf16[384,512]{1,0:T(8,128)(2,1)S(1)} %get-tuple-element.1376), channel_id=1, source_target_pairs={{0,8},{8,16},{16,24},{24,28},{28,20},{20,12},{12,4},{4,0},{1,9},{9... | collective-permute-start | bytes 1179656 | tf_op jit(solution)/shard_map/ppermute | solution.py:117
  520.4 25.8 %collective-permute-start.52 = (bf16[256,2048]{1,0:T(8,128)(2,1)S(1)}, bf16[256,2048]{1,0:T(8,128)(2,1)}, u32[]{:S(2)}, u32[]{:S(2)}) collective-permute-start(bf16[256,2048]{1,0:T(8,128)(2,1)S(1)} %add_convert_fusion.3.refs_0_), channel_id=1, source_target_pairs={{0,2},{1,3},{2,0},{3,1},{4,6},{5,7},{6,4},{7,5},{8,10},{9,11},{10,... | collective-permute-start | bytes 3145736 | tf_op jit(solution)/shard_map/ppermute | solution.py:178
  531.1 17.6 %collective-permute-start.50 = (bf16[768,512]{1,0:T(8,128)(2,1)}, bf16[768,512]{1,0:T(8,128)(2,1)S(1)}, u32[]{:S(2)}, u32[]{:S(2)}) collective-permute-start(bf16[768,512]{1,0:T(8,128)(2,1)} %pad_maximum_fusion.6), channel_id=1, source_target_pairs={{0,8},{8,16},{16,24},{24,28},{28,20},{20,12},{12,4},{4,0},{1,9},{9... | collective-permute-start | bytes 2359304 | tf_op jit(solution)/shard_map/ppermute | solution.py:117
  531.6 17.3 %collective-permute-start.51 = (bf16[768,512]{1,0:T(8,128)(2,1)}, bf16[768,512]{1,0:T(8,128)(2,1)}, u32[]{:S(2)}, u32[]{:S(2)}) collective-permute-start(bf16[768,512]{1,0:T(8,128)(2,1)} %pad_maximum_fusion.5), channel_id=1, source_target_pairs={{8,0},{16,8},{24,16},{28,24},{20,28},{12,20},{4,12},{0,4},{9,1},{1... | collective-permute-start | bytes 2359304 | tf_op jit(solution)/shard_map/ppermute | solution.py:118
  552.0 20.2 %collective-permute-start.55 = (bf16[512,2048]{1,0:T(8,128)(2,1)S(1)}, bf16[512,2048]{1,0:T(8,128)(2,1)}, u32[]{:S(2)}, u32[]{:S(2)}) collective-permute-start(bf16[512,2048]{1,0:T(8,128)(2,1)S(1)} %pad_maximum_fusion.3), channel_id=1, source_target_pairs={{0,1},{1,0},{2,3},{3,2},{4,5},{5,4},{6,7},{7,6},{8,9},{9,8},{10,11... | collective-permute-start | bytes 6291464 | tf_op jit(solution)/shard_map/ppermute | solution.py:184
  552.1 19.9 %collective-permute-start.53 = (bf16[768,512]{1,0:T(8,128)(2,1)S(1)}, bf16[768,512]{1,0:T(8,128)(2,1)S(1)}, u32[]{:S(2)}, u32[]{:S(2)}) collective-permute-start(bf16[768,512]{1,0:T(8,128)(2,1)S(1)} %get-tuple-element.1117), channel_id=1, source_target_pairs={{0,8},{8,16},{16,24},{24,28},{28,20},{20,12},{12,4},{4,0},{1,9},{9... | collective-permute-start | bytes 2359304 | tf_op jit(solution)/shard_map/ppermute | solution.py:117
  552.6 19.6 %collective-permute-start.54 = (bf16[768,512]{1,0:T(8,128)(2,1)S(1)}, bf16[768,512]{1,0:T(8,128)(2,1)S(1)}, u32[]{:S(2)}, u32[]{:S(2)}) collective-permute-start(bf16[768,512]{1,0:T(8,128)(2,1)S(1)} %get-tuple-element.1118), channel_id=1, source_target_pairs={{8,0},{16,8},{24,16},{28,24},{20,28},{12,20},{4,12},{0,4},{9,1},{1... | collective-permute-start | bytes 2359304 | tf_op jit(solution)/shard_map/ppermute | solution.py:118
  572.6 19.1 %collective-permute-start.56 = (bf16[768,512]{1,0:T(8,128)(2,1)S(1)}, bf16[768,512]{1,0:T(8,128)(2,1)}, u32[]{:S(2)}, u32[]{:S(2)}) collective-permute-start(bf16[768,512]{1,0:T(8,128)(2,1)S(1)} %get-tuple-element.1154), channel_id=1, source_target_pairs={{0,8},{8,16},{16,24},{24,28},{28,20},{20,12},{12,4},{4,0},{1,9},{9... | collective-permute-start | bytes 2359304 | tf_op jit(solution)/shard_map/ppermute | solution.py:117
  573.2 18.7 %collective-permute-start.57 = (bf16[768,512]{1,0:T(8,128)(2,1)S(1)}, bf16[768,512]{1,0:T(8,128)(2,1)}, u32[]{:S(2)}, u32[]{:S(2)}) collective-permute-start(bf16[768,512]{1,0:T(8,128)(2,1)S(1)} %get-tuple-element.1155), channel_id=1, source_target_pairs={{8,0},{16,8},{24,16},{28,24},{20,28},{12,20},{4,12},{0,4},{9,1},{1... | collective-permute-start | bytes 2359304 | tf_op jit(solution)/shard_map/ppermute | solution.py:118
  600.0 15.0 %collective-permute-start.58 = (bf16[128,1536]{1,0:T(8,128)(2,1)}, bf16[128,1536]{1,0:T(8,128)(2,1)S(1)}, u32[]{:S(2)}, u32[]{:S(2)}) collective-permute-start(bf16[128,1536]{1,0:T(8,128)(2,1)} %get-tuple-element.1381), channel_id=1, source_target_pairs={{0,8},{8,16},{16,24},{24,28},{28,20},{20,12},{12,4},{4,0},{1,9},{9... | collective-permute-start | bytes 1179656 | tf_op jit(solution)/shard_map/ppermute | solution.py:117
  601.6 13.5 %collective-permute-start.59 = (bf16[128,1536]{1,0:T(8,128)(2,1)}, bf16[128,1536]{1,0:T(8,128)(2,1)S(1)}, u32[]{:S(2)}, u32[]{:S(2)}) collective-permute-start(bf16[128,1536]{1,0:T(8,128)(2,1)} %get-tuple-element.1380), channel_id=1, source_target_pairs={{8,0},{16,8},{24,16},{28,24},{20,28},{12,20},{4,12},{0,4},{9,1},{1... | collective-permute-start | bytes 1179656 | tf_op jit(solution)/shard_map/ppermute | solution.py:118
  618.8 20.4 %collective-permute-start.60 = (bf16[256,1536]{1,0:T(8,128)(2,1)S(1)}, bf16[256,1536]{1,0:T(8,128)(2,1)S(1)}, u32[]{:S(2)}, u32[]{:S(2)}) collective-permute-start(bf16[256,1536]{1,0:T(8,128)(2,1)S(1)} %pad_maximum_fusion.8), channel_id=1, source_target_pairs={{0,8},{8,16},{16,24},{24,28},{28,20},{20,12},{12,4},{4,0},{1,9},{9... | collective-permute-start | bytes 2359304 | tf_op jit(solution)/shard_map/ppermute | solution.py:117
  620.4 20.4 %collective-permute-start.61 = (bf16[256,1536]{1,0:T(8,128)(2,1)S(1)}, bf16[256,1536]{1,0:T(8,128)(2,1)S(1)}, u32[]{:S(2)}, u32[]{:S(2)}) collective-permute-start(bf16[256,1536]{1,0:T(8,128)(2,1)S(1)} %pad_maximum_fusion.7), channel_id=1, source_target_pairs={{8,0},{16,8},{24,16},{28,24},{20,28},{12,20},{4,12},{0,4},{9,1},{1... | collective-permute-start | bytes 2359304 | tf_op jit(solution)/shard_map/ppermute | solution.py:118
  620.9 87.2 %collective-permute-start.68 = (bf16[512,2048]{1,0:T(8,128)(2,1)}, bf16[512,2048]{1,0:T(8,128)(2,1)}, u32[]{:S(2)}, u32[]{:S(2)}) collective-permute-start(bf16[512,2048]{1,0:T(8,128)(2,1)} %get-tuple-element.1303), channel_id=1, source_target_pairs={{0,8},{8,16},{16,24},{24,28},{28,20},{20,12},{12,4},{4,0},{1,9},{9... | collective-permute-start | bytes 6291464 | tf_op jit(solution)/shard_map/ppermute | solution.py:117
  622.6 85.4 %collective-permute-start.69 = (bf16[512,2048]{1,0:T(8,128)(2,1)}, bf16[512,2048]{1,0:T(8,128)(2,1)}, u32[]{:S(2)}, u32[]{:S(2)}) collective-permute-start(bf16[512,2048]{1,0:T(8,128)(2,1)} %get-tuple-element.1304), channel_id=1, source_target_pairs={{8,0},{16,8},{24,16},{28,24},{20,28},{12,20},{4,12},{0,4},{9,1},{1... | collective-permute-start | bytes 6291464 | tf_op jit(solution)/shard_map/ppermute | solution.py:118
  623.5 24.6 %collective-permute-start.65 = (bf16[256,2048]{1,0:T(8,128)(2,1)S(1)}, bf16[256,2048]{1,0:T(8,128)(2,1)}, u32[]{:S(2)}, u32[]{:S(2)}) collective-permute-start(bf16[256,2048]{1,0:T(8,128)(2,1)S(1)} %add_convert_fusion.2), channel_id=1, source_target_pairs={{0,2},{1,3},{2,0},{3,1},{4,6},{5,7},{6,4},{7,5},{8,10},{9,11},{10,... | collective-permute-start | bytes 3145736 | tf_op jit(solution)/shard_map/ppermute | solution.py:174
  644.5 56.2 %collective-permute-start.63 = (bf16[256,1536]{1,0:T(8,128)(2,1)}, bf16[256,1536]{1,0:T(8,128)(2,1)}, u32[]{:S(2)}, u32[]{:S(2)}) collective-permute-start(bf16[256,1536]{1,0:T(8,128)(2,1)} %fusion.2), channel_id=1, source_target_pairs={{0,8},{8,16},{16,24},{24,28},{28,20},{20,12},{12,4},{4,0},{1,9},{9... | collective-permute-start | bytes 2359304 | tf_op jit(solution)/shard_map/ppermute | solution.py:117
  645.9 56.0 %collective-permute-start.64 = (bf16[256,1536]{1,0:T(8,128)(2,1)}, bf16[256,1536]{1,0:T(8,128)(2,1)}, u32[]{:S(2)}, u32[]{:S(2)}) collective-permute-start(bf16[256,1536]{1,0:T(8,128)(2,1)} %fusion.1), channel_id=1, source_target_pairs={{8,0},{16,8},{24,16},{28,24},{20,28},{12,20},{4,12},{0,4},{9,1},{1... | collective-permute-start | bytes 2359304 | tf_op jit(solution)/shard_map/ppermute | solution.py:118
  654.2 53.9 %collective-permute-start.70 = (bf16[256,2048]{1,0:T(8,128)(2,1)}, bf16[256,2048]{1,0:T(8,128)(2,1)S(1)}, u32[]{:S(2)}, u32[]{:S(2)}) collective-permute-start(bf16[256,2048]{1,0:T(8,128)(2,1)} %get-tuple-element.1333.refs_0_), channel_id=1, source_target_pairs={{0,2},{1,3},{2,0},{3,1},{4,6},{5,7},{6,4},{7,5},{8,10},{9,11},{10,... | collective-permute-start | bytes 3145736 | tf_op jit(solution)/shard_map/ppermute | solution.py:178
  709.8 17.2 %collective-permute-start.71 = (bf16[512,2048]{1,0:T(8,128)(2,1)}, bf16[512,2048]{1,0:T(8,128)(2,1)}, u32[]{:S(2)}, u32[]{:S(2)}) collective-permute-start(bf16[512,2048]{1,0:T(8,128)(2,1)} %pad_maximum_fusion.4), channel_id=1, source_target_pairs={{0,1},{1,0},{2,3},{3,2},{4,5},{5,4},{6,7},{7,6},{8,9},{9,8},{10,11... | collective-permute-start | bytes 6291464 | tf_op jit(solution)/shard_map/ppermute | solution.py:184
  710.0 24.3 %collective-permute-start.66 = (bf16[256,1536]{1,0:T(8,128)(2,1)}, bf16[256,1536]{1,0:T(8,128)(2,1)}, u32[]{:S(2)}, u32[]{:S(2)}) collective-permute-start(bf16[256,1536]{1,0:T(8,128)(2,1)} %fusion.4), channel_id=1, source_target_pairs={{0,8},{8,16},{16,24},{24,28},{28,20},{20,12},{12,4},{4,0},{1,9},{9... | collective-permute-start | bytes 2359304 | tf_op jit(solution)/shard_map/ppermute | solution.py:117
  711.4 22.9 %collective-permute-start.67 = (bf16[256,1536]{1,0:T(8,128)(2,1)}, bf16[256,1536]{1,0:T(8,128)(2,1)}, u32[]{:S(2)}, u32[]{:S(2)}) collective-permute-start(bf16[256,1536]{1,0:T(8,128)(2,1)} %fusion.3), channel_id=1, source_target_pairs={{8,0},{16,8},{24,16},{28,24},{20,28},{12,20},{4,12},{0,4},{9,1},{1... | collective-permute-start | bytes 2359304 | tf_op jit(solution)/shard_map/ppermute | solution.py:118
  (80 other events, 1195.6 us)
